TPU v7x, 32 devices: a whole 2x2x4 slice. The times are simulated.
32 devices in a mesh: dp: 4 (over y, x), tile: 8 (over z, core).
Axes of the slice: x: 2, y: 2, z: 4, core: 2. Of those that a mesh axis runs over, the one named last changes fastest.
Arguments:
- features: bfloat16 [4, 4, 64, 8, 192], P('dp', None, 'tile'), may hold values from -40 to 40
- out_grad: bfloat16 [4, 4, 64, 8, 192], P('dp', None, 'tile'), may hold values from -6 to 6
- weight: bfloat16 [192, 27, 192], P('tile', None, 'dp'), may hold values from -0.078125 to 0.078125
- bias: float32 [192], replicated, may hold values from -3 to 3
- gamma: float32 [192], replicated, may hold values from 0.1 to 1.9
- beta: float32 [192], replicated, may hold values from -3 to 3
- tile_clip: int32 [4, 8], P('dp'), may hold values from 0 to 6, as said below
- tile_rows: int32 [4, 8], P('dp'), may hold values from 1 to 8, as said below
- clip_cols: int32 [4, 8], P('dp'), may hold values from 4 to 8, as said below
- clip_start: int32 [4, 8], P('dp'), may hold values from 0 to 2, as said below
Outputs:
- conv_out: bfloat16 [4, 4, 64, 8, 192], P('dp', None, 'tile')
- input_grad: bfloat16 [4, 4, 64, 8, 192], P('dp', None, 'tile')
- weight_grad: float32 [192, 27, 192], P('tile', None, 'dp')
Inputs may be any that keep to these rules, and one draw needn't show every extreme that they name: `tile_clip`: in each batch clip numbers start at 0 at tile 0 and rise by 0 or 1 from one tile to the next, so a clip's tiles are consecutive; tiles 0 and 1 share a clip. `tile_rows`: 8 for every tile but the last of its clip, which may have fewer. `clip_cols`: entries past a batch's last clip are not read. `clip_start`: entries past a batch's last clip are not read.
All inputs are finite; a program needn't handle non-finite values.
Results may differ from a plain program's by a relative error of at most 0.0039.
Values may be sent and summed in bfloat16 or wider, within the bound.
No kernel may reach another device: no remote copies, remote signals or barrier semaphores. Data moves between devices by JAX's collectives and lax.ppermute only.
A program may use at most 64 MiB of HBM per device.

v0:
```python
import jax
import jax.numpy as jnp
from jax import lax
from jax.sharding import PartitionSpec as P

G = 32


EPSILON = 1e-05


def with_halo(block, sides, width):
    for axis, dim in sides:
        count = lax.axis_size(axis)
        forward = [(i, i + 1) for i in range(count - 1)]
        backward = [(target, source) for source, target in forward]
        low = lax.ppermute(
            lax.slice_in_dim(block, block.shape[dim] - width, None, axis=dim), axis, forward
        )
        high = lax.ppermute(lax.slice_in_dim(block, 0, width, axis=dim), axis, backward)
        block = jnp.concatenate([low, block, high], axis=dim)
    return block


def tap_stack(padded, frames, height, width, count):
    slices = []
    for time_shift in range(3):
        for row_shift in range(3):
            for col_shift in range(3):
                slices.append(
                    padded[
                        ...,
                        time_shift : time_shift + frames,
                        row_shift : row_shift + height,
                        col_shift : col_shift + width,
                        :,
                    ]
                )
    stacked = jnp.stack(slices, axis=-1)
    return stacked.reshape(-1, count * 27)


def mend_rims(extended, above_keep, below_keep):
    top_row = extended[:, :1] * above_keep
    bottom_row = extended[:, -1:] * below_keep
    return jnp.concatenate([top_row, extended[:, 1:-1], bottom_row], axis=1)


def on_device(
    features, out_grad, weight, bias, gamma, beta, tile_clip, tile_rows, clip_cols, clip_start
):
    frames, height, width, channels = features.shape[1:]
    tile_count = lax.axis_size("tile")
    position = lax.axis_index("tile")
    group_size = channels // G
    num_cells = frames * height * width
    tiles = jnp.arange(tile_count, dtype=jnp.int32)
    clip_row = tile_clip[0]
    rows_row = tile_rows[0]
    own_clip = jnp.sum(jnp.where(tiles == position, clip_row, 0))
    own_rows = jnp.sum(jnp.where(tiles == position, rows_row, 0))
    clip_onehot = tiles == own_clip
    own_cols = jnp.sum(jnp.where(clip_onehot, clip_cols[0], 0))
    own_first = jnp.sum(jnp.where(clip_onehot, clip_start[0], 0))
    clip_rows = jnp.sum(jnp.where(clip_row == own_clip, rows_row, 0))
    above_clip = jnp.sum(jnp.where(tiles == position - 1, clip_row, 0))
    below_clip = jnp.sum(jnp.where(tiles == position + 1, clip_row, 0))
    above_keep = ((position > 0) & (above_clip == own_clip)).astype(jnp.bfloat16)
    below_keep = ((position < tile_count - 1) & (below_clip == own_clip)).astype(jnp.bfloat16)
    counted = ((frames - own_first) * own_cols * clip_rows * group_size).astype(jnp.float32)
    frame_index = lax.broadcasted_iota(jnp.int32, (frames, height, width), 0)
    row_index = lax.broadcasted_iota(jnp.int32, (frames, height, width), 1)
    col_index = lax.broadcasted_iota(jnp.int32, (frames, height, width), 2)
    valid = ((frame_index >= own_first) & (row_index < own_rows) & (col_index < own_cols)).astype(
        jnp.float32
    )[..., None]
    select = clip_onehot.astype(jnp.float32)[:, None]
    masked = features[0].astype(jnp.float32) * valid
    grouped = masked.reshape(frames, height, width, G, group_size)
    first_sum = jnp.sum(grouped, axis=(0, 1, 2, 4))
    square_sum = jnp.sum(grouped * grouped, axis=(0, 1, 2, 4))
    table_one, table_two = lax.psum(
        (select * first_sum[None, :], select * square_sum[None, :]), "tile"
    )
    mean_value = jnp.sum(select * table_one, axis=0) / counted
    variance = jnp.sum(select * table_two, axis=0) / counted - mean_value * mean_value
    inv_std = lax.rsqrt(variance + EPSILON)
    normed_groups = (grouped - mean_value[:, None]) * inv_std[:, None]
    normed = normed_groups.reshape(frames, height, width, channels)
    activation = normed * gamma + beta
    sigmoid_act = jax.nn.sigmoid(activation)
    hidden = (activation * sigmoid_act * valid).astype(jnp.bfloat16)
    grad_masked = (out_grad[0].astype(jnp.float32) * valid).astype(jnp.bfloat16)
    both_ext = with_halo(jnp.stack([hidden, grad_masked]), (("tile", 2),), 1)
    hidden_ext = both_ext[0]
    grad_ext = both_ext[1]
    hidden_ext = mend_rims(hidden_ext, above_keep, below_keep)
    hidden_pad = jnp.pad(hidden_ext, ((2, 0), (0, 0), (1, 1), (0, 0)))
    weight_rows = lax.all_gather(weight, "dp", axis=2, tiled=True)
    piece = lax.all_gather(weight_rows, "tile", axis=0, tiled=True)
    count = piece.shape[0]
    patches = tap_stack(hidden_pad, frames, height, width, count)
    conv_sum = jnp.dot(
        patches, piece.reshape(count * 27, channels), preferred_element_type=jnp.float32
    )
    conv_out = ((conv_sum.reshape(frames, height, width, channels) + bias) * valid).astype(
        jnp.bfloat16
    )
    grad_ext = mend_rims(grad_ext, above_keep, below_keep)
    grad_flat = grad_ext.reshape(-1, channels)
    piece = lax.all_gather(weight_rows, "tile", axis=0, tiled=True)
    count = piece.shape[0]
    products = lax.dot_general(
        grad_flat, piece, (((1,), (2,)), ((), ())), preferred_element_type=jnp.float32
    )
    products = products.reshape(frames, height + 2, width, count, 27)
    padded = jnp.pad(products, ((0, 2), (0, 0), (1, 1), (0, 0), (0, 0)))
    total = jnp.zeros((frames, height, width, count), jnp.float32)
    for time_shift in range(3):
        for row_shift in range(3):
            for col_shift in range(3):
                tap = 9 * time_shift + 3 * row_shift + col_shift
                total = (
                    total
                    + padded[
                        2 - time_shift : 2 - time_shift + frames,
                        2 - row_shift : 2 - row_shift + height,
                        2 - col_shift : 2 - col_shift + width,
                        :,
                        tap,
                    ]
                )
    dnormed = total * valid * sigmoid_act * (1.0 + activation * (1.0 - sigmoid_act)) * gamma
    dgroups = dnormed.reshape(frames, height, width, G, group_size)
    grad_one = jnp.sum(dgroups, axis=(0, 1, 2, 4))
    grad_two = jnp.sum(dgroups * normed_groups, axis=(0, 1, 2, 4))
    back_one, back_two = lax.psum((select * grad_one[None, :], select * grad_two[None, :]), "tile")
    first_total = jnp.sum(select * back_one, axis=0) / counted
    second_total = jnp.sum(select * back_two, axis=0) / counted
    input_groups = inv_std[:, None] * (
        dgroups - first_total[:, None] - normed_groups * second_total[:, None]
    )
    input_grad = (input_groups.reshape(frames, height, width, channels) * valid).astype(
        jnp.bfloat16
    )
    owned = channels // tile_count
    grad_cells = grad_masked.reshape(num_cells, channels)
    patches = tap_stack(hidden_pad, frames, height, width, owned * lax.axis_size("tile"))
    product = lax.dot_general(
        patches, grad_cells, (((0,), (0,)), ((), ())), preferred_element_type=jnp.float32
    )
    grad_rows = lax.psum_scatter(
        product.reshape(owned * lax.axis_size("tile"), 27, channels),
        "tile",
        scatter_dimension=0,
        tiled=True,
    )
    weight_grad = lax.psum_scatter(grad_rows, "dp", scatter_dimension=2, tiled=True)
    return (conv_out[None], input_grad[None], weight_grad)


def solution(mesh):
    in_specs = (
        P("dp", None, "tile", None, None),
        P("dp", None, "tile", None, None),
        P("tile", None, "dp"),
        P(),
        P(),
        P(),
        P("dp", None),
        P("dp", None),
        P("dp", None),
        P("dp", None),
    )
    out_specs = (
        P("dp", None, "tile", None, None),
        P("dp", None, "tile", None, None),
        P("tile", None, "dp"),
    )
    return jax.shard_map(
        on_device, mesh=mesh, in_specs=in_specs, out_specs=out_specs, check_vma=False
    )
```

profile of v0, /device:TPU:0, one launch (start us, length us, event | category | flops | bytes accessed | tf_op | source)
XLA Modules:
  0.0 203.7 jit_solution(2599986388782281632)
XLA Ops:
  7.2 1.4 fusion.103
  8.6 0.7 fusion.110
  9.3 2.0 fusion.109
  11.3 0.6 iota_compare_fusion.6
  12.6 2.1 %fusion.106 = (s32[]{:T(128)}, s32[]{:T(128)}, s32[]{:T(128)}, s32[]{:T(128)}, s32[]{:T(128)}) fusion(s32[1,8]{1,0:T(1,128)} %param.16, s32[]{:T(128)S(6)} %sub.92, s32[1,8]{1,0:T(1,128)} %param.17, s32[]{:T(128)} %fusion.103, s32[]{:T(128)S(6)} %axis_index.12, s32[]{:T(128)S(6)} %add.520, s32[1,8]{1,0:T(1,128)} %param.18), kind=kLoop, calls=%fused_computation.191 | loop fusion | flops 115 | bytes 132 | tf_op jit(solution)/shard_map/reduce_sum | solution.py:66
  14.7 0.6 iota_compare_fusion.3
  16.7 0.7 iota_compare_fusion.4
  17.3 0.1 and_convert_fusion
  17.4 1.0 fusion.58
  18.4 0.1 reduce_sum.173
  18.5 0.1 reduce_sum.168
  18.6 0.1 reduce_sum.174
  18.8 0.1 reduce_sum.169
  18.9 0.1 broadcast_multiply_fusion.3
  18.9 18.3 %all-reduce.3 = (f32[8,32]{1,0:T(8,128)S(1)}, f32[8,32]{1,0:T(8,128)S(1)}) all-reduce(f32[8,32]{1,0:T(8,128)S(1)} %get-tuple-element.36, f32[8,32]{1,0:T(8,128)S(1)} %get-tuple-element.35), channel_id=1, replica_groups=mesh['dp'=4,'tile'=8] {'tile'}, use_global_device_ids=true, to_apply=%region_11.12 | all-reduce | flops 512 | bytes 4096 | tf_op jit(solution)/shard_map/psum | solution.py:82
  37.3 0.1 multiply_reduce_fusion.2
  37.4 0.1 mul.355
  37.4 0.1 mul.356
  37.6 0.1 sub.87
  37.6 0.1 sub.88
  37.8 1.2 multiply_convert_fusion.1
  39.0 1.3 collective-permute-start
  40.3 1.3 collective-permute-start.1
  41.6 1.2 copy.140
  42.8 16.7 %all_gather.7 = bf16[24,27,192]{1,0,2:T(8,128)(2,1)S(1)} all-gather(bf16[24,27,48]{1,0,2:T(8,128)(2,1)S(1)} %copy.140), channel_id=1, replica_groups=mesh['dp'=4,'tile'=8] {'dp'}, dimensions={2}, use_global_device_ids=true | all-gather | bytes 311040 | tf_op jit(solution)/shard_map/all_gather | solution.py:99
  59.5 1.6 copy.141
  61.2 0.0 reduce-scatter.5.cloned.1.call-start
  64.0 0.1 pad_maximum_fusion
  64.1 0.7 slice_bitcast_fusion
  64.8 0.1 fusion.28
  66.0 1.8 copy-done.1
  67.8 10.5 %copy.146 = bf16[4,8,8,192,27]{4,3,2,1,0:T(8,128)(2,1)} copy(bf16[4,8,8,192,27]{3,2,4,1,0:T(8,128)(2,1)S(1)} %fusion.75) | data formatting | bytes 5308416 | tf_op jit(solution)/shard_map/stack | solution.py:39
  78.3 15.2 %reshape.504 = bf16[256,5184]{1,0:T(8,128)(2,1)S(1)} reshape(bf16[4,8,8,192,27]{4,3,2,1,0:T(8,128)(2,1)} %copy.146) | data formatting | bytes 5308416 | tf_op jit(solution)/shard_map/reshape | solution.py:40
  93.5 2.9 %copy.147 = bf16[5184,256]{1,0:T(8,128)(2,1)} copy(bf16[5184,256]{0,1:T(8,128)(2,1)S(1)} %bitcast.295) | data formatting | bytes 5308416 | tf_op jit(solution)/shard_map/dot_general | solution.py:149
  96.4 3.7 %dot_general.16 = bf16[192,27,256]{2,1,0:T(8,128)(2,1)S(1)} reshape(bf16[5184,256]{1,0:T(8,128)(2,1)} %copy.147) | data formatting | bytes 5308416 | tf_op jit(solution)/shard_map/dot_general | solution.py:149
  100.1 5.3 %fusion.4 = f32[192,27,192]{2,0,1:T(8,128)} fusion(bf16[256,192,1]{1,0,2:T(8,128)(2,1)S(1)} %bitcast.297, bf16[192,27,256]{2,1,0:T(8,128)(2,1)S(1)} %dot_general.16), kind=kOutput, calls=%fused_computation.28 | convolution fusion | flops 509607936 | bytes 6733824 | tf_op jit(solution)/shard_map/dot_general | solution.py:149
  105.5 0.2 reduce-scatter.7.cloned.1.call-start
  105.7 0.7 copy-done.7
  106.5 3.1 %fusion = f32[4,10,8,192,27]{3,2,1,0,4:T(8,128)S(1)} fusion(bf16[192,27,192]{2,0,1:T(8,128)(2,1)} %all-gather.2.cloned.1.call-done, bf16[4,1,8,192]{3,2,1,0:T(8,128)(2,1)S(1)} %get-tuple-element.28, bf16[4,8,8,192]{3,2,1,0:T(8,128)(2,1)S(1)} %slice.318, bf16[4,1,8,192]{3,2,1,0:T(8,128)(2,1)S(1)} %get-tuple-element.27), kind=kOutput, calls=%fused_computation.24 | convolution fusion | flops 637378560 | bytes 8749056 | tf_op jit(solution)/shard_map/dot_general | solution.py:113
  109.7 0.6 multiply_multiply_fusion
  110.3 2.8 %copy-done = f32[4,10,8,192,27]{3,2,1,0,4:T(8,128)} copy-done((f32[4,10,8,192,27]{3,2,1,0,4:T(8,128)}, f32[4,10,8,192,27]{3,2,1,0,4:T(8,128)S(1)}, u32[]{:S(2)}) %copy-start) | copy-done | bytes 6635544
  113.1 0.1 fusion.112
  113.3 0.1 reduce_sum.179
  113.4 0.1 reduce_sum.180
  113.5 0.1 reduce_sum.183
  113.6 0.1 reduce_sum.184
  113.8 0.1 broadcast_multiply_fusion
  113.8 15.0 %all-reduce.2 = (f32[8,32]{1,0:T(8,128)S(1)}, f32[8,32]{1,0:T(8,128)S(1)}) all-reduce(f32[8,32]{1,0:T(8,128)S(1)} %get-tuple-element.34, f32[8,32]{1,0:T(8,128)S(1)} %get-tuple-element.33), channel_id=1, replica_groups=mesh['dp'=4,'tile'=8] {'tile'}, use_global_device_ids=true, to_apply=%region_17.18 | all-reduce | flops 512 | bytes 4096 | tf_op jit(solution)/shard_map/psum | solution.py:137
  128.8 0.6 multiply_reduce_fusion.1
  129.4 34.6 %reduce-scatter.5.cloned.1.call-done = f32[24,27,192]{2,0,1:T(8,128)} async-done(((f32[192,27,192]{2,0,1:T(8,128)}), f32[24,27,192]{2,0,1:T(8,128)}) %reduce-scatter.5.cloned.1.call-update) | async-done | bytes 497680 | tf_op jit(solution)/shard_map/reduce_scatter | solution.py:152
  164.0 4.2 %copy.156 = f32[24,27,192]{0,1,2:T(8,128)S(1)} copy(f32[24,27,192]{2,0,1:T(8,128)} %reduce-scatter.5.cloned.1.call-done) | data formatting | bytes 995328
  168.2 2.7 %reshape.522 = f32[192,648]{1,0:T(8,128)} reshape(f32[192,27,24]{2,1,0:T(8,128)S(1)} %bitcast.294) | data formatting | bytes 995328
  171.0 0.7 broadcast_divide_fusion
  171.7 0.1 mul.395
  171.7 0.1 mul.396
  171.8 0.7 broadcast_divide_fusion.1
  172.5 0.1 sub.97
  172.6 0.1 sub.98
  172.7 2.9 %fusion.57 = bf16[1,4,8,8,192]{4,3,2,1,0:T(8,128)(2,1)} fusion(bf16[1,4,8,8,192]{4,3,2,1,0:T(8,128)(2,1)S(1)} %copy-done.3, f32[4,8,8,192,1]{3,2,1,0,4:T(8,128)S(1)} %get-tuple-element.20, f32[4,10,8,192,27]{3,2,1,0,4:T(8,128)} %copy-done, f32[192]{0:T(256)S(1)} %mul.396, f32[192]{0:T(256)S(1)} %sub.98, f32[192]{0:T(256)} %param.15, f32[192]{0:T(256)} %param.14, ...), kind=kLoop, calls=%fused_computation.77 | loop fusion | flops 1572864 | bytes 10033664 | tf_op jit(solution)/shard_map/convert_element_type | solution.py:143
  175.7 0.8 copy-done.4
  176.5 1.6 fusion.18
  178.1 16.5 %reduce-scatter.7.cloned.1.call-done = f32[48,648]{1,0:T(8,128)} async-done(((f32[192,648]{1,0:T(8,128)}), f32[48,648]{1,0:T(8,128)}) %reduce-scatter.7.cloned.1.call-update) | async-done | bytes 124432
  194.6 1.4 reshape.523
  196.0 1.1 copy.157
  (70 shorter events, 1.1 us)
Async XLA Ops:
  7.2 99.2 %all-gather.2.cloned.1.call-start = ((), (), s32[]{:S(2)}) async-start(), calls=%async_computation.2 | async-start | bytes 2985984 | tf_op jit(solution)/shard_map/all_gather | solution.py:100
  9.3 28.4 %copy-start.14 = (f32[8]{0:T(128)}, f32[8]{0:T(128)S(1)}, u32[]{:S(2)}) copy-start(f32[8]{0:T(128)S(1)} %fusion.110) | copy-start | bytes 100
  37.6 4.1 %copy-start.8 = (f32[192]{0:T(256)}, f32[192]{0:T(256)S(1)}, u32[]{:S(2)}) copy-start(f32[192]{0:T(256)S(1)} %mul.356) | copy-start | bytes 2308
  37.7 3.9 %copy-start.10 = (f32[192]{0:T(256)}, f32[192]{0:T(256)S(1)}, u32[]{:S(2)}) copy-start(f32[192]{0:T(256)S(1)} %sub.88) | copy-start | bytes 2308
  39.0 25.8 %copy-start.5 = (bf16[1,4,8,8,192]{4,3,2,1,0:T(8,128)(2,1)}, bf16[1,4,8,8,192]{4,3,2,1,0:T(8,128)(2,1)S(1)}, u32[]{:S(2)}) copy-start(bf16[1,4,8,8,192]{4,3,2,1,0:T(8,128)(2,1)S(1)} %get-tuple-element.32) | copy-start | bytes 294916
  39.0 25.0 %collective-permute-start = (bf16[2,4,1,8,192]{4,3,2,1,0:T(8,128)(2,1)S(1)}, bf16[2,4,1,8,192]{4,3,2,1,0:T(8,128)(2,1)S(1)}, u32[]{:S(2)}, u32[]{:S(2)}) collective-permute-start(bf16[2,4,1,8,192]{4,3,2,1,0:T(8,128)(2,1)S(1)} %get-tuple-element.25), channel_id=1, source_target_pairs={{0,1},{1,2},{2,3},{3,4},{4,5},{5,6},{6,7},{8,9},{9,10},{10,11},{11... | collective-permute-start | bytes 73736 | tf_op jit(solution)/shard_map/ppermute | solution.py:17
  40.3 23.7 %collective-permute-start.1 = (bf16[2,4,1,8,192]{4,3,2,1,0:T(8,128)(2,1)S(1)}, bf16[2,4,1,8,192]{4,3,2,1,0:T(8,128)(2,1)S(1)}, u32[]{:S(2)}, u32[]{:S(2)}) collective-permute-start(bf16[2,4,1,8,192]{4,3,2,1,0:T(8,128)(2,1)S(1)} %get-tuple-element.26), channel_id=1, source_target_pairs={{1,0},{2,1},{3,2},{4,3},{5,4},{6,5},{7,6},{9,8},{10,9},{11,10},{12... | collective-permute-start | bytes 73736 | tf_op jit(solution)/shard_map/ppermute | solution.py:20
  61.2 102.8 %reduce-scatter.5.cloned.1.call-start = ((), (), s32[]{:S(2)}) async-start(), calls=%async_computation.3 | async-start | bytes 5971968 | tf_op jit(solution)/shard_map/reduce_scatter | solution.py:152
  65.9 1.8 copy-start.1
  96.4 3.7 %copy-start.6 = (bf16[1,4,8,8,192]{4,3,2,1,0:T(8,128)(2,1)S(1)}, bf16[1,4,8,8,192]{4,3,2,1,0:T(8,128)(2,1)}, u32[]{:S(2)}) copy-start(bf16[1,4,8,8,192]{4,3,2,1,0:T(8,128)(2,1)} %copy-done.5) | copy-start | bytes 294916
  105.4 0.9 copy-start.7
  105.5 89.1 %reduce-scatter.7.cloned.1.call-start = ((), (), s32[]{:S(2)}) async-start(), calls=%async_computation.4 | async-start | bytes 737280
  106.4 3.2 %copy-start.3 = (bf16[1,4,8,8,192]{4,3,2,1,0:T(8,128)(2,1)S(1)}, bf16[1,4,8,8,192]{4,3,2,1,0:T(8,128)(2,1)}, u32[]{:S(2)}) copy-start(bf16[1,4,8,8,192]{4,3,2,1,0:T(8,128)(2,1)} %param.10) | copy-start | bytes 294916
  106.4 3.2 %copy-start.9 = (f32[192]{0:T(256)S(1)}, f32[192]{0:T(256)}, u32[]{:S(2)}) copy-start(f32[192]{0:T(256)} %copy-done.8) | copy-start | bytes 2308
  106.4 3.2 %copy-start.11 = (f32[192]{0:T(256)S(1)}, f32[192]{0:T(256)}, u32[]{:S(2)}) copy-start(f32[192]{0:T(256)} %copy-done.10) | copy-start | bytes 2308
  106.4 3.2 %copy-start.12 = (f32[192]{0:T(256)S(1)}, f32[192]{0:T(256)}, u32[]{:S(2)}) copy-start(f32[192]{0:T(256)} %param.15) | copy-start | bytes 2308
  106.5 3.2 %copy-start.13 = (f32[192]{0:T(256)S(1)}, f32[192]{0:T(256)}, u32[]{:S(2)}) copy-start(f32[192]{0:T(256)} %param.14) | copy-start | bytes 2308
  109.7 3.5 %copy-start = (f32[4,10,8,192,27]{3,2,1,0,4:T(8,128)}, f32[4,10,8,192,27]{3,2,1,0,4:T(8,128)S(1)}, u32[]{:S(2)}) copy-start(f32[4,10,8,192,27]{3,2,1,0,4:T(8,128)S(1)} %fusion) | copy-start | bytes 19906564
  109.7 4.1 %copy-start.15 = (f32[8]{0:T(128)S(1)}, f32[8]{0:T(128)}, u32[]{:S(2)}) copy-start(f32[8]{0:T(128)} %copy-done.14) | copy-start | bytes 100
  172.7 3.0 %copy-start.2 = (bf16[4,8,8,192,27]{3,2,4,1,0:T(8,128)(2,1)S(1)}, bf16[4,8,8,192,27]{3,2,4,1,0:T(8,128)(2,1)}, u32[]{:S(2)}) copy-start(bf16[4,8,8,192,27]{3,2,4,1,0:T(8,128)(2,1)} %copy-done.1) | copy-start | bytes 7962628
  172.7 3.8 %copy-start.4 = (bf16[192,27,192]{2,0,1:T(8,128)(2,1)S(1)}, bf16[192,27,192]{2,0,1:T(8,128)(2,1)}, u32[]{:S(2)}) copy-start(bf16[192,27,192]{2,0,1:T(8,128)(2,1)} %all-gather.2.cloned.1.call-done) | copy-start | bytes 5971972
  172.7 3.7 %copy-start.16 = (f32[192]{0:T(256)S(1)}, f32[192]{0:T(256)}, u32[]{:S(2)}) copy-start(f32[192]{0:T(256)} %param.13) | copy-start | bytes 2308
Sparse Core Ops, SparseCore 0:
  61.3 31.4 all-gather.1
  105.6 58.3 reduce-scatter.4
  171.1 23.4 reduce-scatter.6
where the time goes:
time: 205 us; the launch traced here: 204 us
  local copies, waits for them, and re-layouts  53.4 us (26%)
  waiting for transfers between devices  51.2 us (25%)
  blocking collectives  50 us (24%)
  between operations  19.1 us (9%)
  other arithmetic  17.1 us (8%)
  matrix products  10.1 us (5%)
  starting transfers between devices  2.88 us (1%)
    reduce_scatter x1, waiting for transfers between devices, on_device(): lax.psum_scatter(product.reshape(owned * lax.axis_size('tile'), 27, chann...  34.6 us
    psum x1, blocking collectives, on_device(): lax.psum((select * first_sum[None, :], select * square_sum[None, :]), 'ti...  18.3 us
    unnamed x63, local copies, waits for them, and re-layouts  17.6 us
    all_gather x1, blocking collectives, on_device(): weight_rows = lax.all_gather(weight, 'dp', axis=2, tiled=True)  16.7 us
    unnamed x4, waiting for transfers between devices  16.5 us
    reshape x1, local copies, waits for them, and re-layouts, tap_stack(): return stacked.reshape(-1, count * 27)  15.2 us
    psum x1, blocking collectives, on_device(): lax.psum((select * grad_one[None, :], select * grad_two[None, :]), 'tile')  15 us
    another operation x2, local copies, waits for them, and re-layouts, tap_stack(): stacked = jnp.stack(slices, axis=-1)  10.6 us
  transfers between devices with their start and end apart: 5, of which 2 were waited for; matrix products, arithmetic and copies ran while one was open for 26% of the time, Pallas kernels for 0%

commit v1 on v0

v1 whole, which is shorter than its diff:
```python
import functools

import jax
import jax.numpy as jnp
from jax import lax
from jax.experimental import pallas as pl
from jax.experimental.pallas import tpu as pltpu
from jax.sharding import PartitionSpec as P

G = 32
EPSILON = 1e-05
WIDE = 256
HALF_TAPS = 14
FRAMES, HEIGHT, WIDTH = 4, 8, 8
CELLS = FRAMES * HEIGHT * WIDTH
VMEM_LIMIT = 56 * 1024 * 1024
BF16, F32 = jnp.bfloat16, jnp.float32

TAPS = [9 * a + 3 * b + e for b in range(3) for a in range(3) for e in range(3)]


def up(value, multiple):
    return -(-value // multiple) * multiple


def params():
    return pltpu.CompilerParams(vmem_limit_bytes=VMEM_LIMIT)


def roll(x, shift):
    size = x.shape[-1]
    shift = shift % size
    return pltpu.roll(x, shift, x.ndim - 1) if shift else x


def exact_dot(x, y):
    return jnp.dot(x, y, preferred_element_type=F32, precision=lax.Precision.HIGHEST)


class Layout:
    def __init__(self, n, clip_ref, rows_ref, cols_ref, start_ref):
        position = lax.axis_index("tile")
        self.n = n
        self.core = lax.rem(position, 2)
        self.chip = lax.div(position, 2)
        self.tiles, self.clip, self.rows, self.cols, self.start = [], [], [], [], []
        self.above, self.below = [], []
        for m in range(n):
            tile = lax.rem(2 * self.chip + m, n)
            clip = clip_ref[0, tile]
            self.clip.append(clip)
            self.rows.append(rows_ref[0, tile])
            self.cols.append(cols_ref[0, clip])
            self.start.append(start_ref[0, clip])
            over = clip_ref[0, jnp.maximum(tile - 1, 0)]
            under = clip_ref[0, jnp.minimum(tile + 1, n - 1)]
            self.above.append(((tile > 0) & (over == clip)).astype(jnp.int32))
            self.below.append(((tile < n - 1) & (under == clip)).astype(jnp.int32))
        cell = lax.broadcasted_iota(jnp.int32, (1, CELLS), 1)
        self.f = lax.shift_right_logical(cell, 6)
        self.r = lax.bitwise_and(lax.shift_right_logical(cell, 3), 7)
        self.c = lax.bitwise_and(cell, 7)

    def valid(self, m):
        inside = (self.f >= self.start[m]) & (self.r < self.rows[m]) & (self.c < self.cols[m])
        return inside.astype(F32)

    def valid_rows(self, m):
        cell = lax.broadcasted_iota(jnp.int32, (CELLS, WIDE), 0)
        f = lax.shift_right_logical(cell, 6)
        r = lax.bitwise_and(lax.shift_right_logical(cell, 3), 7)
        c = lax.bitwise_and(cell, 7)
        return ((f >= self.start[m]) & (r < self.rows[m]) & (c < self.cols[m])).astype(F32)

    def lanes(self, parts):
        return jnp.concatenate(parts, axis=1)

    def repeat(self, part, count=None):
        return jnp.concatenate([part] * (count or self.n), axis=1)

    def counted(self, group_size):
        lane = lax.broadcasted_iota(jnp.int32, (1, 128), 1)
        counted = jnp.ones((1, 128), jnp.int32)
        for m in range(self.n):
            clip_rows = jnp.int32(0)
            for other in range(self.n):
                clip_rows += jnp.where(self.clip[other] == self.clip[m], self.rows[other], 0)
            cells = (FRAMES - self.start[m]) * self.cols[m] * clip_rows * group_size
            counted = jnp.where(lane == m, cells, counted)
        return counted.astype(F32)

    def clip_totals(self, sums):
        lane = lax.broadcasted_iota(jnp.int32, (1, 128), 1)
        total = jnp.zeros((sums[0].shape[0], 128), F32)
        for m in range(self.n):
            same = jnp.zeros((1, 128), F32)
            for other in range(self.n):
                hit = (self.clip[other] == self.clip[m]).astype(F32)
                same = jnp.where(lane == other, hit, same)
            total = total + sums[m] * same
        return total


def group_matrix(rows, real, padded, group_size):
    def group(index):
        block = index // padded
        inner = index - block * padded
        channel = block * real + inner
        return jnp.where(inner < real, channel // group_size, -1 - index)

    first = group(lax.broadcasted_iota(jnp.int32, (rows, rows), 0))
    second = group(lax.broadcasted_iota(jnp.int32, (rows, rows), 1))
    return (first == second).astype(F32)


def column(row_ref, channel_of, rows):
    channels = row_ref.shape[1]
    lane = lax.broadcasted_iota(jnp.int32, (rows, channels), 1)
    index = channel_of(lax.broadcasted_iota(jnp.int32, (rows, channels), 0))
    return jnp.sum(jnp.where(lane == index, row_ref[...], 0.0), axis=1, keepdims=True)


def own_channels(first, real, padded):
    def channel(index):
        block = index // padded
        inner = index - block * padded
        return jnp.where(inner < real, first + block * real + inner, -1)

    return channel


def prepare_kernel(nc, ir, irp, x_ref, g_ref, w_ref, *rest):
    outs, (w_out, blocks, wide, packed) = rest[:nc], rest[nc:]
    cbp = 2 * irp
    chip = lax.div(lax.axis_index("tile"), 2)
    turned = x_ref[...].astype(F32).T
    if irp != ir:
        blocks[...] = jnp.zeros_like(blocks)
    for q in range(nc):
        for core in range(2):
            at = (2 * q + core) * ir
            blocks[q, core * irp : core * irp + ir, :] = turned[at : at + ir]
    low = g_ref[:, :128]
    high = g_ref[:, 128:192].astype(F32)
    high = jnp.concatenate([high[: CELLS // 2], high[CELLS // 2 :]], axis=1).astype(BF16)
    for j in range(nc):
        mine = blocks[lax.rem(chip + j, nc)].astype(BF16)
        out = outs[j]
        out[0:cbp] = mine[:, :128]
        out[cbp : 2 * cbp] = mine[:, 128:]
        out[2 * cbp : 2 * cbp + CELLS] = low
        out[2 * cbp + CELLS :] = high
    ob = w_ref.shape[2]
    wide[...] = w_ref[...].astype(F32)
    packed[...] = jnp.zeros_like(packed)
    for p in range(HALF_TAPS):
        packed[p * irp : p * irp + ir, 0:ob] = wide[:, TAPS[p], :]
        if p + HALF_TAPS < 27:
            packed[p * irp : p * irp + ir, 64 : 64 + ob] = wide[:, TAPS[p + HALF_TAPS], :]
    w_out[...] = packed[...].astype(BF16)


def feature_block(ref, cbp):
    return jnp.concatenate([ref[0:cbp], ref[cbp : 2 * cbp]], axis=1).astype(F32)


def load_weight(refs, ob):
    nd = len(refs)
    dp = lax.axis_index("dp")
    joined = jnp.concatenate([ref[...] for ref in refs], axis=1)
    halves = []
    for start in (0, 64):
        picks = []
        for j in range(nd):
            lane = lax.broadcasted_iota(jnp.int32, (128, WIDE), 0) - start
            out = lax.broadcasted_iota(jnp.int32, (128, WIDE), 1) - lax.rem(dp + j, nd) * ob
            picks.append(((lane == out) & (lane >= 0) & (lane < ob)).astype(F32))
        pick = jnp.concatenate(picks, axis=0).astype(BF16)
        halves.append(jnp.dot(joined, pick, preferred_element_type=F32))
    return jnp.concatenate(halves, axis=0)


def conv_kernel(nc, nd, ir, irp, ob, group_size, *refs):
    n = 2 * nc
    cbp = 2 * irp
    table, refs = refs[:4], refs[4:]
    gamma_ref, beta_ref = refs[:2]
    refs = refs[2:]
    own, other, refs = refs[:nc], refs[nc:n], refs[n:]
    w_own, w_other, refs = refs[:nd], refs[nd : 2 * nd], refs[2 * nd :]
    outs, (stats_out, hidden_out, patches) = refs[:nc], refs[nc:]
    place = Layout(n, *table)
    even = place.core == 0
    channel = own_channels(place.chip * 2 * ir, ir, irp)
    gamma = column(gamma_ref, channel, cbp)
    beta = column(beta_ref, channel, cbp)
    masked, valid, first, square = [], [], [], []
    for k in range(nc):
        mine, theirs = feature_block(own[k], cbp), feature_block(other[k], cbp)
        for p, block in enumerate((jnp.where(even, mine, theirs), jnp.where(even, theirs, mine))):
            keep = place.valid(2 * k + p)
            block = block * keep
            valid.append(keep)
            masked.append(block)
            first.append(jnp.sum(block, axis=1, keepdims=True))
            square.append(jnp.sum(block * block, axis=1, keepdims=True))
    groups = group_matrix(cbp, ir, irp, group_size)
    counted = place.counted(group_size)
    mean = exact_dot(groups, place.clip_totals(first)) / counted
    variance = exact_dot(groups, place.clip_totals(square)) / counted - mean * mean
    inv_std = lax.rsqrt(variance + EPSILON)
    stats_out[0] = mean
    stats_out[1] = inv_std
    hidden = []
    for m in range(n):
        normed = (masked[m] - mean[:, m : m + 1]) * inv_std[:, m : m + 1]
        activation = normed * gamma + beta
        hidden.append(activation * jax.nn.sigmoid(activation) * valid[m])
    hidden = place.lanes(hidden).astype(BF16).astype(F32)
    top, bottom = hidden[:irp], hidden[irp:]
    mine, theirs = jnp.where(even, top, bottom), jnp.where(even, bottom, top)
    hidden_out[...] = mine.astype(BF16)
    hidden = jnp.concatenate([mine, theirs], axis=0)
    above, below = row_neighbours(place, hidden)

    def own_tiles(x):
        parts = []
        for k in range(nc):
            low = x[:, 2 * k * CELLS : (2 * k + 1) * CELLS]
            high = x[:, (2 * k + 1) * CELLS : (2 * k + 2) * CELLS]
            parts.append(jnp.where(even, low, high))
        return jnp.concatenate(parts, axis=1)

    f, c = place.repeat(place.f, nc), place.repeat(place.c, nc)
    for b, rows in enumerate((above, hidden, below)):
        for a, e, block in shifts(own_tiles(rows), f, c):
            u = 9 * b + 3 * a + e
            patches[u * cbp : (u + 1) * cbp] = block.astype(BF16)
    patches[27 * cbp :] = jnp.zeros((cbp, nc * CELLS), BF16)
    mine, theirs = load_weight(w_own, ob), load_weight(w_other, ob)
    pair = jnp.concatenate(
        [mine.reshape(2 * HALF_TAPS, irp, WIDE), theirs.reshape(2 * HALF_TAPS, irp, WIDE)], axis=1
    ).reshape(2 * HALF_TAPS * cbp, WIDE)
    turned = pair.T[:192].astype(BF16)
    total = jnp.dot(turned, patches[...], preferred_element_type=F32)
    for k in range(nc):
        outs[k][...] = total[:, k * CELLS : (k + 1) * CELLS].astype(outs[k].dtype)


def row_neighbours(place, x):
    r = place.repeat(place.r)
    edge_above = place.lanes([((place.r > 0) | (place.above[m] > 0)).astype(F32) for m in range(place.n)])
    edge_below = place.lanes([((place.r < 7) | (place.below[m] > 0)).astype(F32) for m in range(place.n)])
    above = roll(jnp.where(r == 7, roll(x, CELLS - 64), x), 8) * edge_above
    below = roll(jnp.where(r == 0, roll(x, 64 - CELLS), x), -8) * edge_below
    return above, below


def shifts(x, f, c):
    for e in range(3):
        if e == 0:
            moved = jnp.where(c > 0, roll(x, 1), 0.0)
        elif e == 2:
            moved = jnp.where(c < 7, roll(x, -1), 0.0)
        else:
            moved = x
        for a in range(3):
            late = 2 - a
            yield a, e, (jnp.where(f >= late, roll(moved, 64 * late), 0.0) if late else moved)


def grad_kernel(nc, nd, ir, irp, ob, group_size, *refs):
    n = 2 * nc
    cbp = 2 * irp
    table, refs = refs[:4], refs[4:]
    gamma_ref, beta_ref, stats_ref, hidden_ref = refs[:4]
    refs = refs[4:]
    own, other, refs = refs[:nc], refs[nc:n], refs[n:]
    w_own, refs = refs[:nd], refs[nd:]
    outs, refs = refs[:nc], refs[nc:]
    w_outs, (grads, centre, over, under, patches) = refs[:nd], refs[nd:]
    place = Layout(n, *table)
    even = place.core == 0
    width = n * CELLS
    lane = lax.broadcasted_iota(jnp.int32, (CELLS // 2, 128), 1)
    for k in range(nc):
        for mine, ref in ((True, own[k]), (False, other[k])):
            low = ref[2 * cbp : 2 * cbp + CELLS].astype(F32)
            high = ref[2 * cbp + CELLS :].astype(F32)
            right = jnp.concatenate([jnp.where(lane < 64, high, 0.0), jnp.where(lane < 64, roll(high, 64), 0.0)], axis=0)
            core = place.core if mine else 1 - place.core
            grads[2 * k + core] = jnp.concatenate([low, right], axis=1)
    for m in range(n):
        grads[m] = grads[m] * place.valid_rows(m)
    split = (FRAMES, HEIGHT, WIDTH, WIDE)
    for m in range(n):
        here = grads[m]
        rows = here.reshape(split)
        last = grads[(m - 1) % n].reshape(split)[:, 7:] * place.above[m].astype(F32)
        next_ = grads[(m + 1) % n].reshape(split)[:, :1] * place.below[m].astype(F32)
        at = slice(m * CELLS, (m + 1) * CELLS)
        centre[at] = here.astype(BF16)
        over[at] = jnp.concatenate([last, rows[:, :7]], axis=1).reshape(CELLS, WIDE).astype(BF16)
        under[at] = jnp.concatenate([rows[:, 1:], next_], axis=1).reshape(CELLS, WIDE).astype(BF16)
    weight = load_weight(w_own, ob)
    total = jnp.zeros((9 * irp, width), F32)
    for b, block in enumerate((under, centre, over)):
        part = weight[b * 9 * irp : (b + 1) * 9 * irp].astype(BF16)
        total = total + lax.dot_general(part, block[...], (((1,), (1,)), ((), ())), preferred_element_type=F32)
    f, c = place.repeat(place.f), place.repeat(place.c)
    hidden_grad = jnp.zeros((irp, width), F32)
    for e in range(3):
        moved = jnp.zeros((irp, width), F32)
        for a in range(3):
            late = 2 - a
            block = total[(3 * a + e) * irp : (3 * a + e + 1) * irp]
            moved = moved + (jnp.where(f < FRAMES - late, roll(block, -64 * late), 0.0) if late else block)
        if e == 0:
            moved = jnp.where(c < 7, roll(moved, -1), 0.0)
        elif e == 2:
            moved = jnp.where(c > 0, roll(moved, 1), 0.0)
        hidden_grad = hidden_grad + moved
    first_channel = (place.chip * 2 + place.core) * ir
    channel = own_channels(first_channel, ir, irp)
    gamma = column(gamma_ref, channel, irp)
    beta = column(beta_ref, channel, irp)
    mean = jnp.where(even, stats_ref[0, :irp], stats_ref[0, irp:])
    inv_std = jnp.where(even, stats_ref[1, :irp], stats_ref[1, irp:])
    valid, normed, dnormed, first, second = [], [], [], [], []
    for k in range(nc):
        mine, theirs = feature_block(own[k], cbp), feature_block(other[k], cbp)
        mine = jnp.where(even, mine[:irp], mine[irp:])
        theirs = jnp.where(even, theirs[:irp], theirs[irp:])
        for p, block in enumerate((jnp.where(even, mine, theirs), jnp.where(even, theirs, mine))):
            m = 2 * k + p
            keep = place.valid(m)
            norm = (block * keep - mean[:, m : m + 1]) * inv_std[:, m : m + 1]
            activation = norm * gamma + beta
            s = jax.nn.sigmoid(activation)
            grad = hidden_grad[:, m * CELLS : (m + 1) * CELLS]
            grad = grad * keep * s * (1.0 + activation * (1.0 - s)) * gamma
            valid.append(keep)
            normed.append(norm)
            dnormed.append(grad)
            first.append(jnp.sum(grad, axis=1, keepdims=True))
            second.append(jnp.sum(grad * norm, axis=1, keepdims=True))
    groups = group_matrix(irp, ir, irp, group_size)
    counted = place.counted(group_size)
    first_total = exact_dot(groups, place.clip_totals(first)) / counted
    second_total = exact_dot(groups, place.clip_totals(second)) / counted
    for m in range(n):
        grad = dnormed[m] - first_total[:, m : m + 1] - normed[m] * second_total[:, m : m + 1]
        grad = grad * inv_std[:, m : m + 1] * valid[m]
        outs[m // 2][:, (m % 2) * CELLS : (m % 2 + 1) * CELLS] = grad.astype(BF16)
    hidden = hidden_ref[...].astype(F32)
    above, below = row_neighbours(place, hidden)
    blocks = {}
    for b, rows in enumerate((above, hidden, below)):
        for a, e, block in shifts(rows, f, c):
            blocks[9 * b + 3 * a + e] = block
    blocks[27] = jnp.zeros((irp, width), F32)
    for p in range(HALF_TAPS):
        both = jnp.concatenate([blocks[2 * p], blocks[2 * p + 1]], axis=0)
        patches[p * cbp : (p + 1) * cbp] = both.astype(BF16)
    product = jnp.dot(patches[...], centre[...], preferred_element_type=F32)
    dp = lax.axis_index("dp")
    half = HALF_TAPS * irp
    lane = lax.broadcasted_iota(jnp.int32, (half, 128), 1)
    for j in range(nd):
        target = lax.rem(dp + j, nd)
        moved = pltpu.roll(product, lax.rem(WIDE - target * ob, WIDE), 1)[:, :128]
        low = jnp.where(lane < ob, moved[:half], 0.0)
        high = jnp.where(lane < ob, moved[half:], 0.0)
        w_outs[j][...] = (low + roll(high, 64)).astype(w_outs[j].dtype)


def conv_end_kernel(n, *refs):
    table, bias_ref, mine_ref = refs[:4], refs[4], refs[5]
    received, out_ref = refs[6:-1], refs[-1]
    place = Layout(n, *table)
    position = lax.axis_index("tile")
    total = mine_ref[...]
    for ref in received:
        total = total + ref[...].astype(F32)
    clip = table[0][0, position]
    rows, cols, start = table[1][0, position], table[2][0, clip], table[3][0, clip]
    inside = (place.f >= start) & (place.r < rows) & (place.c < cols)
    bias = column(bias_ref, lambda index: index, total.shape[0])
    out_ref[...] = jnp.where(inside, total + bias, 0.0).T.astype(BF16)


def grad_end_kernel(nc, ir, irp, *refs):
    own, other, out_ref, blocks = refs[:nc], refs[nc : 2 * nc], refs[2 * nc], refs[2 * nc + 1]
    position = lax.axis_index("tile")
    core, chip = lax.rem(position, 2), lax.div(position, 2)
    for j in range(nc):
        source = lax.rem(chip + nc - j, nc)
        for mine, ref in ((True, own[j]), (False, other[j])):
            x = ref[...].astype(F32)
            x = jnp.where(core == 0, x[:, :CELLS], x[:, CELLS:])
            blocks[2 * source + (core if mine else 1 - core)] = x
    joined = jnp.concatenate([blocks[q][:ir] for q in range(2 * nc)], axis=0)
    out_ref[...] = joined.T.astype(BF16)


def weight_end_kernel(ir, irp, ob, mine_ref, *refs):
    received, (out_ref, total) = refs[:-2], refs[-2:]
    value = mine_ref[...]
    for ref in received:
        value = value + ref[...].astype(F32)
    total[...] = value
    for u in range(27):
        p, start = (u, 0) if u < HALF_TAPS else (u - HALF_TAPS, 64)
        out_ref[:, TAPS[u], :] = total[p * irp : p * irp + ir, start : start + ob]


def on_device(
    features, out_grad, weight, bias, gamma, beta, tile_clip, tile_rows, clip_cols, clip_start
):
    n, nd = lax.axis_size("tile"), lax.axis_size("dp")
    nc = n // 2
    channels = features.shape[-1]
    group_size = channels // G
    ir, _, ob = weight.shape
    irp = up(ir, 8)
    cbp = 2 * irp
    width = n * CELLS
    smem = pl.BlockSpec(memory_space=pltpu.SMEM)
    vmem = pl.BlockSpec(memory_space=pltpu.VMEM)
    table = (tile_clip, tile_rows, clip_cols, clip_start)

    def shape(dims, dtype=BF16):
        return jax.ShapeDtypeStruct(dims, dtype)

    def call(kernel, args, out, scratch=(), scalars=0):
        return pl.pallas_call(
            kernel,
            out_shape=out,
            in_specs=[smem] * scalars + [vmem] * (len(args) - scalars),
            out_specs=jax.tree.map(lambda _: vmem, out),
            scratch_shapes=list(scratch),
            compiler_params=params(),
        )(*args)

    def along_chips(x, j):
        pairs = [(2 * q + core, 2 * ((q + j) % nc) + core) for q in range(nc) for core in range(2)]
        return lax.ppermute(x, "tile", pairs)

    def swap(x):
        return lax.ppermute(x, "tile", [(i, i ^ 1) for i in range(n)])

    def along_dp(x, j):
        return lax.ppermute(x, "dp", [(i, (i + j) % nd) for i in range(nd)])

    packed_rows = 2 * cbp + CELLS + CELLS // 2
    sent = call(
        functools.partial(prepare_kernel, nc, ir, irp),
        (features.reshape(CELLS, channels), out_grad.reshape(CELLS, channels), weight),
        [shape((packed_rows, 128))] * nc + [shape((HALF_TAPS * irp, 128))],
        [
            pltpu.VMEM((nc, cbp, CELLS), F32),
            pltpu.VMEM(weight.shape, F32),
            pltpu.VMEM((HALF_TAPS * irp, 128), F32),
        ],
    )
    sent, w_block = sent[:nc], sent[nc]
    own = [sent[0]] + [along_chips(sent[nc - j], nc - j) for j in range(1, nc)]
    other = [swap(x) for x in own]
    w_own = [w_block] + [along_dp(w_block, nd - j) for j in range(1, nd)]
    w_other = [swap(x) for x in w_own]
    gamma, beta, bias = gamma[None], beta[None], bias[None]

    first = call(
        functools.partial(conv_kernel, nc, nd, ir, irp, ob, group_size),
        (*table, gamma, beta, *own, *other, *w_own, *w_other),
        [shape((channels, CELLS), F32)]
        + [shape((channels, CELLS))] * (nc - 1)
        + [shape((2, cbp, 128), F32), shape((irp, width))],
        [pltpu.VMEM((2 * HALF_TAPS * cbp, nc * CELLS), BF16)],
        4,
    )
    parts, stats, hidden = first[:nc], first[nc], first[nc + 1]
    received = [along_chips(parts[j], j) for j in range(1, nc)]

    second = call(
        functools.partial(grad_kernel, nc, nd, ir, irp, ob, group_size),
        (*table, gamma, beta, stats, hidden, *own, *other, *w_own),
        [shape((irp, 2 * CELLS))] * nc
        + [shape((HALF_TAPS * irp, 128), F32)]
        + [shape((HALF_TAPS * irp, 128))] * (nd - 1),
        [
            pltpu.VMEM((n, CELLS, WIDE), F32),
            pltpu.VMEM((width, WIDE), BF16),
            pltpu.VMEM((width, WIDE), BF16),
            pltpu.VMEM((width, WIDE), BF16),
            pltpu.VMEM((HALF_TAPS * cbp, width), BF16),
        ],
        4,
    )
    grads, w_parts = second[:nc], second[nc:]
    w_received = [along_dp(w_parts[j], j) for j in range(1, nd)]
    grads = [grads[0]] + [along_chips(grads[j], j) for j in range(1, nc)]
    grads_other = [swap(x) for x in grads]

    conv_out = call(
        functools.partial(conv_end_kernel, n),
        (*table, bias, parts[0], *received),
        shape((CELLS, channels)),
        (),
        4,
    )
    weight_grad = call(
        functools.partial(weight_end_kernel, ir, irp, ob),
        (w_parts[0], *w_received),
        shape(weight.shape, F32),
        [pltpu.VMEM((HALF_TAPS * irp, 128), F32)],
    )
    input_grad = call(
        functools.partial(grad_end_kernel, nc, ir, irp),
        (*grads, *grads_other),
        shape((CELLS, channels)),
        [pltpu.VMEM((n, irp, CELLS), F32)],
    )
    return (
        conv_out.reshape(features.shape),
        input_grad.reshape(features.shape),
        weight_grad,
    )


def solution(mesh):
    in_specs = (
        P("dp", None, "tile", None, None),
        P("dp", None, "tile", None, None),
        P("tile", None, "dp"),
        P(),
        P(),
        P(),
        P("dp", None),
        P("dp", None),
        P("dp", None),
        P("dp", None),
    )
    out_specs = (
        P("dp", None, "tile", None, None),
        P("dp", None, "tile", None, None),
        P("tile", None, "dp"),
    )
    return jax.shard_map(
        on_device, mesh=mesh, in_specs=in_specs, out_specs=out_specs, check_vma=False
    )
```

time: 205 us -> 66.2 us (0.32)
  blocking collectives: 50 us -> 0 us
  local copies, waits for them, and re-layouts: 53.4 us -> 5.57 us
  waiting for transfers between devices: 51.2 us -> 13.2 us
  starting transfers between devices: 2.88 us -> 27 us
  Pallas kernels: 0 us -> 19.1 us
  between operations: 19.1 us -> 0.93 us
  other arithmetic: 17.1 us -> 0 us
  matrix products: 10.1 us -> 0 us
    reduce_scatter x1 -> x0, waiting for transfers between devices: 34.6 us -> none  [on_device(): lax.psum_scatter(product.reshape(owned * lax.axis_size('tile'), 27, chann...]
    psum x2 -> x0, blocking collectives: 33.3 us -> none  [the longest x1 18.3 us: on_device(): lax.psum((select * first_sum[None, :], select * square_sum[None, :]), 'ti...]
    ppermute x2 -> x27, starting transfers between devices: 2.58 us -> 27 us  [the longest x9 15.9 us: along_chips(): return lax.ppermute(x, 'tile', pairs)]
    pallas_call x0 -> x6, Pallas kernels: none -> 19.1 us  [call(): pl.pallas_call(kernel, out_shape=out, in_specs=[smem] * scalars + [vmem]...]
    all_gather x1 -> x0, blocking collectives: 16.7 us -> none  [on_device(): weight_rows = lax.all_gather(weight, 'dp', axis=2, tiled=True)]
    unnamed x4 -> x0, waiting for transfers between devices: 16.5 us -> none
    reshape x1 -> x0, local copies, waits for them, and re-layouts: 15.2 us -> none  [tap_stack(): return stacked.reshape(-1, count * 27)]
    ppermute x2 -> x27, waiting for transfers between devices: 0.01 us -> 13.2 us  [the longest x9 9.4 us: along_chips(): return lax.ppermute(x, 'tile', pairs)]
  transfers between devices with their start and end apart: 5 -> 27, of which waited for: 2 -> 9; matrix products, arithmetic and copies ran while one was open for 26% -> 3% of each run, Pallas kernels for 0% -> 6%
where the time goes in v1:
time: 66.2 us; the launch traced here: 65.8 us
  starting transfers between devices  27 us (41%)
  Pallas kernels  19.1 us (29%)
  waiting for transfers between devices  13.2 us (20%)
  local copies, waits for them, and re-layouts  5.57 us (8%)
  between operations  0.93 us (1%)
    pallas_call x6, Pallas kernels, call(): pl.pallas_call(kernel, out_shape=out, in_specs=[smem] * scalars + [vmem]...  19.1 us
    ppermute x9, starting transfers between devices, along_chips(): return lax.ppermute(x, 'tile', pairs)  15.9 us
    ppermute x9, waiting for transfers between devices, along_chips(): return lax.ppermute(x, 'tile', pairs)  9.4 us
    ppermute x6, starting transfers between devices, along_dp(): return lax.ppermute(x, 'dp', [(i, (i + j) % nd) for i in range(nd)])  9.04 us
    unnamed x62, local copies, waits for them, and re-layouts  5.57 us
    ppermute x6, waiting for transfers between devices, along_dp(): return lax.ppermute(x, 'dp', [(i, (i + j) % nd) for i in range(nd)])  2.88 us
    ppermute x12, starting transfers between devices, swap(): return lax.ppermute(x, 'tile', [(i, i ^ 1) for i in range(n)])  2.01 us
  transfers between devices with their start and end apart: 27, of which 9 were waited for; matrix products, arithmetic and copies ran while one was open for 3% of the time, Pallas kernels for 6%

profile of v1, /device:TPU:0, one launch (start us, length us, event | category | flops | bytes accessed | tf_op | source)
XLA Modules:
  0.0 65.8 jit_solution(10072901119630572320)
XLA Ops:
  0.6 1.6 %copy.13.w_ref = bf16[24,27,48]{2,1,0:T(8,128)(2,1)} copy(bf16[24,27,48]{2,0,1:T(8,128)(2,1)} %param.12) | data formatting | bytes 124416 | tf_op args[2]
  2.3 2.2 %shard_map.121 = (bf16[480,128]{1,0:T(8,128)(2,1)}, bf16[480,128]{1,0:T(8,128)(2,1)}, bf16[480,128]{1,0:T(8,128)(2,1)}, bf16[480,128]{1,0:T(8,128)(2,1)}, bf16[336,128]{1,0:T(8,128)(2,1)}) custom-call(bf16[256,192]{1,0:T(8,128)(2,1)} %bitcast.7, bf16[256,192]{1,0:T(8,128)(2,1)} %bitcast.8, bf16[24,27,48]{2,1,0:T(8,128)(2,1)} %copy.13.w_ref), custom_call_target="tpu_custom_call" | custom-call | tf_op jit(solution)/shard_map/pallas_call | solution.py:436
  4.4 3.9 %collective-permute-start.7 = (bf16[336,128]{1,0:T(8,128)(2,1)}, bf16[336,128]{1,0:T(8,128)(2,1)S(1)}, u32[]{:S(2)}, u32[]{:S(2)}) collective-permute-start(bf16[336,128]{1,0:T(8,128)(2,1)} %get-tuple-element.26.refs_14_.refs_16_), channel_id=1, source_target_pairs={{0,24},{8,0},{16,8},{24,16},{1,25},{9,1},{17,9},{25,17},{2,26},{10... | collective-permute-start | bytes 258056 | tf_op jit(solution)/shard_map/ppermute | solution.py:453
  8.3 0.5 collective-permute-start.8
  8.8 0.6 collective-permute-start.9
  9.4 0.0 collective-permute-start.10
  9.4 3.6 %collective-permute-start = (bf16[480,128]{1,0:T(8,128)(2,1)}, bf16[480,128]{1,0:T(8,128)(2,1)S(1)}, u32[]{:S(2)}, u32[]{:S(2)}) collective-permute-start(bf16[480,128]{1,0:T(8,128)(2,1)} %get-tuple-element.23), channel_id=1, source_target_pairs={{0,6},{1,7},{2,0},{3,1},{4,2},{5,3},{6,4},{7,5},{8,14},{9,15},{10,... | collective-permute-start | bytes 368648 | tf_op jit(solution)/shard_map/ppermute | solution.py:447
  13.0 0.0 collective-permute-done.7.refs_15_.refs_17_
  13.0 0.9 %collective-permute-start.1 = (bf16[480,128]{1,0:T(8,128)(2,1)}, bf16[480,128]{1,0:T(8,128)(2,1)S(1)}, u32[]{:S(2)}, u32[]{:S(2)}) collective-permute-start(bf16[480,128]{1,0:T(8,128)(2,1)} %get-tuple-element.24), channel_id=1, source_target_pairs={{0,4},{1,5},{2,6},{3,7},{4,0},{5,1},{6,2},{7,3},{8,12},{9,13},{10,... | collective-permute-start | bytes 368648 | tf_op jit(solution)/shard_map/ppermute | solution.py:447
  13.9 0.6 collective-permute-done.8.refs_16_.refs_18_
  14.6 1.6 %collective-permute-start.2 = (bf16[480,128]{1,0:T(8,128)(2,1)}, bf16[480,128]{1,0:T(8,128)(2,1)S(1)}, u32[]{:S(2)}, u32[]{:S(2)}) collective-permute-start(bf16[480,128]{1,0:T(8,128)(2,1)} %get-tuple-element.25), channel_id=1, source_target_pairs={{0,2},{1,3},{2,4},{3,5},{4,6},{5,7},{6,0},{7,1},{8,10},{9,11},{10,... | collective-permute-start | bytes 368648 | tf_op jit(solution)/shard_map/ppermute | solution.py:447
  16.1 0.0 collective-permute-done.9.refs_17_.refs_19_
  16.1 0.0 collective-permute-start.3
  16.2 0.0 collective-permute-done.10.refs_18_
  16.2 0.0 copy-start.16
  16.2 0.5 collective-permute-start.11
  16.7 0.4 collective-permute-done.refs_7_.refs_9_
  17.1 0.0 collective-permute-start.4
  17.1 7.8 %collective-permute-done.1.refs_8_.refs_10_ = bf16[480,128]{1,0:T(8,128)(2,1)S(1)} collective-permute-done((bf16[480,128]{1,0:T(8,128)(2,1)}, bf16[480,128]{1,0:T(8,128)(2,1)S(1)}, u32[]{:S(2)}, u32[]{:S(2)}) %collective-permute-start.1) | collective-permute-done | bytes 122912 | tf_op jit(solution)/shard_map/ppermute | solution.py:447
  24.9 0.0 collective-permute-start.5
  24.9 0.0 collective-permute-done.2.refs_9_.refs_11_
  24.9 0.0 copy-start.2
  24.9 0.5 collective-permute-start.6
  25.4 0.1 collective-permute-start.12
  25.5 0.0 collective-permute-done.11.refs_19_
  25.5 0.4 collective-permute-start.13
  25.9 0.8 %collective-permute-done.12.refs_20_ = bf16[336,128]{1,0:T(8,128)(2,1)S(1)} collective-permute-done((bf16[336,128]{1,0:T(8,128)(2,1)S(1)}, bf16[336,128]{1,0:T(8,128)(2,1)S(1)}, u32[]{:S(2)}, u32[]{:S(2)}) %collective-permute-start.12) | collective-permute-done | bytes 86048 | tf_op jit(solution)/shard_map/ppermute | solution.py:450
  26.7 0.2 collective-permute-done.13.refs_21_
  26.8 0.0 collective-permute-done.5.refs_12_.refs_14_
  26.8 0.0 collective-permute-done.6.refs_13_.refs_15_
  27.0 0.3 copy-done.18
  27.3 0.2 copy-done.19
  27.4 0.0 copy-done.4
  27.5 0.1 copy-done.5
  27.6 0.0 copy-done.6
  27.6 4.6 %shard_map.122 = (f32[192,256]{1,0:T(8,128)}, bf16[192,256]{1,0:T(8,128)(2,1)}, bf16[192,256]{1,0:T(8,128)(2,1)}, bf16[192,256]{1,0:T(8,128)(2,1)}, f32[2,48,128]{2,1,0:T(8,128)}, /*index=5*/bf16[24,2048]{1,0:T(8,128)(2,1)}) custom-call(s32[1,8]{1,0:T(1,128)} %refs_0_.5, s32[1,8]{1,0:T(1,128)} %refs_1_.5, s32[1,8]{1,0:T(1,128)} %refs_2_.5, s32[1,8]{1,0:T(1,128)} %refs_3_.5, ...), custom_call_target="tpu_custom_call" | custom-call | tf_op jit(solution)/shard_map/pallas_call | solution.py:436
  32.2 6.5 %shard_map.124 = (bf16[24,512]{1,0:T(8,128)(2,1)}, bf16[24,512]{1,0:T(8,128)(2,1)}, bf16[24,512]{1,0:T(8,128)(2,1)}, bf16[24,512]{1,0:T(8,128)(2,1)}, f32[336,12...) custom-call(s32[1,8]{1,0:T(1,128)} %refs_0_.5, s32[1,8]{1,0:T(1,128)} %refs_1_.5, ...), custom_call_target="tpu_custom_call" | custom-call | tf_op jit(solution)/shard_map/pallas_call | solution.py:436
  38.7 2.5 %collective-permute-start.24 = (bf16[336,128]{1,0:T(8,128)(2,1)}, bf16[336,128]{1,0:T(8,128)(2,1)S(1)}, u32[]{:S(2)}, u32[]{:S(2)}) collective-permute-start(bf16[336,128]{1,0:T(8,128)(2,1)} %get-tuple-element.38), channel_id=1, source_target_pairs={{0,8},{8,16},{16,24},{24,0},{1,9},{9,17},{17,25},{25,1},{2,10},{10... | collective-permute-start | bytes 258056 | tf_op jit(solution)/shard_map/ppermute | solution.py:453
  41.2 0.2 collective-permute-start.17
  41.4 1.8 %collective-permute-start.18 = (bf16[24,512]{1,0:T(8,128)(2,1)}, bf16[24,512]{1,0:T(8,128)(2,1)S(1)}, u32[]{:S(2)}, u32[]{:S(2)}) collective-permute-start(bf16[24,512]{1,0:T(8,128)(2,1)} %get-tuple-element.35), channel_id=1, source_target_pairs={{0,4},{1,5},{2,6},{3,7},{4,0},{5,1},{6,2},{7,3},{8,12},{9,13},{10,... | collective-permute-start | bytes 73736 | tf_op jit(solution)/shard_map/ppermute | solution.py:447
  43.2 2.9 %collective-permute-start.19 = (bf16[24,512]{1,0:T(8,128)(2,1)}, bf16[24,512]{1,0:T(8,128)(2,1)S(1)}, u32[]{:S(2)}, u32[]{:S(2)}) collective-permute-start(bf16[24,512]{1,0:T(8,128)(2,1)} %get-tuple-element.36), channel_id=1, source_target_pairs={{0,6},{1,7},{2,0},{3,1},{4,2},{5,3},{6,4},{7,5},{8,14},{9,15},{10,... | collective-permute-start | bytes 73736 | tf_op jit(solution)/shard_map/ppermute | solution.py:447
  46.2 1.1 %collective-permute-done.17.refs_1_ = bf16[24,512]{1,0:T(8,128)(2,1)S(1)} collective-permute-done((bf16[24,512]{1,0:T(8,128)(2,1)}, bf16[24,512]{1,0:T(8,128)(2,1)S(1)}, u32[]{:S(2)}, u32[]{:S(2)}) %collective-permute-start.17) | collective-permute-done | bytes 24608 | tf_op jit(solution)/shard_map/ppermute | solution.py:447
  47.3 0.5 collective-permute-start.22
  47.8 0.1 collective-permute-done.19.refs_3_
  47.9 0.0 collective-permute-start.23
  47.9 1.8 %collective-permute-start.14 = (bf16[192,256]{1,0:T(8,128)(2,1)S(1)}, bf16[192,256]{1,0:T(8,128)(2,1)S(1)}, u32[]{:S(2)}, u32[]{:S(2)}) collective-permute-start(bf16[192,256]{1,0:T(8,128)(2,1)S(1)} %copy-done.29), channel_id=1, source_target_pairs={{0,2},{1,3},{2,4},{3,5},{4,6},{5,7},{6,0},{7,1},{8,10},{9,11},{10,... | collective-permute-start | bytes 294920 | tf_op jit(solution)/shard_map/ppermute | solution.py:447
  49.7 0.0 collective-permute-done.21.refs_5_
  49.7 3.0 %collective-permute-start.15 = (bf16[192,256]{1,0:T(8,128)(2,1)S(1)}, bf16[192,256]{1,0:T(8,128)(2,1)S(1)}, u32[]{:S(2)}, u32[]{:S(2)}) collective-permute-start(bf16[192,256]{1,0:T(8,128)(2,1)S(1)} %copy-done.28), channel_id=1, source_target_pairs={{0,4},{1,5},{2,6},{3,7},{4,0},{5,1},{6,2},{7,3},{8,12},{9,13},{10,... | collective-permute-start | bytes 294920 | tf_op jit(solution)/shard_map/ppermute | solution.py:447
  52.7 0.0 collective-permute-done.22.refs_6_
  52.7 0.1 collective-permute-start.16
  52.8 0.8 %collective-permute-start.25 = (bf16[336,128]{1,0:T(8,128)(2,1)}, bf16[336,128]{1,0:T(8,128)(2,1)S(1)}, u32[]{:S(2)}, u32[]{:S(2)}) collective-permute-start(bf16[336,128]{1,0:T(8,128)(2,1)} %get-tuple-element.39), channel_id=1, source_target_pairs={{0,16},{8,24},{16,0},{24,8},{1,17},{9,25},{17,1},{25,9},{2,18},{10... | collective-permute-start | bytes 258056 | tf_op jit(solution)/shard_map/ppermute | solution.py:453
  53.7 0.8 %collective-permute-start.26 = (bf16[336,128]{1,0:T(8,128)(2,1)}, bf16[336,128]{1,0:T(8,128)(2,1)S(1)}, u32[]{:S(2)}, u32[]{:S(2)}) collective-permute-start(bf16[336,128]{1,0:T(8,128)(2,1)} %get-tuple-element.40), channel_id=1, source_target_pairs={{0,24},{8,0},{16,8},{24,16},{1,25},{9,1},{17,9},{25,17},{2,26},{10... | collective-permute-start | bytes 258056 | tf_op jit(solution)/shard_map/ppermute | solution.py:453
  54.5 1.6 %shard_map.125 = bf16[256,192]{1,0:T(8,128)(2,1)} custom-call(bf16[24,512]{1,0:T(8,128)(2,1)} %get-tuple-element.33.refs_0_, bf16[24,512]{1,0:T(8,128)(2,1)} %copy-done.20, bf16[24,512]{1,0:T(8,128)(2,1)} %copy-done.21, bf16[24,512]{1,0:T(8,128)(2,1)} %copy-done.22, bf16[24,512]{1,0:T(8,128)(2,1)} %copy-done.23, bf16[24,512]{1,0:T(8,128)(2,1)} %copy-done.24, ...), custom_call_target="tpu_custom_call" | custom-call | tf_op jit(solution)/shard_map/pallas_call | solution.py:436
  56.1 1.5 %collective-permute-done.25.refs_1_ = bf16[336,128]{1,0:T(8,128)(2,1)S(1)} collective-permute-done((bf16[336,128]{1,0:T(8,128)(2,1)}, bf16[336,128]{1,0:T(8,128)(2,1)S(1)}, u32[]{:S(2)}, u32[]{:S(2)}) %collective-permute-start.25) | collective-permute-done | bytes 86048 | tf_op jit(solution)/shard_map/ppermute | solution.py:453
  57.6 0.8 %collective-permute-done.26.refs_2_ = bf16[336,128]{1,0:T(8,128)(2,1)S(1)} collective-permute-done((bf16[336,128]{1,0:T(8,128)(2,1)}, bf16[336,128]{1,0:T(8,128)(2,1)S(1)}, u32[]{:S(2)}, u32[]{:S(2)}) %collective-permute-start.26) | collective-permute-done | bytes 86048 | tf_op jit(solution)/shard_map/ppermute | solution.py:453
  58.4 0.6 copy-done.15
  59.0 2.2 %shard_map.126 = f32[24,27,48]{2,1,0:T(8,128)} custom-call(f32[336,128]{1,0:T(8,128)} %get-tuple-element.37.mine_ref, bf16[336,128]{1,0:T(8,128)(2,1)} %copy-done.13, bf16[336,128]{1,0:T(8,128)(2,1)} %copy-done.14, bf16[336,128]{1,0:T(8,128)(2,1)} %copy-done.15), custom_call_target="tpu_custom_call" | custom-call | tf_op jit(solution)/shard_map/pallas_call | solution.py:436
  61.2 1.9 %copy.14 = f32[24,27,48]{2,0,1:T(8,128)} copy(f32[24,27,48]{2,1,0:T(8,128)} %shard_map.126) | data formatting | bytes 248832
  63.1 0.0 collective-permute-done.14.refs_6_
  63.1 0.0 collective-permute-done.16.refs_8_
  63.2 0.6 copy-done.10
  63.8 0.0 copy-done.11
  63.8 0.0 copy-done.12
  63.8 2.0 %shard_map.123 = bf16[256,192]{1,0:T(8,128)(2,1)} custom-call(s32[1,8]{1,0:T(1,128)} %refs_0_.5, s32[1,8]{1,0:T(1,128)} %refs_1_.5, s32[1,8]{1,0:T(1,128)} %refs_2_.5, s32[1,8]{1,0:T(1,128)} %refs_3_.5, f32[1,192]{1,0:T(1,128)} %bitcast.15, f32[192,256]{1,0:T(8,128)} %get-tuple-element.27.refs_5_, bf16[192,256]{1,0:T(8,128)(2,1)} %copy-done.10, ...), custom_call_target="tpu_custom_call" | custom-call | tf_op jit(solution)/shard_map/pallas_call | solution.py:436
  (58 shorter events, 0.1 us)
Async XLA Ops:
  4.4 8.6 %collective-permute-start.7 = (bf16[336,128]{1,0:T(8,128)(2,1)}, bf16[336,128]{1,0:T(8,128)(2,1)S(1)}, u32[]{:S(2)}, u32[]{:S(2)}) collective-permute-start(bf16[336,128]{1,0:T(8,128)(2,1)} %get-tuple-element.26.refs_14_.refs_16_), channel_id=1, source_target_pairs={{0,24},{8,0},{16,8},{24,16},{1,25},{9,1},{17,9},{25,17},{2,26},{10... | collective-permute-start | bytes 258056 | tf_op jit(solution)/shard_map/ppermute | solution.py:453
  8.3 6.2 %collective-permute-start.8 = (bf16[336,128]{1,0:T(8,128)(2,1)}, bf16[336,128]{1,0:T(8,128)(2,1)S(1)}, u32[]{:S(2)}, u32[]{:S(2)}) collective-permute-start(bf16[336,128]{1,0:T(8,128)(2,1)} %get-tuple-element.26.refs_14_.refs_16_), channel_id=1, source_target_pairs={{0,16},{8,24},{16,0},{24,8},{1,17},{9,25},{17,1},{25,9},{2,18},{10... | collective-permute-start | bytes 258056 | tf_op jit(solution)/shard_map/ppermute | solution.py:453
  8.8 7.3 %collective-permute-start.9 = (bf16[336,128]{1,0:T(8,128)(2,1)}, bf16[336,128]{1,0:T(8,128)(2,1)S(1)}, u32[]{:S(2)}, u32[]{:S(2)}) collective-permute-start(bf16[336,128]{1,0:T(8,128)(2,1)} %get-tuple-element.26.refs_14_.refs_16_), channel_id=1, source_target_pairs={{0,8},{8,16},{16,24},{24,0},{1,9},{9,17},{17,25},{25,1},{2,10},{10... | collective-permute-start | bytes 258056 | tf_op jit(solution)/shard_map/ppermute | solution.py:453
  9.4 6.7 %collective-permute-start.10 = (bf16[336,128]{1,0:T(8,128)(2,1)}, bf16[336,128]{1,0:T(8,128)(2,1)S(1)}, u32[]{:S(2)}, u32[]{:S(2)}) collective-permute-start(bf16[336,128]{1,0:T(8,128)(2,1)} %get-tuple-element.26.refs_14_.refs_16_), channel_id=1, source_target_pairs={{0,1},{1,0},{2,3},{3,2},{4,5},{5,4},{6,7},{7,6},{8,9},{9,8},{10,11... | collective-permute-start | bytes 258056 | tf_op jit(solution)/shard_map/ppermute | solution.py:450
  9.4 7.6 %collective-permute-start = (bf16[480,128]{1,0:T(8,128)(2,1)}, bf16[480,128]{1,0:T(8,128)(2,1)S(1)}, u32[]{:S(2)}, u32[]{:S(2)}) collective-permute-start(bf16[480,128]{1,0:T(8,128)(2,1)} %get-tuple-element.23), channel_id=1, source_target_pairs={{0,6},{1,7},{2,0},{3,1},{4,2},{5,3},{6,4},{7,5},{8,14},{9,15},{10,... | collective-permute-start | bytes 368648 | tf_op jit(solution)/shard_map/ppermute | solution.py:447
  13.0 13.8 %copy-start.7 = (bf16[336,128]{1,0:T(8,128)(2,1)}, bf16[336,128]{1,0:T(8,128)(2,1)S(1)}, u32[]{:S(2)}) copy-start(bf16[336,128]{1,0:T(8,128)(2,1)S(1)} %collective-permute-done.7.refs_15_.refs_17_) | copy-start | bytes 258052
  13.0 11.8 %collective-permute-start.1 = (bf16[480,128]{1,0:T(8,128)(2,1)}, bf16[480,128]{1,0:T(8,128)(2,1)S(1)}, u32[]{:S(2)}, u32[]{:S(2)}) collective-permute-start(bf16[480,128]{1,0:T(8,128)(2,1)} %get-tuple-element.24), channel_id=1, source_target_pairs={{0,4},{1,5},{2,6},{3,7},{4,0},{5,1},{6,2},{7,3},{8,12},{9,13},{10,... | collective-permute-start | bytes 368648 | tf_op jit(solution)/shard_map/ppermute | solution.py:447
  14.6 12.3 %copy-start.8 = (bf16[336,128]{1,0:T(8,128)(2,1)}, bf16[336,128]{1,0:T(8,128)(2,1)S(1)}, u32[]{:S(2)}) copy-start(bf16[336,128]{1,0:T(8,128)(2,1)S(1)} %collective-permute-done.8.refs_16_.refs_18_) | copy-start | bytes 258052
  14.6 10.3 %collective-permute-start.2 = (bf16[480,128]{1,0:T(8,128)(2,1)}, bf16[480,128]{1,0:T(8,128)(2,1)S(1)}, u32[]{:S(2)}, u32[]{:S(2)}) collective-permute-start(bf16[480,128]{1,0:T(8,128)(2,1)} %get-tuple-element.25), channel_id=1, source_target_pairs={{0,2},{1,3},{2,4},{3,5},{4,6},{5,7},{6,0},{7,1},{8,10},{9,11},{10,... | collective-permute-start | bytes 368648 | tf_op jit(solution)/shard_map/ppermute | solution.py:447
  16.1 10.7 %copy-start.9 = (bf16[336,128]{1,0:T(8,128)(2,1)}, bf16[336,128]{1,0:T(8,128)(2,1)S(1)}, u32[]{:S(2)}) copy-start(bf16[336,128]{1,0:T(8,128)(2,1)S(1)} %collective-permute-done.9.refs_17_.refs_19_) | copy-start | bytes 258052
  16.1 9.2 %collective-permute-start.3 = (bf16[480,128]{1,0:T(8,128)(2,1)}, bf16[480,128]{1,0:T(8,128)(2,1)S(1)}, u32[]{:S(2)}, u32[]{:S(2)}) collective-permute-start(bf16[480,128]{1,0:T(8,128)(2,1)} %get-tuple-element.22.refs_6_.refs_8_), channel_id=1, source_target_pairs={{0,1},{1,0},{2,3},{3,2},{4,5},{5,4},{6,7},{7,6},{8,9},{9,8},{10,11... | collective-permute-start | bytes 368648 | tf_op jit(solution)/shard_map/ppermute | solution.py:450
  16.2 10.7 %copy-start.16 = (bf16[336,128]{1,0:T(8,128)(2,1)}, bf16[336,128]{1,0:T(8,128)(2,1)S(1)}, u32[]{:S(2)}) copy-start(bf16[336,128]{1,0:T(8,128)(2,1)S(1)} %collective-permute-done.10.refs_18_) | copy-start | bytes 258052
  16.2 9.3 %collective-permute-start.11 = (bf16[336,128]{1,0:T(8,128)(2,1)S(1)}, bf16[336,128]{1,0:T(8,128)(2,1)S(1)}, u32[]{:S(2)}, u32[]{:S(2)}) collective-permute-start(bf16[336,128]{1,0:T(8,128)(2,1)S(1)} %collective-permute-done.7.refs_15_.refs_17_), channel_id=1, source_target_pairs={{0,1},{1,0},{2,3},{3,2},{4,5},{5,4},{6,7},{7,6},{8,9},{9,8},{10,11... | collective-permute-start | bytes 258056 | tf_op jit(solution)/shard_map/ppermute | solution.py:450
  17.1 9.9 %copy-start = (bf16[480,128]{1,0:T(8,128)(2,1)}, bf16[480,128]{1,0:T(8,128)(2,1)S(1)}, u32[]{:S(2)}) copy-start(bf16[480,128]{1,0:T(8,128)(2,1)S(1)} %collective-permute-done.refs_7_.refs_9_) | copy-start | bytes 368644
  17.1 9.8 %collective-permute-start.4 = (bf16[480,128]{1,0:T(8,128)(2,1)S(1)}, bf16[480,128]{1,0:T(8,128)(2,1)S(1)}, u32[]{:S(2)}, u32[]{:S(2)}) collective-permute-start(bf16[480,128]{1,0:T(8,128)(2,1)S(1)} %collective-permute-done.refs_7_.refs_9_), channel_id=1, source_target_pairs={{0,1},{1,0},{2,3},{3,2},{4,5},{5,4},{6,7},{7,6},{8,9},{9,8},{10,11... | collective-permute-start | bytes 368648 | tf_op jit(solution)/shard_map/ppermute | solution.py:450
  24.9 2.1 %copy-start.1 = (bf16[480,128]{1,0:T(8,128)(2,1)}, bf16[480,128]{1,0:T(8,128)(2,1)S(1)}, u32[]{:S(2)}) copy-start(bf16[480,128]{1,0:T(8,128)(2,1)S(1)} %collective-permute-done.1.refs_8_.refs_10_) | copy-start | bytes 368644
  24.9 2.0 %collective-permute-start.5 = (bf16[480,128]{1,0:T(8,128)(2,1)S(1)}, bf16[480,128]{1,0:T(8,128)(2,1)S(1)}, u32[]{:S(2)}, u32[]{:S(2)}) collective-permute-start(bf16[480,128]{1,0:T(8,128)(2,1)S(1)} %collective-permute-done.1.refs_8_.refs_10_), channel_id=1, source_target_pairs={{0,1},{1,0},{2,3},{3,2},{4,5},{5,4},{6,7},{7,6},{8,9},{9,8},{10,11... | collective-permute-start | bytes 368648 | tf_op jit(solution)/shard_map/ppermute | solution.py:450
  24.9 2.1 %copy-start.2 = (bf16[480,128]{1,0:T(8,128)(2,1)}, bf16[480,128]{1,0:T(8,128)(2,1)S(1)}, u32[]{:S(2)}) copy-start(bf16[480,128]{1,0:T(8,128)(2,1)S(1)} %collective-permute-done.2.refs_9_.refs_11_) | copy-start | bytes 368644
  24.9 2.0 %collective-permute-start.6 = (bf16[480,128]{1,0:T(8,128)(2,1)S(1)}, bf16[480,128]{1,0:T(8,128)(2,1)S(1)}, u32[]{:S(2)}, u32[]{:S(2)}) collective-permute-start(bf16[480,128]{1,0:T(8,128)(2,1)S(1)} %collective-permute-done.2.refs_9_.refs_11_), channel_id=1, source_target_pairs={{0,1},{1,0},{2,3},{3,2},{4,5},{5,4},{6,7},{7,6},{8,9},{9,8},{10,11... | collective-permute-start | bytes 368648 | tf_op jit(solution)/shard_map/ppermute | solution.py:450
  25.4 1.6 %copy-start.3 = (bf16[480,128]{1,0:T(8,128)(2,1)}, bf16[480,128]{1,0:T(8,128)(2,1)S(1)}, u32[]{:S(2)}) copy-start(bf16[480,128]{1,0:T(8,128)(2,1)S(1)} %collective-permute-done.3.refs_10_.refs_12_) | copy-start | bytes 368644
  25.4 1.3 %collective-permute-start.12 = (bf16[336,128]{1,0:T(8,128)(2,1)S(1)}, bf16[336,128]{1,0:T(8,128)(2,1)S(1)}, u32[]{:S(2)}, u32[]{:S(2)}) collective-permute-start(bf16[336,128]{1,0:T(8,128)(2,1)S(1)} %collective-permute-done.8.refs_16_.refs_18_), channel_id=1, source_target_pairs={{0,1},{1,0},{2,3},{3,2},{4,5},{5,4},{6,7},{7,6},{8,9},{9,8},{10,11... | collective-permute-start | bytes 258056 | tf_op jit(solution)/shard_map/ppermute | solution.py:450
  25.5 1.5 %copy-start.17 = (bf16[336,128]{1,0:T(8,128)(2,1)}, bf16[336,128]{1,0:T(8,128)(2,1)S(1)}, u32[]{:S(2)}) copy-start(bf16[336,128]{1,0:T(8,128)(2,1)S(1)} %collective-permute-done.11.refs_19_) | copy-start | bytes 258052
  25.5 1.4 %collective-permute-start.13 = (bf16[336,128]{1,0:T(8,128)(2,1)S(1)}, bf16[336,128]{1,0:T(8,128)(2,1)S(1)}, u32[]{:S(2)}, u32[]{:S(2)}) collective-permute-start(bf16[336,128]{1,0:T(8,128)(2,1)S(1)} %collective-permute-done.9.refs_17_.refs_19_), channel_id=1, source_target_pairs={{0,1},{1,0},{2,3},{3,2},{4,5},{5,4},{6,7},{7,6},{8,9},{9,8},{10,11... | collective-permute-start | bytes 258056 | tf_op jit(solution)/shard_map/ppermute | solution.py:450
  26.7 0.6 copy-start.18
  26.8 0.6 copy-start.19
  26.8 0.7 %copy-start.4 = (bf16[480,128]{1,0:T(8,128)(2,1)}, bf16[480,128]{1,0:T(8,128)(2,1)S(1)}, u32[]{:S(2)}) copy-start(bf16[480,128]{1,0:T(8,128)(2,1)S(1)} %collective-permute-done.4.refs_11_.refs_13_) | copy-start | bytes 368644
  26.8 0.7 %copy-start.5 = (bf16[480,128]{1,0:T(8,128)(2,1)}, bf16[480,128]{1,0:T(8,128)(2,1)S(1)}, u32[]{:S(2)}) copy-start(bf16[480,128]{1,0:T(8,128)(2,1)S(1)} %collective-permute-done.5.refs_12_.refs_14_) | copy-start | bytes 368644
  26.9 0.7 %copy-start.6 = (bf16[480,128]{1,0:T(8,128)(2,1)}, bf16[480,128]{1,0:T(8,128)(2,1)S(1)}, u32[]{:S(2)}) copy-start(bf16[480,128]{1,0:T(8,128)(2,1)S(1)} %collective-permute-done.6.refs_13_.refs_15_) | copy-start | bytes 368644
  32.2 15.7 %copy-start.29 = (bf16[192,256]{1,0:T(8,128)(2,1)S(1)}, bf16[192,256]{1,0:T(8,128)(2,1)}, u32[]{:S(2)}) copy-start(bf16[192,256]{1,0:T(8,128)(2,1)} %get-tuple-element.28) | copy-start | bytes 294916
  32.2 17.5 %copy-start.28 = (bf16[192,256]{1,0:T(8,128)(2,1)S(1)}, bf16[192,256]{1,0:T(8,128)(2,1)}, u32[]{:S(2)}) copy-start(bf16[192,256]{1,0:T(8,128)(2,1)} %get-tuple-element.29) | copy-start | bytes 294916
  32.2 20.5 %copy-start.27 = (bf16[192,256]{1,0:T(8,128)(2,1)S(1)}, bf16[192,256]{1,0:T(8,128)(2,1)}, u32[]{:S(2)}) copy-start(bf16[192,256]{1,0:T(8,128)(2,1)} %get-tuple-element.30) | copy-start | bytes 294916
  38.7 14.9 %collective-permute-start.24 = (bf16[336,128]{1,0:T(8,128)(2,1)}, bf16[336,128]{1,0:T(8,128)(2,1)S(1)}, u32[]{:S(2)}, u32[]{:S(2)}) collective-permute-start(bf16[336,128]{1,0:T(8,128)(2,1)} %get-tuple-element.38), channel_id=1, source_target_pairs={{0,8},{8,16},{16,24},{24,0},{1,9},{9,17},{17,25},{25,1},{2,10},{10... | collective-permute-start | bytes 258056 | tf_op jit(solution)/shard_map/ppermute | solution.py:453
  41.2 6.1 %collective-permute-start.17 = (bf16[24,512]{1,0:T(8,128)(2,1)}, bf16[24,512]{1,0:T(8,128)(2,1)S(1)}, u32[]{:S(2)}, u32[]{:S(2)}) collective-permute-start(bf16[24,512]{1,0:T(8,128)(2,1)} %get-tuple-element.34), channel_id=1, source_target_pairs={{0,2},{1,3},{2,4},{3,5},{4,6},{5,7},{6,0},{7,1},{8,10},{9,11},{10,... | collective-permute-start | bytes 73736 | tf_op jit(solution)/shard_map/ppermute | solution.py:447
  41.4 5.9 %collective-permute-start.18 = (bf16[24,512]{1,0:T(8,128)(2,1)}, bf16[24,512]{1,0:T(8,128)(2,1)S(1)}, u32[]{:S(2)}, u32[]{:S(2)}) collective-permute-start(bf16[24,512]{1,0:T(8,128)(2,1)} %get-tuple-element.35), channel_id=1, source_target_pairs={{0,4},{1,5},{2,6},{3,7},{4,0},{5,1},{6,2},{7,3},{8,12},{9,13},{10,... | collective-permute-start | bytes 73736 | tf_op jit(solution)/shard_map/ppermute | solution.py:447
  43.2 4.7 %collective-permute-start.19 = (bf16[24,512]{1,0:T(8,128)(2,1)}, bf16[24,512]{1,0:T(8,128)(2,1)S(1)}, u32[]{:S(2)}, u32[]{:S(2)}) collective-permute-start(bf16[24,512]{1,0:T(8,128)(2,1)} %get-tuple-element.36), channel_id=1, source_target_pairs={{0,6},{1,7},{2,0},{3,1},{4,2},{5,3},{6,4},{7,5},{8,14},{9,15},{10,... | collective-permute-start | bytes 73736 | tf_op jit(solution)/shard_map/ppermute | solution.py:447
  46.2 1.7 %collective-permute-start.20 = (bf16[24,512]{1,0:T(8,128)(2,1)}, bf16[24,512]{1,0:T(8,128)(2,1)S(1)}, u32[]{:S(2)}, u32[]{:S(2)}) collective-permute-start(bf16[24,512]{1,0:T(8,128)(2,1)} %get-tuple-element.33.refs_0_), channel_id=1, source_target_pairs={{0,1},{1,0},{2,3},{3,2},{4,5},{5,4},{6,7},{7,6},{8,9},{9,8},{10,11... | collective-permute-start | bytes 73736 | tf_op jit(solution)/shard_map/ppermute | solution.py:450
  47.3 7.1 %copy-start.20 = (bf16[24,512]{1,0:T(8,128)(2,1)}, bf16[24,512]{1,0:T(8,128)(2,1)S(1)}, u32[]{:S(2)}) copy-start(bf16[24,512]{1,0:T(8,128)(2,1)S(1)} %collective-permute-done.17.refs_1_) | copy-start | bytes 73732
  47.3 2.4 %collective-permute-start.21 = (bf16[24,512]{1,0:T(8,128)(2,1)S(1)}, bf16[24,512]{1,0:T(8,128)(2,1)S(1)}, u32[]{:S(2)}, u32[]{:S(2)}) collective-permute-start(bf16[24,512]{1,0:T(8,128)(2,1)S(1)} %collective-permute-done.17.refs_1_), channel_id=1, source_target_pairs={{0,1},{1,0},{2,3},{3,2},{4,5},{5,4},{6,7},{7,6},{8,9},{9,8},{10,11... | collective-permute-start | bytes 73736 | tf_op jit(solution)/shard_map/ppermute | solution.py:450
  47.3 7.1 %copy-start.21 = (bf16[24,512]{1,0:T(8,128)(2,1)}, bf16[24,512]{1,0:T(8,128)(2,1)S(1)}, u32[]{:S(2)}) copy-start(bf16[24,512]{1,0:T(8,128)(2,1)S(1)} %collective-permute-done.18.refs_2_) | copy-start | bytes 73732
  47.3 5.4 %collective-permute-start.22 = (bf16[24,512]{1,0:T(8,128)(2,1)S(1)}, bf16[24,512]{1,0:T(8,128)(2,1)S(1)}, u32[]{:S(2)}, u32[]{:S(2)}) collective-permute-start(bf16[24,512]{1,0:T(8,128)(2,1)S(1)} %collective-permute-done.18.refs_2_), channel_id=1, source_target_pairs={{0,1},{1,0},{2,3},{3,2},{4,5},{5,4},{6,7},{7,6},{8,9},{9,8},{10,11... | collective-permute-start | bytes 73736 | tf_op jit(solution)/shard_map/ppermute | solution.py:450
  47.9 6.5 %copy-start.22 = (bf16[24,512]{1,0:T(8,128)(2,1)}, bf16[24,512]{1,0:T(8,128)(2,1)S(1)}, u32[]{:S(2)}) copy-start(bf16[24,512]{1,0:T(8,128)(2,1)S(1)} %collective-permute-done.19.refs_3_) | copy-start | bytes 73732
  47.9 4.9 %collective-permute-start.23 = (bf16[24,512]{1,0:T(8,128)(2,1)S(1)}, bf16[24,512]{1,0:T(8,128)(2,1)S(1)}, u32[]{:S(2)}, u32[]{:S(2)}) collective-permute-start(bf16[24,512]{1,0:T(8,128)(2,1)S(1)} %collective-permute-done.19.refs_3_), channel_id=1, source_target_pairs={{0,1},{1,0},{2,3},{3,2},{4,5},{5,4},{6,7},{7,6},{8,9},{9,8},{10,11... | collective-permute-start | bytes 73736 | tf_op jit(solution)/shard_map/ppermute | solution.py:450
  47.9 6.5 %copy-start.23 = (bf16[24,512]{1,0:T(8,128)(2,1)}, bf16[24,512]{1,0:T(8,128)(2,1)S(1)}, u32[]{:S(2)}) copy-start(bf16[24,512]{1,0:T(8,128)(2,1)S(1)} %collective-permute-done.20.refs_4_) | copy-start | bytes 73732
  47.9 15.2 %collective-permute-start.14 = (bf16[192,256]{1,0:T(8,128)(2,1)S(1)}, bf16[192,256]{1,0:T(8,128)(2,1)S(1)}, u32[]{:S(2)}, u32[]{:S(2)}) collective-permute-start(bf16[192,256]{1,0:T(8,128)(2,1)S(1)} %copy-done.29), channel_id=1, source_target_pairs={{0,2},{1,3},{2,4},{3,5},{4,6},{5,7},{6,0},{7,1},{8,10},{9,11},{10,... | collective-permute-start | bytes 294920 | tf_op jit(solution)/shard_map/ppermute | solution.py:447
  49.7 4.7 %copy-start.24 = (bf16[24,512]{1,0:T(8,128)(2,1)}, bf16[24,512]{1,0:T(8,128)(2,1)S(1)}, u32[]{:S(2)}) copy-start(bf16[24,512]{1,0:T(8,128)(2,1)S(1)} %collective-permute-done.21.refs_5_) | copy-start | bytes 73732
  49.7 13.4 %collective-permute-start.15 = (bf16[192,256]{1,0:T(8,128)(2,1)S(1)}, bf16[192,256]{1,0:T(8,128)(2,1)S(1)}, u32[]{:S(2)}, u32[]{:S(2)}) collective-permute-start(bf16[192,256]{1,0:T(8,128)(2,1)S(1)} %copy-done.28), channel_id=1, source_target_pairs={{0,4},{1,5},{2,6},{3,7},{4,0},{5,1},{6,2},{7,3},{8,12},{9,13},{10,... | collective-permute-start | bytes 294920 | tf_op jit(solution)/shard_map/ppermute | solution.py:447
  52.7 1.7 %copy-start.25 = (bf16[24,512]{1,0:T(8,128)(2,1)}, bf16[24,512]{1,0:T(8,128)(2,1)S(1)}, u32[]{:S(2)}) copy-start(bf16[24,512]{1,0:T(8,128)(2,1)S(1)} %collective-permute-done.22.refs_6_) | copy-start | bytes 73732
  52.7 10.4 %collective-permute-start.16 = (bf16[192,256]{1,0:T(8,128)(2,1)S(1)}, bf16[192,256]{1,0:T(8,128)(2,1)S(1)}, u32[]{:S(2)}, u32[]{:S(2)}) collective-permute-start(bf16[192,256]{1,0:T(8,128)(2,1)S(1)} %copy-done.27), channel_id=1, source_target_pairs={{0,6},{1,7},{2,0},{3,1},{4,2},{5,3},{6,4},{7,5},{8,14},{9,15},{10,... | collective-permute-start | bytes 294920 | tf_op jit(solution)/shard_map/ppermute | solution.py:447
  52.8 1.6 %copy-start.26 = (bf16[24,512]{1,0:T(8,128)(2,1)}, bf16[24,512]{1,0:T(8,128)(2,1)S(1)}, u32[]{:S(2)}) copy-start(bf16[24,512]{1,0:T(8,128)(2,1)S(1)} %collective-permute-done.23.refs_7_) | copy-start | bytes 73732
  52.8 4.8 %collective-permute-start.25 = (bf16[336,128]{1,0:T(8,128)(2,1)}, bf16[336,128]{1,0:T(8,128)(2,1)S(1)}, u32[]{:S(2)}, u32[]{:S(2)}) collective-permute-start(bf16[336,128]{1,0:T(8,128)(2,1)} %get-tuple-element.39), channel_id=1, source_target_pairs={{0,16},{8,24},{16,0},{24,8},{1,17},{9,25},{17,1},{25,9},{2,18},{10... | collective-permute-start | bytes 258056 | tf_op jit(solution)/shard_map/ppermute | solution.py:453
  53.7 2.5 %copy-start.13 = (bf16[336,128]{1,0:T(8,128)(2,1)}, bf16[336,128]{1,0:T(8,128)(2,1)S(1)}, u32[]{:S(2)}) copy-start(bf16[336,128]{1,0:T(8,128)(2,1)S(1)} %collective-permute-done.24.refs_0_) | copy-start | bytes 258052
  53.7 4.7 %collective-permute-start.26 = (bf16[336,128]{1,0:T(8,128)(2,1)}, bf16[336,128]{1,0:T(8,128)(2,1)S(1)}, u32[]{:S(2)}, u32[]{:S(2)}) collective-permute-start(bf16[336,128]{1,0:T(8,128)(2,1)} %get-tuple-element.40), channel_id=1, source_target_pairs={{0,24},{8,0},{16,8},{24,16},{1,25},{9,1},{17,9},{25,17},{2,26},{10... | collective-permute-start | bytes 258056 | tf_op jit(solution)/shard_map/ppermute | solution.py:453
  57.6 0.8 %copy-start.14 = (bf16[336,128]{1,0:T(8,128)(2,1)}, bf16[336,128]{1,0:T(8,128)(2,1)S(1)}, u32[]{:S(2)}) copy-start(bf16[336,128]{1,0:T(8,128)(2,1)S(1)} %collective-permute-done.25.refs_1_) | copy-start | bytes 258052
  58.4 0.6 copy-start.15
  63.1 0.6 copy-start.10
  63.1 0.7 %copy-start.11 = (bf16[192,256]{1,0:T(8,128)(2,1)}, bf16[192,256]{1,0:T(8,128)(2,1)S(1)}, u32[]{:S(2)}) copy-start(bf16[192,256]{1,0:T(8,128)(2,1)S(1)} %collective-permute-done.15.refs_7_) | copy-start | bytes 294916
  63.2 0.7 %copy-start.12 = (bf16[192,256]{1,0:T(8,128)(2,1)}, bf16[192,256]{1,0:T(8,128)(2,1)S(1)}, u32[]{:S(2)}) copy-start(bf16[192,256]{1,0:T(8,128)(2,1)S(1)} %collective-permute-done.16.refs_8_) | copy-start | bytes 294916

commit v2 on v0

v2 whole, which is shorter than its diff:
```python
import functools

import jax
import jax.numpy as jnp
from jax import lax
from jax.experimental import pallas as pl
from jax.experimental.pallas import tpu as pltpu
from jax.sharding import PartitionSpec as P

G = 32
EPSILON = 1e-05
WIDE = 256
HALF_TAPS = 14
FRAMES, HEIGHT, WIDTH = 4, 8, 8
CELLS = FRAMES * HEIGHT * WIDTH
BF16, F32 = jnp.bfloat16, jnp.float32
NT = (((1,), (1,)), ((), ()))

TAPS = [9 * a + 3 * b + e for b in range(3) for a in range(3) for e in range(3)]


def up(value, multiple):
    return -(-value // multiple) * multiple


def roll(x, shift):
    size = x.shape[-1]
    shift = shift % size
    return pltpu.roll(x, shift, x.ndim - 1) if shift else x


def dot(x, y):
    return jnp.dot(x, y, preferred_element_type=F32)


def exact_dot(x, y):
    return jnp.dot(x, y, preferred_element_type=F32, precision=lax.Precision.HIGHEST)


def place():
    position = lax.axis_index("tile")
    core = lax.rem(position, 2)
    return lax.div(position, 2), core, core == 0


def cell_index(shape, axis):
    cell = lax.broadcasted_iota(jnp.int32, shape, axis)
    return (
        lax.shift_right_logical(cell, 6),
        lax.bitwise_and(lax.shift_right_logical(cell, 3), 7),
        lax.bitwise_and(cell, 7),
    )


def column(row_ref, channel_of, rows):
    channels = row_ref.shape[1]
    lane = lax.broadcasted_iota(jnp.int32, (rows, channels), 1)
    index = channel_of(lax.broadcasted_iota(jnp.int32, (rows, channels), 0))
    return jnp.sum(jnp.where(lane == index, row_ref[...], 0.0), axis=1, keepdims=True)


def block_row(index, real, padded):
    block = index // padded
    return block, index - block * padded


def prepare_kernel(nc, ir, irp, x_hbm, g_hbm, w_hbm, *rest):
    outs, (w_out, x_ref, g_ref, w_ref, blocks, packed, sems) = rest[:nc], rest[nc:]
    cbp = 2 * irp
    ob = w_ref.shape[2]
    copies = [
        pltpu.make_async_copy(src, dst, sems.at[i])
        for i, (src, dst) in enumerate(((x_hbm, x_ref), (g_hbm, g_ref), (w_hbm, w_ref)))
    ]
    for copy in copies:
        copy.start()
    chip = place()[0]
    packed[...] = jnp.zeros_like(packed)
    if irp != ir:
        blocks[...] = jnp.zeros_like(blocks)
    copies[0].wait()
    turned = x_ref[...].astype(F32).T
    for q in range(nc):
        for core in range(2):
            at = (2 * q + core) * ir
            blocks[q, core * irp : core * irp + ir, :] = turned[at : at + ir]
    for j in range(nc):
        mine = blocks[lax.bitwise_xor(chip, j)].astype(BF16)
        outs[j][0:cbp] = mine[:, :128]
        outs[j][cbp : 2 * cbp] = mine[:, 128:]
    copies[1].wait()
    low = g_ref[:, :128]
    high = g_ref[:, 128:192].astype(F32)
    high = jnp.concatenate([high[: CELLS // 2], high[CELLS // 2 :]], axis=1).astype(BF16)
    for j in range(nc):
        outs[j][2 * cbp : 2 * cbp + CELLS] = low
        outs[j][2 * cbp + CELLS :] = high
    copies[2].wait()
    for u in range(27):
        p, start = (u, 0) if u < HALF_TAPS else (u - HALF_TAPS, 64)
        packed[p * irp : p * irp + ir, start : start + ob] = w_ref[TAPS[u]].astype(F32)
    w_out[...] = packed[...].astype(BF16)


def setup_kernel(n, nd, ir, irp, ob, channels, *refs):
    clip_ref, rows_ref, cols_ref, start_ref, gamma_ref, beta_ref, bias_ref = refs[:7]
    w_sets, refs = (refs[7 : 7 + nd], refs[7 + nd : 7 + 2 * nd]), refs[7 + 2 * nd :]
    conv_out, grad_out, lanes_out, rows_out, columns_out, tiles_out, end_out, bias_out = refs
    group_size = channels // G
    cbp = 2 * irp
    chip = place()[0]
    position = lax.axis_index("tile")
    clip = [clip_ref[0, m] for m in range(n)]
    rows = [rows_ref[0, m] for m in range(n)]
    cols = [cols_ref[0, clip[m]] for m in range(n)]
    start = [start_ref[0, clip[m]] for m in range(n)]
    same = [[(clip[k] == clip[m]).astype(jnp.int32) for k in range(n)] for m in range(n)]
    above = [same[m][m - 1] if m else jnp.int32(0) for m in range(n)]
    below = [same[m][m + 1] if m < n - 1 else jnp.int32(0) for m in range(n)]

    def valid(m, f, r, c):
        return (f >= start[m]) & (r < rows[m]) & (c < cols[m])

    f, r, c = cell_index((1, CELLS), 1)
    lanes_out[...] = jnp.zeros_like(lanes_out)
    for m in range(n):
        at = slice(m * CELLS, (m + 1) * CELLS)
        lanes_out[0:1, at] = valid(m, f, r, c).astype(F32)
        lanes_out[1:2, at] = ((r > 0) | (above[m] > 0)).astype(F32)
        lanes_out[2:3, at] = ((r < 7) | (below[m] > 0)).astype(F32)
    own_clip = clip_ref[0, position]
    inside = (f >= start_ref[0, own_clip]) & (r < rows_ref[0, position]) & (c < cols_ref[0, own_clip])
    end_out[...] = jnp.broadcast_to(inside.astype(F32), end_out.shape)
    f, r, c = cell_index((CELLS, 128), 0)
    for m in range(n):
        rows_out[m * CELLS : (m + 1) * CELLS] = valid(m, f, r, c).astype(F32)
    lane = lax.broadcasted_iota(jnp.int32, (1, 128), 1)
    count = jnp.ones((1, 128), jnp.int32)
    tiles_out[...] = jnp.zeros_like(tiles_out)
    for m in range(n):
        clip_rows = jnp.int32(0)
        mates = jnp.zeros((1, 128), jnp.int32)
        for k in range(n):
            clip_rows += same[m][k] * rows[k]
            mates = jnp.where(lane == k, same[m][k], mates)
        cells = (FRAMES - start[m]) * cols[m] * clip_rows * group_size
        count = jnp.where(lane == m, cells, count)
        tiles_out[0, m : m + 1] = mates.astype(F32)
        tiles_out[1, m : m + 1] = jnp.full((1, 128), above[m]).astype(F32)
        tiles_out[2, m : m + 1] = jnp.full((1, 128), below[m]).astype(F32)
    tiles_out[3, 0:1] = count.astype(F32)

    def channel(index):
        block, inner = block_row(index, ir, irp)
        return jnp.where(inner < ir, chip * 2 * ir + block * ir + inner, -1)

    columns_out[0] = jnp.broadcast_to(column(gamma_ref, channel, cbp), (cbp, 128))
    columns_out[1] = jnp.broadcast_to(column(beta_ref, channel, cbp), (cbp, 128))
    bias_out[...] = jnp.broadcast_to(column(bias_ref, lambda index: index, channels), (channels, 128))
    dp = lax.axis_index("dp")
    straight_picks, turned_picks = [], []
    for first in (0, 64):
        picks, flipped = [], []
        for j in range(nd):
            base = lax.bitwise_xor(dp, j) * ob
            for dims, axis, into in (((128, WIDE), 1, picks), ((WIDE, 128), 0, flipped)):
                lane = lax.broadcasted_iota(jnp.int32, dims, 1 - axis) - first
                out = lax.broadcasted_iota(jnp.int32, dims, axis) - base
                into.append(((lane == out) & (lane >= 0) & (lane < ob)).astype(F32))
        straight_picks.append(jnp.concatenate(picks, axis=0).astype(BF16))
        turned_picks.append(jnp.concatenate(flipped, axis=1).astype(BF16))
    pad = grad_out.shape[1] - 9 * irp
    for s, w_refs in enumerate(w_sets):
        joined = jnp.concatenate([ref[...] for ref in w_refs], axis=1)
        turned = [lax.dot_general(pick, joined, NT, preferred_element_type=F32) for pick in turned_picks]
        conv_out[s] = jnp.concatenate(turned, axis=1)[:channels].astype(BF16)
        straight = jnp.concatenate([dot(joined, pick) for pick in straight_picks], axis=0)
        grad = jnp.concatenate([straight[b * 9 * irp : (b + 1) * 9 * irp] for b in range(3)], axis=1)
        if pad:
            grad = jnp.concatenate([grad, jnp.zeros((pad, 3 * WIDE), F32)], axis=0)
        grad_out[s] = grad.astype(BF16)


def row_neighbours(x, edges_ref):
    n = x.shape[1] // CELLS
    r = jnp.concatenate([cell_index((1, CELLS), 1)[1]] * n, axis=1)
    above = roll(jnp.where(r == 7, roll(x, CELLS - 64), x), 8) * edges_ref[1:2, :]
    below = roll(jnp.where(r == 0, roll(x, 64 - CELLS), x), -8) * edges_ref[2:3, :]
    return above, below


def shifts(x, f, c):
    for e in range(3):
        if e == 0:
            moved = jnp.where(c > 0, roll(x, 1), 0.0)
        elif e == 2:
            moved = jnp.where(c < 7, roll(x, -1), 0.0)
        else:
            moved = x
        for a in range(3):
            late = 2 - a
            yield a, e, (jnp.where(f >= late, roll(moved, 64 * late), 0.0) if late else moved)


def store_patches(ref, variants, f, c, irp):
    blocks = {}
    for b, rows in enumerate(variants):
        for a, e, block in shifts(rows, f, c):
            blocks[9 * b + 3 * a + e] = block
    blocks[27] = jnp.zeros_like(blocks[0])
    for p in range(HALF_TAPS):
        both = jnp.concatenate([blocks[2 * p], blocks[2 * p + 1]], axis=0)
        ref[2 * p * irp : 2 * (p + 1) * irp] = both.astype(BF16)


def main_kernel(nc, nd, ir, irp, ob, channels, *refs):
    n = 2 * nc
    cbp = 2 * irp
    width = n * CELLS
    group_size = channels // G
    lanes_ref, rows_ref, columns_ref, tiles_ref = refs[:4]
    conv_weight, grad_weight, refs = *refs[4:6], refs[6:]
    own, other, refs = refs[:nc], refs[nc:n], refs[n:]
    outs, refs = refs[:nc], refs[nc:]
    w_outs, (features, grads, shifted, patches, own_patches, ends) = refs[:nd], refs[nd:]
    chip, core, even = place()
    lane = lax.broadcasted_iota(jnp.int32, (CELLS // 2, 128), 1)
    for j in range(nc):
        source = 2 * lax.bitwise_xor(chip, j)
        for m, ref in ((source + core, own[j]), (source + 1 - core, other[j])):
            features[m] = jnp.concatenate([ref[0:cbp], ref[cbp : 2 * cbp]], axis=1).astype(F32)
            low = ref[2 * cbp : 2 * cbp + CELLS].astype(F32)
            high = ref[2 * cbp + CELLS :].astype(F32)
            right = [jnp.where(lane < 64, high, 0.0), jnp.where(lane < 64, roll(high, 64), 0.0)]
            grads[m] = jnp.concatenate([low, jnp.concatenate(right, axis=0)], axis=1)
    gamma, beta = columns_ref[0][:, :1], columns_ref[1][:, :1]
    counted = tiles_ref[3, 0:1]

    def clip_totals(sums):
        total = jnp.zeros((cbp, 128), F32)
        for m in range(n):
            total = total + sums[m] * tiles_ref[0, m : m + 1]
        return total

    def group_of(axis):
        index = lax.broadcasted_iota(jnp.int32, (cbp, cbp), axis)
        block, inner = block_row(index, ir, irp)
        return jnp.where(inner < ir, (block * ir + inner) // group_size, -1 - index)

    groups = (group_of(0) == group_of(1)).astype(F32)
    valid, first, square = [], [], []
    for m in range(n):
        keep = lanes_ref[0:1, m * CELLS : (m + 1) * CELLS]
        block = features[m] * keep
        features[m] = block
        valid.append(keep)
        first.append(jnp.sum(block, axis=1, keepdims=True))
        square.append(jnp.sum(block * block, axis=1, keepdims=True))
    mean = exact_dot(groups, clip_totals(first)) / counted
    variance = exact_dot(groups, clip_totals(square)) / counted - mean * mean
    inv_std = lax.rsqrt(variance + EPSILON)

    def normed_of(m):
        return (features[m] - mean[:, m : m + 1]) * inv_std[:, m : m + 1]

    hidden = []
    for m in range(n):
        activation = normed_of(m) * gamma + beta
        hidden.append(activation * jax.nn.sigmoid(activation) * valid[m])
    hidden = jnp.concatenate(hidden, axis=1).astype(BF16).astype(F32)
    above, below = row_neighbours(hidden, lanes_ref)

    def own_rows(x):
        return jnp.where(even, x[:irp], x[irp:])

    def other_rows(x):
        return jnp.where(even, x[irp:], x[:irp])

    def own_tiles(x):
        parts = []
        for k in range(nc):
            low = x[:, 2 * k * CELLS : (2 * k + 1) * CELLS]
            high = x[:, (2 * k + 1) * CELLS : (2 * k + 2) * CELLS]
            parts.append(jnp.where(even, low, high))
        return jnp.concatenate(parts, axis=1)

    frame, _, col = cell_index((1, CELLS), 1)
    f, c = jnp.concatenate([frame] * nc, axis=1), jnp.concatenate([col] * nc, axis=1)
    total = None
    for s, rows_of in enumerate((own_rows, other_rows)):
        part = patches.at[s]
        store_patches(part, [own_tiles(rows_of(x)) for x in (above, hidden, below)], f, c, irp)
        product = dot(conv_weight[s], part[...])
        total = product if total is None else total + product
    for k in range(nc):
        ends[k, :channels] = total[:, k * CELLS : (k + 1) * CELLS]

    for m in range(n):
        keep = rows_ref[m * CELLS : (m + 1) * CELLS]
        grads[m] = grads[m] * jnp.concatenate([keep, keep], axis=1)
    split = (FRAMES, HEIGHT, WIDTH, WIDE)
    for m in range(n):
        here = grads[m]
        rows = here.reshape(split)
        has = [jnp.concatenate([tiles_ref[i, m : m + 1]] * 2, axis=1) for i in (1, 2)]
        last = grads[max(m - 1, 0)].reshape(split)[:, 7:] * has[0]
        next_ = grads[min(m + 1, n - 1)].reshape(split)[:, :1] * has[1]
        at = slice(m * CELLS, (m + 1) * CELLS)
        shifted[at, :WIDE] = jnp.concatenate([rows[:, 1:], next_], axis=1).reshape(CELLS, WIDE).astype(BF16)
        shifted[at, WIDE : 2 * WIDE] = here.astype(BF16)
        shifted[at, 2 * WIDE :] = jnp.concatenate([last, rows[:, :7]], axis=1).reshape(CELLS, WIDE).astype(BF16)
    weight = jnp.concatenate([grad_weight[0], grad_weight[1]], axis=0)
    total = lax.dot_general(weight, shifted[...], NT, preferred_element_type=F32)
    f, c = jnp.concatenate([frame] * n, axis=1), jnp.concatenate([col] * n, axis=1)
    halves = []
    for s in range(2):
        base = s * grad_weight.shape[1]
        hidden_grad = jnp.zeros((irp, width), F32)
        for e in range(3):
            moved = jnp.zeros((irp, width), F32)
            for a in range(3):
                late = 2 - a
                at = base + (3 * a + e) * irp
                block = total[at : at + irp]
                moved = moved + (jnp.where(f < FRAMES - late, roll(block, -64 * late), 0.0) if late else block)
            if e == 0:
                moved = jnp.where(c < 7, roll(moved, -1), 0.0)
            elif e == 2:
                moved = jnp.where(c > 0, roll(moved, 1), 0.0)
            hidden_grad = hidden_grad + moved
        halves.append(hidden_grad)
    hidden_grad = jnp.concatenate([jnp.where(even, *halves), jnp.where(even, *halves[::-1])], axis=0)
    dnormed, first, second = [], [], []
    for m in range(n):
        norm = normed_of(m)
        activation = norm * gamma + beta
        s = jax.nn.sigmoid(activation)
        grad = hidden_grad[:, m * CELLS : (m + 1) * CELLS]
        grad = grad * valid[m] * s * (1.0 + activation * (1.0 - s)) * gamma
        dnormed.append(grad)
        first.append(jnp.sum(grad, axis=1, keepdims=True))
        second.append(jnp.sum(grad * norm, axis=1, keepdims=True))
    first_total = exact_dot(groups, clip_totals(first)) / counted
    second_total = exact_dot(groups, clip_totals(second)) / counted
    for k in range(nc):
        pair = []
        for m in (2 * k, 2 * k + 1):
            grad = dnormed[m] - first_total[:, m : m + 1] - normed_of(m) * second_total[:, m : m + 1]
            pair.append(grad * inv_std[:, m : m + 1] * valid[m])
        ends[k, channels:] = jnp.where(even, *pair)
    for j in range(nc):
        outs[j][...] = ends[lax.bitwise_xor(chip, j)].astype(outs[j].dtype)

    store_patches(own_patches, [own_rows(x) for x in (above, hidden, below)], f, c, irp)
    product = dot(own_patches[...], shifted[:, WIDE : 2 * WIDE])
    dp = lax.axis_index("dp")
    half = HALF_TAPS * irp
    lane = lax.broadcasted_iota(jnp.int32, (half, 128), 1)
    for j in range(nd):
        target = lax.bitwise_xor(dp, j)
        moved = pltpu.roll(product, lax.rem(WIDE - target * ob, WIDE), 1)[:, :128]
        low = jnp.where(lane < ob, moved[:half], 0.0)
        high = jnp.where(lane < ob, moved[half:], 0.0)
        w_outs[j][...] = (low + roll(high, 64)).astype(w_outs[j].dtype)


def end_kernel(n, nd, ir, irp, ob, channels, *refs):
    nc = n // 2
    bias_ref, inside_ref, refs = refs[0], refs[1], refs[2:]
    received, refs = refs[:nc], refs[nc:]
    w_refs, refs = refs[:nd], refs[nd:]
    conv_ref, grad_ref, weight_ref, blocks, total = refs
    chip = place()[0]
    value = w_refs[0][...]
    for ref in w_refs[1:]:
        value = value + ref[...].astype(F32)
    total[...] = value
    for u in range(27):
        p, at = (u, 0) if u < HALF_TAPS else (u - HALF_TAPS, 64)
        weight_ref[TAPS[u]] = total[p * irp : p * irp + ir, at : at + ob]
    conv = received[0][:channels]
    for ref in received[1:]:
        conv = conv + ref[:channels].astype(F32)
    bias = bias_ref[...]
    conv = (conv + jnp.concatenate([bias, bias], axis=1)) * inside_ref[0:1]
    conv_ref[...] = conv.T.astype(BF16)
    for j in range(nc):
        blocks[lax.bitwise_xor(chip, j)] = received[j][channels:].astype(F32)
    parts = [blocks[q, core * irp : core * irp + ir] for q in range(nc) for core in range(2)]
    grad_ref[...] = jnp.concatenate(parts, axis=0).T.astype(BF16)


def on_device(
    features, out_grad, weight, bias, gamma, beta, tile_clip, tile_rows, clip_cols, clip_start
):
    n, nd = lax.axis_size("tile"), lax.axis_size("dp")
    nc = n // 2
    channels = features.shape[-1]
    ir, _, ob = weight.shape
    irp = up(ir, 8)
    cbp = 2 * irp
    width = n * CELLS
    half = HALF_TAPS * irp
    smem = pl.BlockSpec(memory_space=pltpu.SMEM)
    vmem = pl.BlockSpec(memory_space=pltpu.VMEM)
    hbm = pl.BlockSpec(memory_space=pltpu.HBM)

    def shape(dims, dtype=BF16):
        return jax.ShapeDtypeStruct(dims, dtype)

    def call(kernel, args, out, scratch=(), specs=None, us=1.0, room=8, after=()):
        def body(*refs):
            kernel[0](*kernel[1:], *refs[: len(args)], *refs[len(args) + len(after) :])

        return pl.pallas_call(
            body,
            out_shape=out,
            in_specs=(specs or [vmem] * len(args)) + [hbm] * len(after),
            out_specs=jax.tree.map(lambda _: vmem, out),
            scratch_shapes=list(scratch),
            compiler_params=pltpu.CompilerParams(vmem_limit_bytes=room << 20),
            cost_estimate=pl.CostEstimate(flops=int(us * 1e9), bytes_accessed=0, transcendentals=0),
        )(*args, *after)

    def along_chips(x, j):
        return lax.ppermute(x, "tile", [(i, i ^ (2 * j)) for i in range(n)])

    def swap(x):
        return lax.ppermute(x, "tile", [(i, i ^ 1) for i in range(n)])

    def along_dp(x, j):
        return lax.ppermute(x, "dp", [(i, i ^ j) for i in range(nd)])

    packed_rows = 2 * cbp + CELLS + CELLS // 2
    sent = call(
        (prepare_kernel, nc, ir, irp),
        tuple(
            pltpu.with_memory_space_constraint(x, pltpu.HBM)
            for x in (
                features.reshape(CELLS, channels),
                out_grad.reshape(CELLS, channels),
                weight.transpose(1, 0, 2),
            )
        ),
        [shape((packed_rows, 128))] * nc + [shape((half, 128))],
        [
            pltpu.VMEM((CELLS, channels), BF16),
            pltpu.VMEM((CELLS, channels), BF16),
            pltpu.VMEM((27, ir, ob), BF16),
            pltpu.VMEM((nc, cbp, CELLS), F32),
            pltpu.VMEM((half, 128), F32),
            pltpu.SemaphoreType.DMA((3,)),
        ],
        [hbm] * 3,
    )
    sent, w_block = sent[:nc], sent[nc]
    own = [sent[0]] + [along_chips(sent[j], j) for j in range(1, nc)]
    other = [swap(x) for x in own]
    w_blocks = [w_block] + [along_dp(w_block, j) for j in range(1, nd)]
    w_blocks += [swap(x) for x in w_blocks]

    tables = (tile_clip, tile_rows, clip_cols, clip_start)
    ready = call(
        (setup_kernel, n, nd, ir, irp, ob, channels),
        (*tables, gamma[None], beta[None], bias[None], *w_blocks),
        [
            shape((2, channels, 2 * half)),
            shape((2, up(9 * irp, 16), 3 * WIDE)),
            shape((8, width), F32),
            shape((width, 128), F32),
            shape((2, cbp, 128), F32),
            shape((4, up(n, 8), 128), F32),
            shape((8, CELLS), F32),
            shape((channels, 128), F32),
        ],
        (),
        [smem] * 4 + [vmem] * (3 + 2 * nd),
        after=own[-1:],
    )
    conv_weight, grad_weight, lanes, rows, columns, tiles, inside, bias_columns = ready

    parts = call(
        (main_kernel, nc, nd, ir, irp, ob, channels),
        (lanes, rows, columns, tiles, conv_weight, grad_weight)
        + (*own, *other),
        [shape((channels + cbp, CELLS), F32)]
        + [shape((channels + cbp, CELLS))] * (nc - 1)
        + [shape((half, 128), F32)]
        + [shape((half, 128))] * (nd - 1),
        [
            pltpu.VMEM((n, cbp, CELLS), F32),
            pltpu.VMEM((n, CELLS, WIDE), F32),
            pltpu.VMEM((width, 3 * WIDE), BF16),
            pltpu.VMEM((2, 2 * half, nc * CELLS), BF16),
            pltpu.VMEM((2 * half, width), BF16),
            pltpu.VMEM((nc, channels + cbp, CELLS), F32),
        ],
        None,
        8.0,
        16 + 5 * n // 4,
    )
    ends, w_parts = parts[:nc], parts[nc:]
    w_received = [w_parts[0]] + [along_dp(w_parts[j], j) for j in range(1, nd)]
    ends = [ends[0]] + [along_chips(ends[j], j) for j in range(1, nc)]
    conv_out, input_grad, weight_grad = call(
        (end_kernel, n, nd, ir, irp, ob, channels),
        (bias_columns, inside, *ends, *w_received),
        [shape((CELLS, channels)), shape((CELLS, channels)), shape((27, ir, ob), F32)],
        [pltpu.VMEM((nc, cbp, CELLS), F32), pltpu.VMEM((half, 128), F32)],
    )
    return (
        conv_out.reshape(features.shape),
        input_grad.reshape(features.shape),
        weight_grad.transpose(1, 0, 2),
    )


def solution(mesh):
    in_specs = (
        P("dp", None, "tile", None, None),
        P("dp", None, "tile", None, None),
        P("tile", None, "dp"),
        P(),
        P(),
        P(),
        P("dp", None),
        P("dp", None),
        P("dp", None),
        P("dp", None),
    )
    out_specs = (
        P("dp", None, "tile", None, None),
        P("dp", None, "tile", None, None),
        P("tile", None, "dp"),
    )
    return jax.shard_map(
        on_device, mesh=mesh, in_specs=in_specs, out_specs=out_specs, check_vma=False
    )
```

time: 205 us -> 44.2 us (0.22)
  local copies, waits for them, and re-layouts: 53.4 us -> 0.66 us
  blocking collectives: 50 us -> 0 us
  waiting for transfers between devices: 51.2 us -> 13 us
  between operations: 19.1 us -> 0.78 us
  other arithmetic: 17.1 us -> 0 us
  starting transfers between devices: 2.88 us -> 19 us
  Pallas kernels: 0 us -> 10.5 us
  matrix products: 10.1 us -> 0 us
    reduce_scatter x1 -> x0, waiting for transfers between devices: 34.6 us -> none  [on_device(): lax.psum_scatter(product.reshape(owned * lax.axis_size('tile'), 27, chann...]
    psum x2 -> x0, blocking collectives: 33.3 us -> none  [the longest x1 18.3 us: on_device(): lax.psum((select * first_sum[None, :], select * square_sum[None, :]), 'ti...]
    unnamed x63 -> x14, local copies, waits for them, and re-layouts: 17.6 us -> 0.66 us
    all_gather x1 -> x0, blocking collectives: 16.7 us -> none  [on_device(): weight_rows = lax.all_gather(weight, 'dp', axis=2, tiled=True)]
    unnamed x4 -> x0, waiting for transfers between devices: 16.5 us -> none
    ppermute x2 -> x20, starting transfers between devices: 2.58 us -> 19 us  [the longest x6 9.31 us: along_chips(): return lax.ppermute(x, 'tile', [(i, i ^ 2 * j) for i in range(n)])]
    reshape x1 -> x0, local copies, waits for them, and re-layouts: 15.2 us -> none  [tap_stack(): return stacked.reshape(-1, count * 27)]
    ppermute x2 -> x20, waiting for transfers between devices: 0.01 us -> 13 us  [the longest x6 6.89 us: along_chips(): return lax.ppermute(x, 'tile', [(i, i ^ 2 * j) for i in range(n)])]
  transfers between devices with their start and end apart: 5 -> 20, of which waited for: 2 -> 7; matrix products, arithmetic and copies ran while one was open for 26% -> 0% of each run, Pallas kernels for 0% -> 4%
where the time goes in v2:
time: 44.2 us; the launch traced here: 44 us
  starting transfers between devices  19 us (43%)
  waiting for transfers between devices  13 us (29%)
  Pallas kernels  10.5 us (24%)
  between operations  0.78 us (2%)
  local copies, waits for them, and re-layouts  0.66 us (1%)
    pallas_call x4, Pallas kernels, call(): pl.pallas_call(body, out_shape=out, in_specs=(specs or [vmem] * len(args)...  10.5 us
    ppermute x6, starting transfers between devices, along_chips(): return lax.ppermute(x, 'tile', [(i, i ^ 2 * j) for i in range(n)])  9.31 us
    ppermute x6, starting transfers between devices, along_dp(): return lax.ppermute(x, 'dp', [(i, i ^ j) for i in range(nd)])  8.12 us
    ppermute x6, waiting for transfers between devices, along_chips(): return lax.ppermute(x, 'tile', [(i, i ^ 2 * j) for i in range(n)])  6.89 us
    ppermute x6, waiting for transfers between devices, along_dp(): return lax.ppermute(x, 'dp', [(i, i ^ j) for i in range(nd)])  6.09 us
    ppermute x8, starting transfers between devices, swap(): return lax.ppermute(x, 'tile', [(i, i ^ 1) for i in range(n)])  1.61 us
  transfers between devices with their start and end apart: 20, of which 7 were waited for; matrix products, arithmetic and copies ran while one was open for 0% of the time, Pallas kernels for 4%

profile of v2, /device:TPU:0, one launch (start us, length us, event | category | flops | bytes accessed | tf_op | source)
XLA Modules:
  0.0 44.0 jit_solution(3399818185582555261)
XLA Ops:
  0.6 0.0 copy-start.1
  0.6 0.0 copy-start.2
  0.7 0.0 copy-start.4
  0.7 0.0 copy-start.5
  0.7 0.0 copy-start.6
  0.7 1.3 %shard_map.121 = (bf16[480,128]{1,0:T(8,128)(2,1)S(1)}, bf16[480,128]{1,0:T(8,128)(2,1)S(1)}, bf16[480,128]{1,0:T(8,128)(2,1)S(1)}, bf16[480,128]{1,0:T(8,128)(2,1)S(1)}, bf16[336,128]{1,0:T(8,128)(2,1)S(1)}) custom-call(bf16[256,192]{1,0:T(8,128)(2,1)} %bitcast.13, bf16[256,192]{1,0:T(8,128)(2,1)} %bitcast.14, bf16[27,24,48]{2,1,0:T(8,128)(2,1)} %bitcast.12), custom_call_target="tpu_custom_call" | custom-call | flops 1000000000 | tf_op jit(solution)/shard_map/pallas_call | solution.py:415
  2.0 0.5 %collective-permute-start.3 = (bf16[336,128]{1,0:T(8,128)(2,1)S(1)}, bf16[336,128]{1,0:T(8,128)(2,1)S(1)}, u32[]{:S(2)}, u32[]{:S(2)}) collective-permute-start(bf16[336,128]{1,0:T(8,128)(2,1)S(1)} %get-tuple-element.27.refs_7_), channel_id=1, source_target_pairs={{0,1},{1,0},{2,3},{3,2},{4,5},{5,4},{6,7},{7,6},{8,9},{9,8},{10,11... | collective-permute-start | bytes 258056 | tf_op jit(solution)/shard_map/ppermute | solution.py:429
  2.5 3.5 %collective-permute-start.2 = (bf16[336,128]{1,0:T(8,128)(2,1)S(1)}, bf16[336,128]{1,0:T(8,128)(2,1)S(1)}, u32[]{:S(2)}, u32[]{:S(2)}) collective-permute-start(bf16[336,128]{1,0:T(8,128)(2,1)S(1)} %get-tuple-element.27.refs_7_), channel_id=1, source_target_pairs={{0,24},{8,16},{16,8},{24,0},{1,25},{9,17},{17,9},{25,1},{2,26},{10... | collective-permute-start | bytes 258056 | tf_op jit(solution)/shard_map/ppermute | solution.py:432
  6.0 3.6 %collective-permute-start.7 = (bf16[480,128]{1,0:T(8,128)(2,1)S(1)}, bf16[480,128]{1,0:T(8,128)(2,1)S(1)}, u32[]{:S(2)}, u32[]{:S(2)}) collective-permute-start(bf16[480,128]{1,0:T(8,128)(2,1)S(1)} %get-tuple-element.28), channel_id=1, source_target_pairs={{0,6},{1,7},{2,4},{3,5},{4,2},{5,3},{6,0},{7,1},{8,14},{9,15},{10,... | collective-permute-start | bytes 368648 | tf_op jit(solution)/shard_map/ppermute | solution.py:426
  9.6 0.5 %collective-permute-start.1 = (bf16[336,128]{1,0:T(8,128)(2,1)S(1)}, bf16[336,128]{1,0:T(8,128)(2,1)S(1)}, u32[]{:S(2)}, u32[]{:S(2)}) collective-permute-start(bf16[336,128]{1,0:T(8,128)(2,1)S(1)} %get-tuple-element.27.refs_7_), channel_id=1, source_target_pairs={{0,16},{8,24},{16,0},{24,8},{1,17},{9,25},{17,1},{25,9},{2,18},{10... | collective-permute-start | bytes 258056 | tf_op jit(solution)/shard_map/ppermute | solution.py:432
  10.1 0.5 %collective-permute-start = (bf16[336,128]{1,0:T(8,128)(2,1)S(1)}, bf16[336,128]{1,0:T(8,128)(2,1)S(1)}, u32[]{:S(2)}, u32[]{:S(2)}) collective-permute-start(bf16[336,128]{1,0:T(8,128)(2,1)S(1)} %get-tuple-element.27.refs_7_), channel_id=1, source_target_pairs={{0,8},{8,0},{16,24},{24,16},{1,9},{9,1},{17,25},{25,17},{2,10},{10... | collective-permute-start | bytes 258056 | tf_op jit(solution)/shard_map/ppermute | solution.py:432
  10.7 0.0 collective-permute-done.3.refs_11_
  10.7 0.0 collective-permute-start.8
  10.7 0.0 collective-permute-done.2.refs_10_
  10.7 1.3 %collective-permute-start.9 = (bf16[480,128]{1,0:T(8,128)(2,1)S(1)}, bf16[480,128]{1,0:T(8,128)(2,1)S(1)}, u32[]{:S(2)}, u32[]{:S(2)}) collective-permute-start(bf16[480,128]{1,0:T(8,128)(2,1)S(1)} %get-tuple-element.39), channel_id=1, source_target_pairs={{0,4},{1,5},{2,6},{3,7},{4,0},{5,1},{6,2},{7,3},{8,12},{9,13},{10,... | collective-permute-start | bytes 368648 | tf_op jit(solution)/shard_map/ppermute | solution.py:426
  12.0 2.1 %collective-permute-done.1.refs_9_ = bf16[336,128]{1,0:T(8,128)(2,1)S(1)} collective-permute-done((bf16[336,128]{1,0:T(8,128)(2,1)S(1)}, bf16[336,128]{1,0:T(8,128)(2,1)S(1)}, u32[]{:S(2)}, u32[]{:S(2)}) %collective-permute-start.1) | collective-permute-done | bytes 86048 | tf_op jit(solution)/shard_map/ppermute | solution.py:432
  14.1 0.0 collective-permute-start.6
  14.1 0.5 %collective-permute-done.refs_8_ = bf16[336,128]{1,0:T(8,128)(2,1)S(1)} collective-permute-done((bf16[336,128]{1,0:T(8,128)(2,1)S(1)}, bf16[336,128]{1,0:T(8,128)(2,1)S(1)}, u32[]{:S(2)}, u32[]{:S(2)}) %collective-permute-start) | collective-permute-done | bytes 86048 | tf_op jit(solution)/shard_map/ppermute | solution.py:432
  14.6 0.0 collective-permute-start.5
  14.6 0.0 collective-permute-done.7.refs_15_.refs_9_
  14.6 0.5 %collective-permute-start.4 = (bf16[336,128]{1,0:T(8,128)(2,1)S(1)}, bf16[336,128]{1,0:T(8,128)(2,1)S(1)}, u32[]{:S(2)}, u32[]{:S(2)}) collective-permute-start(bf16[336,128]{1,0:T(8,128)(2,1)S(1)} %collective-permute-done.refs_8_), channel_id=1, source_target_pairs={{0,1},{1,0},{2,3},{3,2},{4,5},{5,4},{6,7},{7,6},{8,9},{9,8},{10,11... | collective-permute-start | bytes 258056 | tf_op jit(solution)/shard_map/ppermute | solution.py:429
  15.1 1.9 %collective-permute-done.8.refs_7_ = bf16[480,128]{1,0:T(8,128)(2,1)S(1)} collective-permute-done((bf16[480,128]{1,0:T(8,128)(2,1)S(1)}, bf16[480,128]{1,0:T(8,128)(2,1)S(1)}, u32[]{:S(2)}, u32[]{:S(2)}) %collective-permute-start.8) | collective-permute-done | bytes 122912 | tf_op jit(solution)/shard_map/ppermute | solution.py:426
  17.0 0.0 collective-permute-start.10
  17.0 3.3 %collective-permute-done.9.refs_8_ = bf16[480,128]{1,0:T(8,128)(2,1)S(1)} collective-permute-done((bf16[480,128]{1,0:T(8,128)(2,1)S(1)}, bf16[480,128]{1,0:T(8,128)(2,1)S(1)}, u32[]{:S(2)}, u32[]{:S(2)}) %collective-permute-start.9) | collective-permute-done | bytes 122912 | tf_op jit(solution)/shard_map/ppermute | solution.py:426
  20.3 0.0 collective-permute-start.13
  20.3 0.0 collective-permute-done.6.refs_14_
  20.3 0.5 %collective-permute-start.11 = (bf16[480,128]{1,0:T(8,128)(2,1)S(1)}, bf16[480,128]{1,0:T(8,128)(2,1)S(1)}, u32[]{:S(2)}, u32[]{:S(2)}) collective-permute-start(bf16[480,128]{1,0:T(8,128)(2,1)S(1)} %collective-permute-done.8.refs_7_), channel_id=1, source_target_pairs={{0,1},{1,0},{2,3},{3,2},{4,5},{5,4},{6,7},{7,6},{8,9},{9,8},{10,11... | collective-permute-start | bytes 368648 | tf_op jit(solution)/shard_map/ppermute | solution.py:429
  20.8 0.0 collective-permute-done.5.refs_13_
  20.8 0.1 collective-permute-start.12
  20.9 0.0 collective-permute-done.4.refs_12_
  20.9 0.0 copy-start
  20.9 0.0 copy-start.3
  20.9 0.0 copy-done.1
  20.9 0.0 copy-done.2
  20.9 0.0 copy-done.4
  20.9 0.0 copy-done.5
  20.9 0.0 copy-done.6
  21.0 0.6 %copy-done = f32[192]{0:T(256)S(1)} copy-done((f32[192]{0:T(256)S(1)}, f32[192]{0:T(256)}, u32[]{:S(2)}) %copy-start) | copy-done | bytes 792
  21.6 0.0 copy-done.3
  21.6 1.9 %shard_map.122 = (bf16[2,192,672]{2,1,0:T(8,128)(2,1)S(1)}, bf16[2,224,768]{2,1,0:T(8,128)(2,1)S(1)}, f32[8,2048]{1,0:T(8,128)S(1)}, f32[2048,128]{1,0:T(8,128)S...) custom-call(s32[1,8]{1,0:T(1,128)S(1)} %copy-done.3, ...), custom_call_target="tpu_custom_call" | custom-call | flops 1000000000 | tf_op jit(solution)/shard_map/pallas_call | solution.py:415
  23.5 0.0 collective-permute-done.10.refs_10_
  23.5 0.0 collective-permute-done.13.refs_13_
  23.5 0.0 collective-permute-done.11.refs_11_
  23.5 0.0 collective-permute-done.12.refs_12_
  23.5 6.4 %shard_map.123 = (f32[240,256]{1,0:T(8,128)S(1)}, bf16[240,256]{1,0:T(8,128)(2,1)S(1)}, bf16[240,256]{1,0:T(8,128)(2,1)S(1)}, bf16[240,256]{1,0:T(8,128)(2,1)S(1...) custom-call(f32[8,2048]{1,0:T(8,128)S(1)} %get-tuple-element.31.refs, ...), custom_call_target="tpu_custom_call" | custom-call | flops 8000000000 | tf_op jit(solution)/shard_map/pallas_call | solution.py:415
  29.9 0.6 %collective-permute-start.17 = (bf16[336,128]{1,0:T(8,128)(2,1)S(1)}, bf16[336,128]{1,0:T(8,128)(2,1)S(1)}, u32[]{:S(2)}, u32[]{:S(2)}) collective-permute-start(bf16[336,128]{1,0:T(8,128)(2,1)S(1)} %get-tuple-element.45), channel_id=1, source_target_pairs={{0,8},{8,0},{16,24},{24,16},{1,9},{9,1},{17,25},{25,17},{2,10},{10... | collective-permute-start | bytes 258056 | tf_op jit(solution)/shard_map/ppermute | solution.py:432
  30.5 0.0 collective-permute-start.14
  30.5 3.1 %collective-permute-start.15 = (bf16[240,256]{1,0:T(8,128)(2,1)S(1)}, bf16[240,256]{1,0:T(8,128)(2,1)S(1)}, u32[]{:S(2)}, u32[]{:S(2)}) collective-permute-start(bf16[240,256]{1,0:T(8,128)(2,1)S(1)} %get-tuple-element.42), channel_id=1, source_target_pairs={{0,4},{1,5},{2,6},{3,7},{4,0},{5,1},{6,2},{7,3},{8,12},{9,13},{10,... | collective-permute-start | bytes 368648 | tf_op jit(solution)/shard_map/ppermute | solution.py:426
  33.6 1.3 %collective-permute-start.16 = (bf16[240,256]{1,0:T(8,128)(2,1)S(1)}, bf16[240,256]{1,0:T(8,128)(2,1)S(1)}, u32[]{:S(2)}, u32[]{:S(2)}) collective-permute-start(bf16[240,256]{1,0:T(8,128)(2,1)S(1)} %get-tuple-element.43), channel_id=1, source_target_pairs={{0,6},{1,7},{2,4},{3,5},{4,2},{5,3},{6,0},{7,1},{8,14},{9,15},{10,... | collective-permute-start | bytes 368648 | tf_op jit(solution)/shard_map/ppermute | solution.py:426
  34.9 1.0 %collective-permute-start.18 = (bf16[336,128]{1,0:T(8,128)(2,1)S(1)}, bf16[336,128]{1,0:T(8,128)(2,1)S(1)}, u32[]{:S(2)}, u32[]{:S(2)}) collective-permute-start(bf16[336,128]{1,0:T(8,128)(2,1)S(1)} %get-tuple-element.46), channel_id=1, source_target_pairs={{0,16},{8,24},{16,0},{24,8},{1,17},{9,25},{17,1},{25,9},{2,18},{10... | collective-permute-start | bytes 258056 | tf_op jit(solution)/shard_map/ppermute | solution.py:432
  35.9 0.0 collective-permute-done.17.refs_7_
  35.9 1.9 %collective-permute-start.19 = (bf16[336,128]{1,0:T(8,128)(2,1)S(1)}, bf16[336,128]{1,0:T(8,128)(2,1)S(1)}, u32[]{:S(2)}, u32[]{:S(2)}) collective-permute-start(bf16[336,128]{1,0:T(8,128)(2,1)S(1)} %get-tuple-element.47), channel_id=1, source_target_pairs={{0,24},{8,16},{16,8},{24,0},{1,25},{9,17},{17,9},{25,1},{2,26},{10... | collective-permute-start | bytes 258056 | tf_op jit(solution)/shard_map/ppermute | solution.py:432
  37.9 2.4 %collective-permute-done.18.refs_8_ = bf16[336,128]{1,0:T(8,128)(2,1)S(1)} collective-permute-done((bf16[336,128]{1,0:T(8,128)(2,1)S(1)}, bf16[336,128]{1,0:T(8,128)(2,1)S(1)}, u32[]{:S(2)}, u32[]{:S(2)}) %collective-permute-start.18) | collective-permute-done | bytes 86048 | tf_op jit(solution)/shard_map/ppermute | solution.py:432
  40.3 1.0 %collective-permute-done.19.refs_9_ = bf16[336,128]{1,0:T(8,128)(2,1)S(1)} collective-permute-done((bf16[336,128]{1,0:T(8,128)(2,1)S(1)}, bf16[336,128]{1,0:T(8,128)(2,1)S(1)}, u32[]{:S(2)}, u32[]{:S(2)}) %collective-permute-start.19) | collective-permute-done | bytes 86048 | tf_op jit(solution)/shard_map/ppermute | solution.py:432
  41.3 0.0 collective-permute-done.14.refs_3_
  41.3 1.7 %collective-permute-done.15.refs_4_ = bf16[240,256]{1,0:T(8,128)(2,1)S(1)} collective-permute-done((bf16[240,256]{1,0:T(8,128)(2,1)S(1)}, bf16[240,256]{1,0:T(8,128)(2,1)S(1)}, u32[]{:S(2)}, u32[]{:S(2)}) %collective-permute-start.15) | collective-permute-done | bytes 122912 | tf_op jit(solution)/shard_map/ppermute | solution.py:426
  43.0 0.0 collective-permute-done.16.refs_5_
  43.0 1.0 %shard_map.124 = (bf16[256,192]{1,0:T(8,128)(2,1)}, bf16[256,192]{1,0:T(8,128)(2,1)}, f32[27,24,48]{2,1,0:T(8,128)}) custom-call(f32[192,128]{1,0:T(8,128)S(1)} %get-tuple-element.29.refs_0_, f32[8,256]{1,0:T(8,128)S(1)} %get-tuple-element.30.refs_1_, f32[240,256]{1,0:T(8,128)S(1)} %get-tuple-element.40.refs_2_, ...), custom_call_target="tpu_custom_call" | custom-call | flops 1000000000 | tf_op jit(solution)/shard_map/pallas_call | solution.py:415
Async XLA Ops:
  0.6 20.3 %copy-start.1 = (f32[192]{0:T(256)S(1)}, f32[192]{0:T(256)}, u32[]{:S(2)}) copy-start(f32[192]{0:T(256)} %param.15) | copy-start | bytes 2308
  0.6 20.3 %copy-start.2 = (f32[192]{0:T(256)S(1)}, f32[192]{0:T(256)}, u32[]{:S(2)}) copy-start(f32[192]{0:T(256)} %param.13) | copy-start | bytes 2308
  0.7 20.3 %copy-start.4 = (s32[1,8]{1,0:T(1,128)S(1)}, s32[1,8]{1,0:T(1,128)}, u32[]{:S(2)}) copy-start(s32[1,8]{1,0:T(1,128)} %refs_1_.1) | copy-start | bytes 100
  0.7 20.3 %copy-start.5 = (s32[1,8]{1,0:T(1,128)S(1)}, s32[1,8]{1,0:T(1,128)}, u32[]{:S(2)}) copy-start(s32[1,8]{1,0:T(1,128)} %refs_2_.1) | copy-start | bytes 100
  0.7 20.3 %copy-start.6 = (s32[1,8]{1,0:T(1,128)S(1)}, s32[1,8]{1,0:T(1,128)}, u32[]{:S(2)}) copy-start(s32[1,8]{1,0:T(1,128)} %refs_3_.1) | copy-start | bytes 100
  2.0 8.7 %collective-permute-start.3 = (bf16[336,128]{1,0:T(8,128)(2,1)S(1)}, bf16[336,128]{1,0:T(8,128)(2,1)S(1)}, u32[]{:S(2)}, u32[]{:S(2)}) collective-permute-start(bf16[336,128]{1,0:T(8,128)(2,1)S(1)} %get-tuple-element.27.refs_7_), channel_id=1, source_target_pairs={{0,1},{1,0},{2,3},{3,2},{4,5},{5,4},{6,7},{7,6},{8,9},{9,8},{10,11... | collective-permute-start | bytes 258056 | tf_op jit(solution)/shard_map/ppermute | solution.py:429
  2.5 8.2 %collective-permute-start.2 = (bf16[336,128]{1,0:T(8,128)(2,1)S(1)}, bf16[336,128]{1,0:T(8,128)(2,1)S(1)}, u32[]{:S(2)}, u32[]{:S(2)}) collective-permute-start(bf16[336,128]{1,0:T(8,128)(2,1)S(1)} %get-tuple-element.27.refs_7_), channel_id=1, source_target_pairs={{0,24},{8,16},{16,8},{24,0},{1,25},{9,17},{17,9},{25,1},{2,26},{10... | collective-permute-start | bytes 258056 | tf_op jit(solution)/shard_map/ppermute | solution.py:432
  6.0 8.6 %collective-permute-start.7 = (bf16[480,128]{1,0:T(8,128)(2,1)S(1)}, bf16[480,128]{1,0:T(8,128)(2,1)S(1)}, u32[]{:S(2)}, u32[]{:S(2)}) collective-permute-start(bf16[480,128]{1,0:T(8,128)(2,1)S(1)} %get-tuple-element.28), channel_id=1, source_target_pairs={{0,6},{1,7},{2,4},{3,5},{4,2},{5,3},{6,0},{7,1},{8,14},{9,15},{10,... | collective-permute-start | bytes 368648 | tf_op jit(solution)/shard_map/ppermute | solution.py:426
  9.6 4.5 %collective-permute-start.1 = (bf16[336,128]{1,0:T(8,128)(2,1)S(1)}, bf16[336,128]{1,0:T(8,128)(2,1)S(1)}, u32[]{:S(2)}, u32[]{:S(2)}) collective-permute-start(bf16[336,128]{1,0:T(8,128)(2,1)S(1)} %get-tuple-element.27.refs_7_), channel_id=1, source_target_pairs={{0,16},{8,24},{16,0},{24,8},{1,17},{9,25},{17,1},{25,9},{2,18},{10... | collective-permute-start | bytes 258056 | tf_op jit(solution)/shard_map/ppermute | solution.py:432
  10.1 4.5 %collective-permute-start = (bf16[336,128]{1,0:T(8,128)(2,1)S(1)}, bf16[336,128]{1,0:T(8,128)(2,1)S(1)}, u32[]{:S(2)}, u32[]{:S(2)}) collective-permute-start(bf16[336,128]{1,0:T(8,128)(2,1)S(1)} %get-tuple-element.27.refs_7_), channel_id=1, source_target_pairs={{0,8},{8,0},{16,24},{24,16},{1,9},{9,1},{17,25},{25,17},{2,10},{10... | collective-permute-start | bytes 258056 | tf_op jit(solution)/shard_map/ppermute | solution.py:432
  10.7 6.3 %collective-permute-start.8 = (bf16[480,128]{1,0:T(8,128)(2,1)S(1)}, bf16[480,128]{1,0:T(8,128)(2,1)S(1)}, u32[]{:S(2)}, u32[]{:S(2)}) collective-permute-start(bf16[480,128]{1,0:T(8,128)(2,1)S(1)} %get-tuple-element.38), channel_id=1, source_target_pairs={{0,2},{1,3},{2,0},{3,1},{4,6},{5,7},{6,4},{7,5},{8,10},{9,11},{10,... | collective-permute-start | bytes 368648 | tf_op jit(solution)/shard_map/ppermute | solution.py:426
  10.7 9.6 %collective-permute-start.9 = (bf16[480,128]{1,0:T(8,128)(2,1)S(1)}, bf16[480,128]{1,0:T(8,128)(2,1)S(1)}, u32[]{:S(2)}, u32[]{:S(2)}) collective-permute-start(bf16[480,128]{1,0:T(8,128)(2,1)S(1)} %get-tuple-element.39), channel_id=1, source_target_pairs={{0,4},{1,5},{2,6},{3,7},{4,0},{5,1},{6,2},{7,3},{8,12},{9,13},{10,... | collective-permute-start | bytes 368648 | tf_op jit(solution)/shard_map/ppermute | solution.py:426
  14.1 6.2 %collective-permute-start.6 = (bf16[336,128]{1,0:T(8,128)(2,1)S(1)}, bf16[336,128]{1,0:T(8,128)(2,1)S(1)}, u32[]{:S(2)}, u32[]{:S(2)}) collective-permute-start(bf16[336,128]{1,0:T(8,128)(2,1)S(1)} %collective-permute-done.2.refs_10_), channel_id=1, source_target_pairs={{0,1},{1,0},{2,3},{3,2},{4,5},{5,4},{6,7},{7,6},{8,9},{9,8},{10,11... | collective-permute-start | bytes 258056 | tf_op jit(solution)/shard_map/ppermute | solution.py:429
  14.6 6.2 %collective-permute-start.5 = (bf16[336,128]{1,0:T(8,128)(2,1)S(1)}, bf16[336,128]{1,0:T(8,128)(2,1)S(1)}, u32[]{:S(2)}, u32[]{:S(2)}) collective-permute-start(bf16[336,128]{1,0:T(8,128)(2,1)S(1)} %collective-permute-done.1.refs_9_), channel_id=1, source_target_pairs={{0,1},{1,0},{2,3},{3,2},{4,5},{5,4},{6,7},{7,6},{8,9},{9,8},{10,11... | collective-permute-start | bytes 258056 | tf_op jit(solution)/shard_map/ppermute | solution.py:429
  14.6 6.3 %collective-permute-start.4 = (bf16[336,128]{1,0:T(8,128)(2,1)S(1)}, bf16[336,128]{1,0:T(8,128)(2,1)S(1)}, u32[]{:S(2)}, u32[]{:S(2)}) collective-permute-start(bf16[336,128]{1,0:T(8,128)(2,1)S(1)} %collective-permute-done.refs_8_), channel_id=1, source_target_pairs={{0,1},{1,0},{2,3},{3,2},{4,5},{5,4},{6,7},{7,6},{8,9},{9,8},{10,11... | collective-permute-start | bytes 258056 | tf_op jit(solution)/shard_map/ppermute | solution.py:429
  17.0 6.5 %collective-permute-start.10 = (bf16[480,128]{1,0:T(8,128)(2,1)S(1)}, bf16[480,128]{1,0:T(8,128)(2,1)S(1)}, u32[]{:S(2)}, u32[]{:S(2)}) collective-permute-start(bf16[480,128]{1,0:T(8,128)(2,1)S(1)} %get-tuple-element.37.refs_6_), channel_id=1, source_target_pairs={{0,1},{1,0},{2,3},{3,2},{4,5},{5,4},{6,7},{7,6},{8,9},{9,8},{10,11... | collective-permute-start | bytes 368648 | tf_op jit(solution)/shard_map/ppermute | solution.py:429
  20.3 3.2 %collective-permute-start.13 = (bf16[480,128]{1,0:T(8,128)(2,1)S(1)}, bf16[480,128]{1,0:T(8,128)(2,1)S(1)}, u32[]{:S(2)}, u32[]{:S(2)}) collective-permute-start(bf16[480,128]{1,0:T(8,128)(2,1)S(1)} %collective-permute-done.7.refs_15_.refs_9_), channel_id=1, source_target_pairs={{0,1},{1,0},{2,3},{3,2},{4,5},{5,4},{6,7},{7,6},{8,9},{9,8},{10,11... | collective-permute-start | bytes 368648 | tf_op jit(solution)/shard_map/ppermute | solution.py:429
  20.3 3.2 %collective-permute-start.11 = (bf16[480,128]{1,0:T(8,128)(2,1)S(1)}, bf16[480,128]{1,0:T(8,128)(2,1)S(1)}, u32[]{:S(2)}, u32[]{:S(2)}) collective-permute-start(bf16[480,128]{1,0:T(8,128)(2,1)S(1)} %collective-permute-done.8.refs_7_), channel_id=1, source_target_pairs={{0,1},{1,0},{2,3},{3,2},{4,5},{5,4},{6,7},{7,6},{8,9},{9,8},{10,11... | collective-permute-start | bytes 368648 | tf_op jit(solution)/shard_map/ppermute | solution.py:429
  20.8 2.7 %collective-permute-start.12 = (bf16[480,128]{1,0:T(8,128)(2,1)S(1)}, bf16[480,128]{1,0:T(8,128)(2,1)S(1)}, u32[]{:S(2)}, u32[]{:S(2)}) collective-permute-start(bf16[480,128]{1,0:T(8,128)(2,1)S(1)} %collective-permute-done.9.refs_8_), channel_id=1, source_target_pairs={{0,1},{1,0},{2,3},{3,2},{4,5},{5,4},{6,7},{7,6},{8,9},{9,8},{10,11... | collective-permute-start | bytes 368648 | tf_op jit(solution)/shard_map/ppermute | solution.py:429
  20.9 0.7 %copy-start = (f32[192]{0:T(256)S(1)}, f32[192]{0:T(256)}, u32[]{:S(2)}) copy-start(f32[192]{0:T(256)} %param.14) | copy-start | bytes 2308
  20.9 0.7 %copy-start.3 = (s32[1,8]{1,0:T(1,128)S(1)}, s32[1,8]{1,0:T(1,128)}, u32[]{:S(2)}) copy-start(s32[1,8]{1,0:T(1,128)} %refs_0_.1) | copy-start | bytes 100
  29.9 6.0 %collective-permute-start.17 = (bf16[336,128]{1,0:T(8,128)(2,1)S(1)}, bf16[336,128]{1,0:T(8,128)(2,1)S(1)}, u32[]{:S(2)}, u32[]{:S(2)}) collective-permute-start(bf16[336,128]{1,0:T(8,128)(2,1)S(1)} %get-tuple-element.45), channel_id=1, source_target_pairs={{0,8},{8,0},{16,24},{24,16},{1,9},{9,1},{17,25},{25,17},{2,10},{10... | collective-permute-start | bytes 258056 | tf_op jit(solution)/shard_map/ppermute | solution.py:432
  30.5 10.8 %collective-permute-start.14 = (bf16[240,256]{1,0:T(8,128)(2,1)S(1)}, bf16[240,256]{1,0:T(8,128)(2,1)S(1)}, u32[]{:S(2)}, u32[]{:S(2)}) collective-permute-start(bf16[240,256]{1,0:T(8,128)(2,1)S(1)} %get-tuple-element.41), channel_id=1, source_target_pairs={{0,2},{1,3},{2,0},{3,1},{4,6},{5,7},{6,4},{7,5},{8,10},{9,11},{10,... | collective-permute-start | bytes 368648 | tf_op jit(solution)/shard_map/ppermute | solution.py:426
  30.5 12.5 %collective-permute-start.15 = (bf16[240,256]{1,0:T(8,128)(2,1)S(1)}, bf16[240,256]{1,0:T(8,128)(2,1)S(1)}, u32[]{:S(2)}, u32[]{:S(2)}) collective-permute-start(bf16[240,256]{1,0:T(8,128)(2,1)S(1)} %get-tuple-element.42), channel_id=1, source_target_pairs={{0,4},{1,5},{2,6},{3,7},{4,0},{5,1},{6,2},{7,3},{8,12},{9,13},{10,... | collective-permute-start | bytes 368648 | tf_op jit(solution)/shard_map/ppermute | solution.py:426
  33.6 9.5 %collective-permute-start.16 = (bf16[240,256]{1,0:T(8,128)(2,1)S(1)}, bf16[240,256]{1,0:T(8,128)(2,1)S(1)}, u32[]{:S(2)}, u32[]{:S(2)}) collective-permute-start(bf16[240,256]{1,0:T(8,128)(2,1)S(1)} %get-tuple-element.43), channel_id=1, source_target_pairs={{0,6},{1,7},{2,4},{3,5},{4,2},{5,3},{6,0},{7,1},{8,14},{9,15},{10,... | collective-permute-start | bytes 368648 | tf_op jit(solution)/shard_map/ppermute | solution.py:426
  34.9 5.4 %collective-permute-start.18 = (bf16[336,128]{1,0:T(8,128)(2,1)S(1)}, bf16[336,128]{1,0:T(8,128)(2,1)S(1)}, u32[]{:S(2)}, u32[]{:S(2)}) collective-permute-start(bf16[336,128]{1,0:T(8,128)(2,1)S(1)} %get-tuple-element.46), channel_id=1, source_target_pairs={{0,16},{8,24},{16,0},{24,8},{1,17},{9,25},{17,1},{25,9},{2,18},{10... | collective-permute-start | bytes 258056 | tf_op jit(solution)/shard_map/ppermute | solution.py:432
  35.9 5.4 %collective-permute-start.19 = (bf16[336,128]{1,0:T(8,128)(2,1)S(1)}, bf16[336,128]{1,0:T(8,128)(2,1)S(1)}, u32[]{:S(2)}, u32[]{:S(2)}) collective-permute-start(bf16[336,128]{1,0:T(8,128)(2,1)S(1)} %get-tuple-element.47), channel_id=1, source_target_pairs={{0,24},{8,16},{16,8},{24,0},{1,25},{9,17},{17,9},{25,1},{2,26},{10... | collective-permute-start | bytes 258056 | tf_op jit(solution)/shard_map/ppermute | solution.py:432

commit v3 on v2

--- a/solution.py
+++ b/solution.py
@@ -16,9 +16,6 @@
 BF16, F32 = jnp.bfloat16, jnp.float32
 NT = (((1,), (1,)), ((), ()))
 
-TAPS = [9 * a + 3 * b + e for b in range(3) for a in range(3) for e in range(3)]
-
-
 def up(value, multiple):
     return -(-value // multiple) * multiple
 
@@ -65,9 +62,8 @@
 
 
 def prepare_kernel(nc, ir, irp, x_hbm, g_hbm, w_hbm, *rest):
-    outs, (w_out, x_ref, g_ref, w_ref, blocks, packed, sems) = rest[:nc], rest[nc:]
-    cbp = 2 * irp
-    ob = w_ref.shape[2]
+    outs, (w_ref, x_ref, g_ref, blocks, sems) = rest[:nc], rest[nc:]
+    cbp = 2 * irp
     copies = [
         pltpu.make_async_copy(src, dst, sems.at[i])
         for i, (src, dst) in enumerate(((x_hbm, x_ref), (g_hbm, g_ref), (w_hbm, w_ref)))
@@ -75,7 +71,6 @@
     for copy in copies:
         copy.start()
     chip = place()[0]
-    packed[...] = jnp.zeros_like(packed)
     if irp != ir:
         blocks[...] = jnp.zeros_like(blocks)
     copies[0].wait()
@@ -96,16 +91,24 @@
         outs[j][2 * cbp : 2 * cbp + CELLS] = low
         outs[j][2 * cbp + CELLS :] = high
     copies[2].wait()
+
+
+def pack_kernel(ir, irp, ob, own_ref, other_ref, out_ref, packed):
+    cbp = 2 * irp
+    even = place()[2]
+    packed[...] = jnp.zeros_like(packed)
     for u in range(27):
         p, start = (u, 0) if u < HALF_TAPS else (u - HALF_TAPS, 64)
-        packed[p * irp : p * irp + ir, start : start + ob] = w_ref[TAPS[u]].astype(F32)
-    w_out[...] = packed[...].astype(BF16)
-
-
-def setup_kernel(n, nd, ir, irp, ob, channels, *refs):
+        mine, theirs = own_ref[u].astype(F32), other_ref[u].astype(F32)
+        at = p * cbp
+        packed[at : at + ir, start : start + ob] = jnp.where(even, mine, theirs)
+        packed[at + irp : at + irp + ir, start : start + ob] = jnp.where(even, theirs, mine)
+    out_ref[...] = packed[...].astype(BF16)
+
+
+def tables_kernel(n, nd, ir, irp, ob, channels, *refs):
     clip_ref, rows_ref, cols_ref, start_ref, gamma_ref, beta_ref, bias_ref = refs[:7]
-    w_sets, refs = (refs[7 : 7 + nd], refs[7 + nd : 7 + 2 * nd]), refs[7 + 2 * nd :]
-    conv_out, grad_out, lanes_out, rows_out, columns_out, tiles_out, end_out, bias_out = refs
+    lanes_out, rows_out, columns_out, tiles_out, end_out, bias_out, pick_out, turned_out = refs[7:]
     group_size = channels // G
     cbp = 2 * irp
     chip = place()[0]
@@ -158,27 +161,37 @@
     columns_out[1] = jnp.broadcast_to(column(beta_ref, channel, cbp), (cbp, 128))
     bias_out[...] = jnp.broadcast_to(column(bias_ref, lambda index: index, channels), (channels, 128))
     dp = lax.axis_index("dp")
-    straight_picks, turned_picks = [], []
-    for first in (0, 64):
-        picks, flipped = [], []
+    for half, first in enumerate((0, 64)):
         for j in range(nd):
             base = lax.bitwise_xor(dp, j) * ob
-            for dims, axis, into in (((128, WIDE), 1, picks), ((WIDE, 128), 0, flipped)):
+            at = slice(j * 128, (j + 1) * 128)
+            for dims, axis in (((128, WIDE), 1), ((WIDE, 128), 0)):
                 lane = lax.broadcasted_iota(jnp.int32, dims, 1 - axis) - first
                 out = lax.broadcasted_iota(jnp.int32, dims, axis) - base
-                into.append(((lane == out) & (lane >= 0) & (lane < ob)).astype(F32))
-        straight_picks.append(jnp.concatenate(picks, axis=0).astype(BF16))
-        turned_picks.append(jnp.concatenate(flipped, axis=1).astype(BF16))
-    pad = grad_out.shape[1] - 9 * irp
-    for s, w_refs in enumerate(w_sets):
-        joined = jnp.concatenate([ref[...] for ref in w_refs], axis=1)
-        turned = [lax.dot_general(pick, joined, NT, preferred_element_type=F32) for pick in turned_picks]
-        conv_out[s] = jnp.concatenate(turned, axis=1)[:channels].astype(BF16)
-        straight = jnp.concatenate([dot(joined, pick) for pick in straight_picks], axis=0)
-        grad = jnp.concatenate([straight[b * 9 * irp : (b + 1) * 9 * irp] for b in range(3)], axis=1)
-        if pad:
-            grad = jnp.concatenate([grad, jnp.zeros((pad, 3 * WIDE), F32)], axis=0)
-        grad_out[s] = grad.astype(BF16)
+                pick = ((lane == out) & (lane >= 0) & (lane < ob)).astype(F32).astype(BF16)
+                if axis:
+                    pick_out[half, at] = pick
+                else:
+                    turned_out[half, :, at] = pick
+
+
+def weight_kernel(nd, ir, irp, channels, pick_ref, turned_ref, *refs):
+    conv_out, grad_out = refs[nd:]
+    cbp = 2 * irp
+    joined = jnp.concatenate([ref[...] for ref in refs[:nd]], axis=1)
+    low, high = (lax.dot_general(turned_ref[i], joined, NT, preferred_element_type=F32)[:channels] for i in range(2))
+    frames = (
+        low[:, : 9 * cbp],
+        jnp.concatenate([low[:, 9 * cbp :], high[:, : 4 * cbp]], axis=1),
+        high[:, 4 * cbp : 13 * cbp],
+    )
+    for a in range(3):
+        conv_out[a] = frames[a].astype(BF16)
+    straight = jnp.concatenate([dot(joined, pick_ref[i]) for i in range(2)], axis=0)
+    for b in range(3):
+        taps = [9 * a + 3 * b + e for a in range(3) for e in range(3)]
+        part = jnp.concatenate([straight[t * cbp : (t + 1) * cbp] for t in taps], axis=0)
+        grad_out[:, b * WIDE : (b + 1) * WIDE] = part.astype(BF16)
 
 
 def row_neighbours(x, edges_ref):
@@ -189,28 +202,12 @@
     return above, below
 
 
-def shifts(x, f, c):
-    for e in range(3):
-        if e == 0:
-            moved = jnp.where(c > 0, roll(x, 1), 0.0)
-        elif e == 2:
-            moved = jnp.where(c < 7, roll(x, -1), 0.0)
-        else:
-            moved = x
-        for a in range(3):
-            late = 2 - a
-            yield a, e, (jnp.where(f >= late, roll(moved, 64 * late), 0.0) if late else moved)
-
-
-def store_patches(ref, variants, f, c, irp):
-    blocks = {}
-    for b, rows in enumerate(variants):
-        for a, e, block in shifts(rows, f, c):
-            blocks[9 * b + 3 * a + e] = block
-    blocks[27] = jnp.zeros_like(blocks[0])
-    for p in range(HALF_TAPS):
-        both = jnp.concatenate([blocks[2 * p], blocks[2 * p + 1]], axis=0)
-        ref[2 * p * irp : 2 * (p + 1) * irp] = both.astype(BF16)
+def columns(x, c):
+    return jnp.where(c > 0, roll(x, 1), 0.0), x, jnp.where(c < 7, roll(x, -1), 0.0)
+
+
+def later(x, f, late):
+    return jnp.where(f >= late, roll(x, 64 * late), 0.0) if late else x
 
 
 def main_kernel(nc, nd, ir, irp, ob, channels, *refs):
@@ -222,7 +219,7 @@
     conv_weight, grad_weight, refs = *refs[4:6], refs[6:]
     own, other, refs = refs[:nc], refs[nc:n], refs[n:]
     outs, refs = refs[:nc], refs[nc:]
-    w_outs, (features, grads, shifted, patches, own_patches, ends) = refs[:nd], refs[nd:]
+    centre, hidden_out, features, grads, under, over, patches, ends = refs
     chip, core, even = place()
     lane = lax.broadcasted_iota(jnp.int32, (CELLS // 2, 128), 1)
     for j in range(nc):
@@ -270,11 +267,8 @@
     hidden = jnp.concatenate(hidden, axis=1).astype(BF16).astype(F32)
     above, below = row_neighbours(hidden, lanes_ref)
 
-    def own_rows(x):
-        return jnp.where(even, x[:irp], x[irp:])
-
-    def other_rows(x):
-        return jnp.where(even, x[irp:], x[:irp])
+    for b, x in enumerate((above, hidden, below)):
+        hidden_out[b] = jnp.where(even, x[:irp], x[irp:]).astype(BF16)
 
     def own_tiles(x):
         parts = []
@@ -286,12 +280,13 @@
 
     frame, _, col = cell_index((1, CELLS), 1)
     f, c = jnp.concatenate([frame] * nc, axis=1), jnp.concatenate([col] * nc, axis=1)
-    total = None
-    for s, rows_of in enumerate((own_rows, other_rows)):
-        part = patches.at[s]
-        store_patches(part, [own_tiles(rows_of(x)) for x in (above, hidden, below)], f, c, irp)
-        product = dot(conv_weight[s], part[...])
-        total = product if total is None else total + product
+    for b, x in enumerate((above, hidden, below)):
+        for e, block in enumerate(columns(own_tiles(x), c)):
+            at = (3 * b + e) * cbp
+            patches[at : at + cbp] = block.astype(BF16)
+    total = jnp.zeros((channels, nc * CELLS), F32)
+    for a in range(3):
+        total = total + later(dot(conv_weight[a], patches[...]), f, 2 - a)
     for k in range(nc):
         ends[k, :channels] = total[:, k * CELLS : (k + 1) * CELLS]
 
@@ -306,30 +301,24 @@
         last = grads[max(m - 1, 0)].reshape(split)[:, 7:] * has[0]
         next_ = grads[min(m + 1, n - 1)].reshape(split)[:, :1] * has[1]
         at = slice(m * CELLS, (m + 1) * CELLS)
-        shifted[at, :WIDE] = jnp.concatenate([rows[:, 1:], next_], axis=1).reshape(CELLS, WIDE).astype(BF16)
-        shifted[at, WIDE : 2 * WIDE] = here.astype(BF16)
-        shifted[at, 2 * WIDE :] = jnp.concatenate([last, rows[:, :7]], axis=1).reshape(CELLS, WIDE).astype(BF16)
-    weight = jnp.concatenate([grad_weight[0], grad_weight[1]], axis=0)
-    total = lax.dot_general(weight, shifted[...], NT, preferred_element_type=F32)
+        under[at] = jnp.concatenate([rows[:, 1:], next_], axis=1).reshape(CELLS, WIDE).astype(BF16)
+        centre[at] = here.astype(BF16)
+        over[at] = jnp.concatenate([last, rows[:, :7]], axis=1).reshape(CELLS, WIDE).astype(BF16)
+    rows = jnp.concatenate([under[...], centre[...], over[...]], axis=1)
+    total = lax.dot_general(grad_weight[...], rows, NT, preferred_element_type=F32)
     f, c = jnp.concatenate([frame] * n, axis=1), jnp.concatenate([col] * n, axis=1)
-    halves = []
-    for s in range(2):
-        base = s * grad_weight.shape[1]
-        hidden_grad = jnp.zeros((irp, width), F32)
-        for e in range(3):
-            moved = jnp.zeros((irp, width), F32)
-            for a in range(3):
-                late = 2 - a
-                at = base + (3 * a + e) * irp
-                block = total[at : at + irp]
-                moved = moved + (jnp.where(f < FRAMES - late, roll(block, -64 * late), 0.0) if late else block)
-            if e == 0:
-                moved = jnp.where(c < 7, roll(moved, -1), 0.0)
-            elif e == 2:
-                moved = jnp.where(c > 0, roll(moved, 1), 0.0)
-            hidden_grad = hidden_grad + moved
-        halves.append(hidden_grad)
-    hidden_grad = jnp.concatenate([jnp.where(even, *halves), jnp.where(even, *halves[::-1])], axis=0)
+    hidden_grad = jnp.zeros((cbp, width), F32)
+    for e in range(3):
+        moved = jnp.zeros((cbp, width), F32)
+        for a in range(3):
+            late = 2 - a
+            block = total[(3 * a + e) * cbp : (3 * a + e + 1) * cbp]
+            moved = moved + (jnp.where(f < FRAMES - late, roll(block, -64 * late), 0.0) if late else block)
+        if e == 0:
+            moved = jnp.where(c < 7, roll(moved, -1), 0.0)
+        elif e == 2:
+            moved = jnp.where(c > 0, roll(moved, 1), 0.0)
+        hidden_grad = hidden_grad + moved
     dnormed, first, second = [], [], []
     for m in range(n):
         norm = normed_of(m)
@@ -351,8 +340,22 @@
     for j in range(nc):
         outs[j][...] = ends[lax.bitwise_xor(chip, j)].astype(outs[j].dtype)
 
-    store_patches(own_patches, [own_rows(x) for x in (above, hidden, below)], f, c, irp)
-    product = dot(own_patches[...], shifted[:, WIDE : 2 * WIDE])
+
+def weight_grad_kernel(n, nd, irp, ob, hidden_ref, centre_ref, *refs):
+    w_outs, patches = refs[:nd], refs[nd]
+    cbp = 2 * irp
+    frame, _, col = cell_index((1, CELLS), 1)
+    f, c = jnp.concatenate([frame] * n, axis=1), jnp.concatenate([col] * n, axis=1)
+    blocks = {}
+    for b in range(3):
+        for e, block in enumerate(columns(hidden_ref[b].astype(F32), c)):
+            for a in range(3):
+                blocks[9 * a + 3 * b + e] = later(block, f, 2 - a)
+    blocks[27] = jnp.zeros_like(blocks[0])
+    for p in range(HALF_TAPS):
+        both = jnp.concatenate([blocks[2 * p], blocks[2 * p + 1]], axis=0)
+        patches[p * cbp : (p + 1) * cbp] = both.astype(BF16)
+    product = dot(patches[...], centre_ref[...])
     dp = lax.axis_index("dp")
     half = HALF_TAPS * irp
     lane = lax.broadcasted_iota(jnp.int32, (half, 128), 1)
@@ -364,20 +367,9 @@
         w_outs[j][...] = (low + roll(high, 64)).astype(w_outs[j].dtype)
 
 
-def end_kernel(n, nd, ir, irp, ob, channels, *refs):
-    nc = n // 2
-    bias_ref, inside_ref, refs = refs[0], refs[1], refs[2:]
-    received, refs = refs[:nc], refs[nc:]
-    w_refs, refs = refs[:nd], refs[nd:]
-    conv_ref, grad_ref, weight_ref, blocks, total = refs
+def end_kernel(nc, ir, irp, channels, bias_ref, inside_ref, *refs):
+    received, (conv_ref, grad_ref, blocks) = refs[:nc], refs[nc:]
     chip = place()[0]
-    value = w_refs[0][...]
-    for ref in w_refs[1:]:
-        value = value + ref[...].astype(F32)
-    total[...] = value
-    for u in range(27):
-        p, at = (u, 0) if u < HALF_TAPS else (u - HALF_TAPS, 64)
-        weight_ref[TAPS[u]] = total[p * irp : p * irp + ir, at : at + ob]
     conv = received[0][:channels]
     for ref in received[1:]:
         conv = conv + ref[:channels].astype(F32)
@@ -390,6 +382,17 @@
     grad_ref[...] = jnp.concatenate(parts, axis=0).T.astype(BF16)
 
 
+def weight_end_kernel(ir, irp, ob, *refs):
+    w_refs, (weight_ref, total) = refs[:-2], refs[-2:]
+    value = w_refs[0][...]
+    for ref in w_refs[1:]:
+        value = value + ref[...].astype(F32)
+    total[...] = value
+    for u in range(27):
+        p, at = (u, 0) if u < HALF_TAPS else (u - HALF_TAPS, 64)
+        weight_ref[u] = total[p * irp : p * irp + ir, at : at + ob]
+
+
 def on_device(
     features, out_grad, weight, bias, gamma, beta, tile_clip, tile_rows, clip_cols, clip_start
 ):
@@ -432,81 +435,102 @@
         return lax.ppermute(x, "dp", [(i, i ^ j) for i in range(nd)])
 
     packed_rows = 2 * cbp + CELLS + CELLS // 2
+    taps_first = pltpu.with_memory_space_constraint(weight.transpose(1, 0, 2), pltpu.HBM)
+    taps_other = swap(taps_first)
     sent = call(
         (prepare_kernel, nc, ir, irp),
         tuple(
-            pltpu.with_memory_space_constraint(x, pltpu.HBM)
-            for x in (
-                features.reshape(CELLS, channels),
-                out_grad.reshape(CELLS, channels),
-                weight.transpose(1, 0, 2),
-            )
-        ),
-        [shape((packed_rows, 128))] * nc + [shape((half, 128))],
+            pltpu.with_memory_space_constraint(x.reshape(CELLS, channels), pltpu.HBM)
+            for x in (features, out_grad)
+        )
+        + (taps_first,),
+        [shape((packed_rows, 128))] * nc + [shape((27, ir, ob))],
         [
             pltpu.VMEM((CELLS, channels), BF16),
             pltpu.VMEM((CELLS, channels), BF16),
-            pltpu.VMEM((27, ir, ob), BF16),
             pltpu.VMEM((nc, cbp, CELLS), F32),
-            pltpu.VMEM((half, 128), F32),
             pltpu.SemaphoreType.DMA((3,)),
         ],
         [hbm] * 3,
     )
-    sent, w_block = sent[:nc], sent[nc]
+    sent, taps_first = sent[:nc], sent[nc]
     own = [sent[0]] + [along_chips(sent[j], j) for j in range(1, nc)]
     other = [swap(x) for x in own]
+    w_block = call(
+        (pack_kernel, ir, irp, ob),
+        (taps_first, taps_other),
+        shape((HALF_TAPS * cbp, 128)),
+        [pltpu.VMEM((HALF_TAPS * cbp, 128), F32)],
+    )
     w_blocks = [w_block] + [along_dp(w_block, j) for j in range(1, nd)]
-    w_blocks += [swap(x) for x in w_blocks]
 
     tables = (tile_clip, tile_rows, clip_cols, clip_start)
-    ready = call(
-        (setup_kernel, n, nd, ir, irp, ob, channels),
-        (*tables, gamma[None], beta[None], bias[None], *w_blocks),
+    lanes, rows, columns_, tiles, inside, bias_columns, picks, turned = call(
+        (tables_kernel, n, nd, ir, irp, ob, channels),
+        (*tables, gamma[None], beta[None], bias[None]),
         [
-            shape((2, channels, 2 * half)),
-            shape((2, up(9 * irp, 16), 3 * WIDE)),
             shape((8, width), F32),
             shape((width, 128), F32),
             shape((2, cbp, 128), F32),
             shape((4, up(n, 8), 128), F32),
             shape((8, CELLS), F32),
             shape((channels, 128), F32),
+            shape((2, nd * 128, WIDE)),
+            shape((2, WIDE, nd * 128)),
         ],
         (),
-        [smem] * 4 + [vmem] * (3 + 2 * nd),
-        after=own[-1:],
-    )
-    conv_weight, grad_weight, lanes, rows, columns, tiles, inside, bias_columns = ready
-
+        [smem] * 4 + [vmem] * 3,
+        10.0,
+    )
+    conv_weight, grad_weight = call(
+        (weight_kernel, nd, ir, irp, channels),
+        (picks, turned, *w_blocks),
+        [shape((3, channels, 9 * cbp)), shape((9 * cbp, 3 * WIDE))],
+        us=10.0,
+        after=(),
+    )
     parts = call(
         (main_kernel, nc, nd, ir, irp, ob, channels),
-        (lanes, rows, columns, tiles, conv_weight, grad_weight)
-        + (*own, *other),
+        (lanes, rows, columns_, tiles, conv_weight, grad_weight, *own, *other),
         [shape((channels + cbp, CELLS), F32)]
         + [shape((channels + cbp, CELLS))] * (nc - 1)
-        + [shape((half, 128), F32)]
-        + [shape((half, 128))] * (nd - 1),
+        + [shape((width, WIDE)), shape((3, irp, width))],
         [
             pltpu.VMEM((n, cbp, CELLS), F32),
             pltpu.VMEM((n, CELLS, WIDE), F32),
-            pltpu.VMEM((width, 3 * WIDE), BF16),
-            pltpu.VMEM((2, 2 * half, nc * CELLS), BF16),
-            pltpu.VMEM((2 * half, width), BF16),
+            pltpu.VMEM((width, WIDE), BF16),
+            pltpu.VMEM((width, WIDE), BF16),
+            pltpu.VMEM((9 * cbp, nc * CELLS), BF16),
             pltpu.VMEM((nc, channels + cbp, CELLS), F32),
         ],
         None,
-        8.0,
+        5.0,
         16 + 5 * n // 4,
     )
-    ends, w_parts = parts[:nc], parts[nc:]
+    ends, centre, hidden = parts[:nc], parts[nc], parts[nc + 1]
+    w_parts = call(
+        (weight_grad_kernel, n, nd, irp, ob),
+        (hidden, centre),
+        [shape((half, 128), F32)] + [shape((half, 128))] * (nd - 1),
+        [pltpu.VMEM((2 * half, width), BF16)],
+        None,
+        3.0,
+        8 + n,
+    )
     w_received = [w_parts[0]] + [along_dp(w_parts[j], j) for j in range(1, nd)]
     ends = [ends[0]] + [along_chips(ends[j], j) for j in range(1, nc)]
-    conv_out, input_grad, weight_grad = call(
-        (end_kernel, n, nd, ir, irp, ob, channels),
-        (bias_columns, inside, *ends, *w_received),
-        [shape((CELLS, channels)), shape((CELLS, channels)), shape((27, ir, ob), F32)],
-        [pltpu.VMEM((nc, cbp, CELLS), F32), pltpu.VMEM((half, 128), F32)],
+    conv_out, input_grad = call(
+        (end_kernel, nc, ir, irp, channels),
+        (bias_columns, inside, *ends),
+        [shape((CELLS, channels)), shape((CELLS, channels))],
+        [pltpu.VMEM((nc, cbp, CELLS), F32)],
+    )
+    weight_grad = call(
+        (weight_end_kernel, ir, irp, ob),
+        tuple(w_received),
+        shape((27, ir, ob), F32),
+        [pltpu.VMEM((half, 128), F32)],
+        after=tuple(ends[1:-1]),
     )
     return (
         conv_out.reshape(features.shape),

time: 44.2 us -> 41.5 us (0.939)
  waiting for transfers between devices: 13 us -> 8.66 us
  Pallas kernels: 10.5 us -> 12.6 us
  starting transfers between devices: 19 us -> 17.9 us
  local copies, waits for them, and re-layouts: 0.66 us -> 1.33 us
    ppermute x6, waiting for transfers between devices: 6.09 us -> 2.43 us  [along_dp(): return lax.ppermute(x, 'dp', [(i, i ^ j) for i in range(nd)])]
    pallas_call x4 -> x8, Pallas kernels: 10.5 us -> 12.6 us  [call(): pl.pallas_call(body, out_shape=out, in_specs=(specs or [vmem] * len(args)...]
    ppermute x6, starting transfers between devices: 8.12 us -> 7.11 us  [along_dp(): return lax.ppermute(x, 'dp', [(i, i ^ j) for i in range(nd)])]
    ppermute x6, waiting for transfers between devices: 6.89 us -> 6 us  [along_chips(): return lax.ppermute(x, 'tile', [(i, i ^ 2 * j) for i in range(n)])]
    unnamed x14 -> x16, local copies, waits for them, and re-layouts: 0.66 us -> 1.33 us
    ppermute x8 -> x5, starting transfers between devices: 1.61 us -> 1.11 us  [swap(): return lax.ppermute(x, 'tile', [(i, i ^ 1) for i in range(n)])]
  transfers between devices with their start and end apart: 20 -> 17, of which waited for: 7 -> 5; matrix products, arithmetic and copies ran while one was open for 0% -> 0% of each run, Pallas kernels for 4% -> 18%
where the time goes in v3:
time: 41.5 us; the launch traced here: 41.3 us
  starting transfers between devices  17.9 us (43%)
  Pallas kernels  12.6 us (30%)
  waiting for transfers between devices  8.66 us (21%)
  local copies, waits for them, and re-layouts  1.33 us (3%)
  between operations  0.75 us (2%)
    pallas_call x8, Pallas kernels, call(): pl.pallas_call(body, out_shape=out, in_specs=(specs or [vmem] * len(args)...  12.6 us
    ppermute x6, starting transfers between devices, along_chips(): return lax.ppermute(x, 'tile', [(i, i ^ 2 * j) for i in range(n)])  9.7 us
    ppermute x6, starting transfers between devices, along_dp(): return lax.ppermute(x, 'dp', [(i, i ^ j) for i in range(nd)])  7.11 us
    ppermute x6, waiting for transfers between devices, along_chips(): return lax.ppermute(x, 'tile', [(i, i ^ 2 * j) for i in range(n)])  6 us
    ppermute x6, waiting for transfers between devices, along_dp(): return lax.ppermute(x, 'dp', [(i, i ^ j) for i in range(nd)])  2.43 us
    unnamed x16, local copies, waits for them, and re-layouts  1.33 us
    ppermute x5, starting transfers between devices, swap(): return lax.ppermute(x, 'tile', [(i, i ^ 1) for i in range(n)])  1.11 us
  transfers between devices with their start and end apart: 17, of which 5 were waited for; matrix products, arithmetic and copies ran while one was open for 0% of the time, Pallas kernels for 18%

profile of v3, /device:TPU:0, one launch (start us, length us, event | category | flops | bytes accessed | tf_op | source)
XLA Modules:
  0.0 41.3 jit_solution(9960690653717268334)
XLA Ops:
  0.6 0.5 %collective-permute-start = (bf16[27,24,48]{2,1,0:T(8,128)(2,1)}, bf16[27,24,48]{2,1,0:T(8,128)(2,1)S(1)}, u32[]{:S(2)}, u32[]{:S(2)}) collective-permute-start(bf16[27,24,48]{2,1,0:T(8,128)(2,1)} %bitcast.12), channel_id=1, source_target_pairs={{0,1},{1,0},{2,3},{3,2},{4,5},{5,4},{6,7},{7,6},{8,9},{9,8},{10,11... | collective-permute-start | bytes 186632 | tf_op jit(solution)/shard_map/ppermute | solution.py:432
  1.1 1.1 %shard_map.122 = (bf16[480,128]{1,0:T(8,128)(2,1)S(1)}, bf16[480,128]{1,0:T(8,128)(2,1)S(1)}, bf16[480,128]{1,0:T(8,128)(2,1)S(1)}, bf16[480,128]{1,0:T(8,128)(2,1)S(1)}, bf16[27,24,48]{2,1,0:T(8,128)(2,1)S(1)}) custom-call(bf16[256,192]{1,0:T(8,128)(2,1)} %bitcast.14, bf16[256,192]{1,0:T(8,128)(2,1)} %bitcast.15, bf16[27,24,48]{2,1,0:T(8,128)(2,1)} %bitcast.13), custom_call_target="tpu_custom_call" | custom-call | flops 1000000000 | tf_op jit(solution)/shard_map/pallas_call | solution.py:418
  2.3 2.7 %collective-permute-start.4 = (bf16[480,128]{1,0:T(8,128)(2,1)S(1)}, bf16[480,128]{1,0:T(8,128)(2,1)S(1)}, u32[]{:S(2)}, u32[]{:S(2)}) collective-permute-start(bf16[480,128]{1,0:T(8,128)(2,1)S(1)} %get-tuple-element.42), channel_id=1, source_target_pairs={{0,2},{1,3},{2,0},{3,1},{4,6},{5,7},{6,4},{7,5},{8,10},{9,11},{10,... | collective-permute-start | bytes 368648 | tf_op jit(solution)/shard_map/ppermute | solution.py:429
  5.0 2.6 %collective-permute-start.5 = (bf16[480,128]{1,0:T(8,128)(2,1)S(1)}, bf16[480,128]{1,0:T(8,128)(2,1)S(1)}, u32[]{:S(2)}, u32[]{:S(2)}) collective-permute-start(bf16[480,128]{1,0:T(8,128)(2,1)S(1)} %get-tuple-element.43), channel_id=1, source_target_pairs={{0,4},{1,5},{2,6},{3,7},{4,0},{5,1},{6,2},{7,3},{8,12},{9,13},{10,... | collective-permute-start | bytes 368648 | tf_op jit(solution)/shard_map/ppermute | solution.py:429
  7.5 0.0 collective-permute-start.6
  7.5 0.0 collective-permute-done.refs_1_
  7.5 0.0 copy-start.7
  7.6 0.7 %copy-done.7 = bf16[27,24,48]{2,1,0:T(8,128)(2,1)} copy-done((bf16[27,24,48]{2,1,0:T(8,128)(2,1)}, bf16[27,24,48]{2,1,0:T(8,128)(2,1)S(1)}, u32[]{:S(2)}) %copy-start.7) | copy-done | bytes 62232
  8.2 0.0 copy-start.1
  8.2 0.0 copy-start.2
  8.2 0.0 copy-start.4
  8.2 0.0 copy-start.5
  8.2 0.0 copy-start.6
  8.2 1.1 %shard_map.123.refs_2_ = bf16[672,128]{1,0:T(8,128)(2,1)S(1)} custom-call(bf16[27,24,48]{2,1,0:T(8,128)(2,1)S(1)} %get-tuple-element.38.refs_0_, bf16[27,24,48]{2,1,0:T(8,128)(2,1)} %copy-done.7), custom_call_target="tpu_custom_call" | custom-call | flops 1000000000 | tf_op jit(solution)/shard_map/pallas_call | solution.py:418
  9.4 2.7 %collective-permute-start.3 = (bf16[672,128]{1,0:T(8,128)(2,1)S(1)}, bf16[672,128]{1,0:T(8,128)(2,1)S(1)}, u32[]{:S(2)}, u32[]{:S(2)}) collective-permute-start(bf16[672,128]{1,0:T(8,128)(2,1)S(1)} %shard_map.123.refs_2_), channel_id=1, source_target_pairs={{0,24},{8,16},{16,8},{24,0},{1,25},{9,17},{17,9},{25,1},{2,26},{10... | collective-permute-start | bytes 516104 | tf_op jit(solution)/shard_map/ppermute | solution.py:435
  12.1 0.5 %collective-permute-start.2 = (bf16[672,128]{1,0:T(8,128)(2,1)S(1)}, bf16[672,128]{1,0:T(8,128)(2,1)S(1)}, u32[]{:S(2)}, u32[]{:S(2)}) collective-permute-start(bf16[672,128]{1,0:T(8,128)(2,1)S(1)} %shard_map.123.refs_2_), channel_id=1, source_target_pairs={{0,16},{8,24},{16,0},{24,8},{1,17},{9,25},{17,1},{25,9},{2,18},{10... | collective-permute-start | bytes 516104 | tf_op jit(solution)/shard_map/ppermute | solution.py:435
  12.6 0.0 collective-permute-done.4.refs_7_
  12.6 0.3 collective-permute-start.1
  12.9 0.0 copy-start
  12.9 0.0 copy-start.3
  12.9 0.0 copy-done.1
  12.9 0.0 copy-done.2
  12.9 0.0 copy-done.4
  13.0 0.0 copy-done.5
  13.0 0.0 copy-done.6
  13.0 0.6 %copy-done = f32[192]{0:T(256)S(1)} copy-done((f32[192]{0:T(256)S(1)}, f32[192]{0:T(256)}, u32[]{:S(2)}) %copy-start) | copy-done | bytes 792
  13.6 0.0 copy-done.3
  13.6 1.1 %shard_map.121 = (f32[8,2048]{1,0:T(8,128)S(1)}, f32[2048,128]{1,0:T(8,128)S(1)}, f32[2,48,128]{2,1,0:T(8,128)S(1)}, f32[4,8,128]{2,1,0:T(8,128)S(1)}, f32[8,256...) custom-call(s32[1,8]{1,0:T(1,128)S(1)} %copy-done.3, ...), custom_call_target="tpu_custom_call" | custom-call | flops 10000000000 | tf_op jit(solution)/shard_map/pallas_call | solution.py:418
  14.8 2.6 %collective-permute-done.5.refs_8_ = bf16[480,128]{1,0:T(8,128)(2,1)S(1)} collective-permute-done((bf16[480,128]{1,0:T(8,128)(2,1)S(1)}, bf16[480,128]{1,0:T(8,128)(2,1)S(1)}, u32[]{:S(2)}, u32[]{:S(2)}) %collective-permute-start.5) | collective-permute-done | bytes 122912 | tf_op jit(solution)/shard_map/ppermute | solution.py:429
  17.3 0.0 collective-permute-start.7
  17.3 0.0 collective-permute-done.6.refs_9_
  17.3 0.5 %collective-permute-start.8 = (bf16[480,128]{1,0:T(8,128)(2,1)S(1)}, bf16[480,128]{1,0:T(8,128)(2,1)S(1)}, u32[]{:S(2)}, u32[]{:S(2)}) collective-permute-start(bf16[480,128]{1,0:T(8,128)(2,1)S(1)} %collective-permute-done.4.refs_7_), channel_id=1, source_target_pairs={{0,1},{1,0},{2,3},{3,2},{4,5},{5,4},{6,7},{7,6},{8,9},{9,8},{10,11... | collective-permute-start | bytes 368648 | tf_op jit(solution)/shard_map/ppermute | solution.py:432
  17.8 0.0 collective-permute-done.3.refs_5_
  17.8 0.1 collective-permute-start.9
  17.9 2.3 %collective-permute-done.2.refs_4_ = bf16[672,128]{1,0:T(8,128)(2,1)S(1)} collective-permute-done((bf16[672,128]{1,0:T(8,128)(2,1)S(1)}, bf16[672,128]{1,0:T(8,128)(2,1)S(1)}, u32[]{:S(2)}, u32[]{:S(2)}) %collective-permute-start.2) | collective-permute-done | bytes 172064 | tf_op jit(solution)/shard_map/ppermute | solution.py:435
  20.2 0.0 collective-permute-start.10
  20.3 0.1 collective-permute-done.1.refs_3_
  20.3 1.0 %shard_map.124 = (bf16[3,192,432]{2,1,0:T(8,128)(2,1)S(1)}, bf16[432,768]{1,0:T(8,128)(2,1)S(1)}) custom-call(bf16[2,512,256]{2,1,0:T(8,128)(2,1)S(1)} %get-tuple-element.36.refs_0_, bf16[2,256,512]{2,1,0:T(8,128)(2,1)S(1)} %get-tuple-element.37.refs_1_, bf16[672,128]{1,0:T(8,128)(2,1)S(1)} %shard_map.123.refs_2_, ...), custom_call_target="tpu_custom_call" | custom-call | flops 10000000000 | tf_op jit(solution)/shard_map/pallas_call | solution.py:418
  21.3 0.0 collective-permute-done.7.refs_10_
  21.3 0.0 collective-permute-done.8.refs_11_
  21.3 0.0 collective-permute-done.9.refs_12_
  21.4 0.2 collective-permute-done.10.refs_13_
  21.6 4.4 %shard_map.125 = (f32[240,256]{1,0:T(8,128)S(1)}, bf16[240,256]{1,0:T(8,128)(2,1)S(1)}, bf16[240,256]{1,0:T(8,128)(2,1)S(1)}, bf16[240,256]{1,0:T(8,128)(2,1)S(1...) custom-call(f32[8,2048]{1,0:T(8,128)S(1)} %get-tuple-element.32.refs_0_, ...), custom_call_target="tpu_custom_call" | custom-call | flops 5000000000 | tf_op jit(solution)/shard_map/pallas_call | solution.py:418
  26.0 0.7 %collective-permute-start.11 = (bf16[240,256]{1,0:T(8,128)(2,1)S(1)}, bf16[240,256]{1,0:T(8,128)(2,1)S(1)}, u32[]{:S(2)}, u32[]{:S(2)}) collective-permute-start(bf16[240,256]{1,0:T(8,128)(2,1)S(1)} %get-tuple-element.46), channel_id=1, source_target_pairs={{0,2},{1,3},{2,0},{3,1},{4,6},{5,7},{6,4},{7,5},{8,10},{9,11},{10,... | collective-permute-start | bytes 368648 | tf_op jit(solution)/shard_map/ppermute | solution.py:429
  26.6 3.5 %collective-permute-start.12 = (bf16[240,256]{1,0:T(8,128)(2,1)S(1)}, bf16[240,256]{1,0:T(8,128)(2,1)S(1)}, u32[]{:S(2)}, u32[]{:S(2)}) collective-permute-start(bf16[240,256]{1,0:T(8,128)(2,1)S(1)} %get-tuple-element.47), channel_id=1, source_target_pairs={{0,4},{1,5},{2,6},{3,7},{4,0},{5,1},{6,2},{7,3},{8,12},{9,13},{10,... | collective-permute-start | bytes 368648 | tf_op jit(solution)/shard_map/ppermute | solution.py:429
  30.1 0.3 collective-permute-start.13
  30.4 2.2 %shard_map.127 = (f32[336,128]{1,0:T(8,128)S(1)}, bf16[336,128]{1,0:T(8,128)(2,1)S(1)}, bf16[336,128]{1,0:T(8,128)(2,1)S(1)}, bf16[336,128]{1,0:T(8,128)(2,1)S(1)}) custom-call(bf16[3,24,2048]{2,1,0:T(8,128)(2,1)S(1)} %get-tuple-element.51.refs_0_, bf16[2048,256]{1,0:T(8,128)(2,1)S(1)} %get-tuple-element.52.refs_1_), custom_call_target="tpu_custom_call" | custom-call | flops 3000000000 | tf_op jit(solution)/shard_map/pallas_call | solution.py:418
  32.6 1.6 %collective-permute-start.14 = (bf16[336,128]{1,0:T(8,128)(2,1)S(1)}, bf16[336,128]{1,0:T(8,128)(2,1)S(1)}, u32[]{:S(2)}, u32[]{:S(2)}) collective-permute-start(bf16[336,128]{1,0:T(8,128)(2,1)S(1)} %get-tuple-element.54), channel_id=1, source_target_pairs={{0,8},{8,0},{16,24},{24,16},{1,9},{9,1},{17,25},{25,17},{2,10},{10... | collective-permute-start | bytes 258056 | tf_op jit(solution)/shard_map/ppermute | solution.py:435
  34.2 0.8 %collective-permute-start.15 = (bf16[336,128]{1,0:T(8,128)(2,1)S(1)}, bf16[336,128]{1,0:T(8,128)(2,1)S(1)}, u32[]{:S(2)}, u32[]{:S(2)}) collective-permute-start(bf16[336,128]{1,0:T(8,128)(2,1)S(1)} %get-tuple-element.55), channel_id=1, source_target_pairs={{0,16},{8,24},{16,0},{24,8},{1,17},{9,25},{17,1},{25,9},{2,18},{10... | collective-permute-start | bytes 258056 | tf_op jit(solution)/shard_map/ppermute | solution.py:435
  35.0 0.0 collective-permute-done.11.refs_3_.refs_4_
  35.0 1.2 %collective-permute-start.16 = (bf16[336,128]{1,0:T(8,128)(2,1)S(1)}, bf16[336,128]{1,0:T(8,128)(2,1)S(1)}, u32[]{:S(2)}, u32[]{:S(2)}) collective-permute-start(bf16[336,128]{1,0:T(8,128)(2,1)S(1)} %get-tuple-element.56), channel_id=1, source_target_pairs={{0,24},{8,16},{16,8},{24,0},{1,25},{9,17},{17,9},{25,1},{2,26},{10... | collective-permute-start | bytes 258056 | tf_op jit(solution)/shard_map/ppermute | solution.py:435
  36.2 3.4 %collective-permute-done.12.refs_4_.refs_5_ = bf16[240,256]{1,0:T(8,128)(2,1)S(1)} collective-permute-done((bf16[240,256]{1,0:T(8,128)(2,1)S(1)}, bf16[240,256]{1,0:T(8,128)(2,1)S(1)}, u32[]{:S(2)}, u32[]{:S(2)}) %collective-permute-start.12) | collective-permute-done | bytes 122912 | tf_op jit(solution)/shard_map/ppermute | solution.py:429
  39.6 0.0 collective-permute-done.13.refs_5_
  39.6 0.8 %shard_map.126 = (bf16[256,192]{1,0:T(8,128)(2,1)}, bf16[256,192]{1,0:T(8,128)(2,1)}) custom-call(f32[192,128]{1,0:T(8,128)S(1)} %get-tuple-element.30.refs_0_, f32[8,256]{1,0:T(8,128)S(1)} %get-tuple-element.31.refs_1_, f32[240,256]{1,0:T(8,128)S(1)} %get-tuple-element.45.refs_2_, bf16[240,256]{1,0:T(8,128)(2,1)S(1)} %collective-permute-done.11.refs_3_.refs_4_, ...), custom_call_target="tpu_custom_call" | custom-call | flops 1000000000 | tf_op jit(solution)/shard_map/pallas_call | solution.py:418
  40.4 0.0 collective-permute-done.14.refs_1_
  40.4 0.0 collective-permute-done.15.refs_2_
  40.4 0.0 collective-permute-done.16.refs_3_
  40.4 0.9 %shard_map.128 = f32[27,24,48]{2,1,0:T(8,128)} custom-call(f32[336,128]{1,0:T(8,128)S(1)} %get-tuple-element.53.refs_0_, bf16[336,128]{1,0:T(8,128)(2,1)S(1)} %collective-permute-done.14.refs_1_, bf16[336,128]{1,0:T(8,128)(2,1)S(1)} %collective-permute-done.15.refs_2_, bf16[336,128]{1,0:T(8,128)(2,1)S(1)} %collective-permute-done.16.refs_3_, ...), custom_call_target="tpu_custom_call" | custom-call | flops 1000000000 | tf_op jit(solution)/shard_map/pallas_call | solution.py:418
Async XLA Ops:
  0.6 6.9 %collective-permute-start = (bf16[27,24,48]{2,1,0:T(8,128)(2,1)}, bf16[27,24,48]{2,1,0:T(8,128)(2,1)S(1)}, u32[]{:S(2)}, u32[]{:S(2)}) collective-permute-start(bf16[27,24,48]{2,1,0:T(8,128)(2,1)} %bitcast.12), channel_id=1, source_target_pairs={{0,1},{1,0},{2,3},{3,2},{4,5},{5,4},{6,7},{7,6},{8,9},{9,8},{10,11... | collective-permute-start | bytes 186632 | tf_op jit(solution)/shard_map/ppermute | solution.py:432
  2.3 10.3 %collective-permute-start.4 = (bf16[480,128]{1,0:T(8,128)(2,1)S(1)}, bf16[480,128]{1,0:T(8,128)(2,1)S(1)}, u32[]{:S(2)}, u32[]{:S(2)}) collective-permute-start(bf16[480,128]{1,0:T(8,128)(2,1)S(1)} %get-tuple-element.42), channel_id=1, source_target_pairs={{0,2},{1,3},{2,0},{3,1},{4,6},{5,7},{6,4},{7,5},{8,10},{9,11},{10,... | collective-permute-start | bytes 368648 | tf_op jit(solution)/shard_map/ppermute | solution.py:429
  5.0 12.4 %collective-permute-start.5 = (bf16[480,128]{1,0:T(8,128)(2,1)S(1)}, bf16[480,128]{1,0:T(8,128)(2,1)S(1)}, u32[]{:S(2)}, u32[]{:S(2)}) collective-permute-start(bf16[480,128]{1,0:T(8,128)(2,1)S(1)} %get-tuple-element.43), channel_id=1, source_target_pairs={{0,4},{1,5},{2,6},{3,7},{4,0},{5,1},{6,2},{7,3},{8,12},{9,13},{10,... | collective-permute-start | bytes 368648 | tf_op jit(solution)/shard_map/ppermute | solution.py:429
  7.5 9.8 %collective-permute-start.6 = (bf16[480,128]{1,0:T(8,128)(2,1)S(1)}, bf16[480,128]{1,0:T(8,128)(2,1)S(1)}, u32[]{:S(2)}, u32[]{:S(2)}) collective-permute-start(bf16[480,128]{1,0:T(8,128)(2,1)S(1)} %get-tuple-element.44), channel_id=1, source_target_pairs={{0,6},{1,7},{2,4},{3,5},{4,2},{5,3},{6,0},{7,1},{8,14},{9,15},{10,... | collective-permute-start | bytes 368648 | tf_op jit(solution)/shard_map/ppermute | solution.py:429
  7.5 0.7 %copy-start.7 = (bf16[27,24,48]{2,1,0:T(8,128)(2,1)}, bf16[27,24,48]{2,1,0:T(8,128)(2,1)S(1)}, u32[]{:S(2)}) copy-start(bf16[27,24,48]{2,1,0:T(8,128)(2,1)S(1)} %collective-permute-done.refs_1_) | copy-start | bytes 186628
  8.2 4.7 %copy-start.1 = (f32[192]{0:T(256)S(1)}, f32[192]{0:T(256)}, u32[]{:S(2)}) copy-start(f32[192]{0:T(256)} %param.15) | copy-start | bytes 2308
  8.2 4.7 %copy-start.2 = (f32[192]{0:T(256)S(1)}, f32[192]{0:T(256)}, u32[]{:S(2)}) copy-start(f32[192]{0:T(256)} %param.13) | copy-start | bytes 2308
  8.2 4.7 %copy-start.4 = (s32[1,8]{1,0:T(1,128)S(1)}, s32[1,8]{1,0:T(1,128)}, u32[]{:S(2)}) copy-start(s32[1,8]{1,0:T(1,128)} %refs_1_.1) | copy-start | bytes 100
  8.2 4.7 %copy-start.5 = (s32[1,8]{1,0:T(1,128)S(1)}, s32[1,8]{1,0:T(1,128)}, u32[]{:S(2)}) copy-start(s32[1,8]{1,0:T(1,128)} %refs_2_.1) | copy-start | bytes 100
  8.2 4.7 %copy-start.6 = (s32[1,8]{1,0:T(1,128)S(1)}, s32[1,8]{1,0:T(1,128)}, u32[]{:S(2)}) copy-start(s32[1,8]{1,0:T(1,128)} %refs_3_.1) | copy-start | bytes 100
  9.4 8.5 %collective-permute-start.3 = (bf16[672,128]{1,0:T(8,128)(2,1)S(1)}, bf16[672,128]{1,0:T(8,128)(2,1)S(1)}, u32[]{:S(2)}, u32[]{:S(2)}) collective-permute-start(bf16[672,128]{1,0:T(8,128)(2,1)S(1)} %shard_map.123.refs_2_), channel_id=1, source_target_pairs={{0,24},{8,16},{16,8},{24,0},{1,25},{9,17},{17,9},{25,1},{2,26},{10... | collective-permute-start | bytes 516104 | tf_op jit(solution)/shard_map/ppermute | solution.py:435
  12.1 8.1 %collective-permute-start.2 = (bf16[672,128]{1,0:T(8,128)(2,1)S(1)}, bf16[672,128]{1,0:T(8,128)(2,1)S(1)}, u32[]{:S(2)}, u32[]{:S(2)}) collective-permute-start(bf16[672,128]{1,0:T(8,128)(2,1)S(1)} %shard_map.123.refs_2_), channel_id=1, source_target_pairs={{0,16},{8,24},{16,0},{24,8},{1,17},{9,25},{17,1},{25,9},{2,18},{10... | collective-permute-start | bytes 516104 | tf_op jit(solution)/shard_map/ppermute | solution.py:435
  12.6 7.7 %collective-permute-start.1 = (bf16[672,128]{1,0:T(8,128)(2,1)S(1)}, bf16[672,128]{1,0:T(8,128)(2,1)S(1)}, u32[]{:S(2)}, u32[]{:S(2)}) collective-permute-start(bf16[672,128]{1,0:T(8,128)(2,1)S(1)} %shard_map.123.refs_2_), channel_id=1, source_target_pairs={{0,8},{8,0},{16,24},{24,16},{1,9},{9,1},{17,25},{25,17},{2,10},{10... | collective-permute-start | bytes 516104 | tf_op jit(solution)/shard_map/ppermute | solution.py:435
  12.9 0.7 %copy-start = (f32[192]{0:T(256)S(1)}, f32[192]{0:T(256)}, u32[]{:S(2)}) copy-start(f32[192]{0:T(256)} %param.14) | copy-start | bytes 2308
  12.9 0.7 %copy-start.3 = (s32[1,8]{1,0:T(1,128)S(1)}, s32[1,8]{1,0:T(1,128)}, u32[]{:S(2)}) copy-start(s32[1,8]{1,0:T(1,128)} %refs_0_.1) | copy-start | bytes 100
  17.3 4.0 %collective-permute-start.7 = (bf16[480,128]{1,0:T(8,128)(2,1)S(1)}, bf16[480,128]{1,0:T(8,128)(2,1)S(1)}, u32[]{:S(2)}, u32[]{:S(2)}) collective-permute-start(bf16[480,128]{1,0:T(8,128)(2,1)S(1)} %get-tuple-element.41.refs_6_), channel_id=1, source_target_pairs={{0,1},{1,0},{2,3},{3,2},{4,5},{5,4},{6,7},{7,6},{8,9},{9,8},{10,11... | collective-permute-start | bytes 368648 | tf_op jit(solution)/shard_map/ppermute | solution.py:432
  17.3 4.0 %collective-permute-start.8 = (bf16[480,128]{1,0:T(8,128)(2,1)S(1)}, bf16[480,128]{1,0:T(8,128)(2,1)S(1)}, u32[]{:S(2)}, u32[]{:S(2)}) collective-permute-start(bf16[480,128]{1,0:T(8,128)(2,1)S(1)} %collective-permute-done.4.refs_7_), channel_id=1, source_target_pairs={{0,1},{1,0},{2,3},{3,2},{4,5},{5,4},{6,7},{7,6},{8,9},{9,8},{10,11... | collective-permute-start | bytes 368648 | tf_op jit(solution)/shard_map/ppermute | solution.py:432
  17.8 3.5 %collective-permute-start.9 = (bf16[480,128]{1,0:T(8,128)(2,1)S(1)}, bf16[480,128]{1,0:T(8,128)(2,1)S(1)}, u32[]{:S(2)}, u32[]{:S(2)}) collective-permute-start(bf16[480,128]{1,0:T(8,128)(2,1)S(1)} %collective-permute-done.5.refs_8_), channel_id=1, source_target_pairs={{0,1},{1,0},{2,3},{3,2},{4,5},{5,4},{6,7},{7,6},{8,9},{9,8},{10,11... | collective-permute-start | bytes 368648 | tf_op jit(solution)/shard_map/ppermute | solution.py:432
  20.2 1.3 %collective-permute-start.10 = (bf16[480,128]{1,0:T(8,128)(2,1)S(1)}, bf16[480,128]{1,0:T(8,128)(2,1)S(1)}, u32[]{:S(2)}, u32[]{:S(2)}) collective-permute-start(bf16[480,128]{1,0:T(8,128)(2,1)S(1)} %collective-permute-done.6.refs_9_), channel_id=1, source_target_pairs={{0,1},{1,0},{2,3},{3,2},{4,5},{5,4},{6,7},{7,6},{8,9},{9,8},{10,11... | collective-permute-start | bytes 368648 | tf_op jit(solution)/shard_map/ppermute | solution.py:432
  26.0 9.0 %collective-permute-start.11 = (bf16[240,256]{1,0:T(8,128)(2,1)S(1)}, bf16[240,256]{1,0:T(8,128)(2,1)S(1)}, u32[]{:S(2)}, u32[]{:S(2)}) collective-permute-start(bf16[240,256]{1,0:T(8,128)(2,1)S(1)} %get-tuple-element.46), channel_id=1, source_target_pairs={{0,2},{1,3},{2,0},{3,1},{4,6},{5,7},{6,4},{7,5},{8,10},{9,11},{10,... | collective-permute-start | bytes 368648 | tf_op jit(solution)/shard_map/ppermute | solution.py:429
  26.6 12.9 %collective-permute-start.12 = (bf16[240,256]{1,0:T(8,128)(2,1)S(1)}, bf16[240,256]{1,0:T(8,128)(2,1)S(1)}, u32[]{:S(2)}, u32[]{:S(2)}) collective-permute-start(bf16[240,256]{1,0:T(8,128)(2,1)S(1)} %get-tuple-element.47), channel_id=1, source_target_pairs={{0,4},{1,5},{2,6},{3,7},{4,0},{5,1},{6,2},{7,3},{8,12},{9,13},{10,... | collective-permute-start | bytes 368648 | tf_op jit(solution)/shard_map/ppermute | solution.py:429
  30.1 9.5 %collective-permute-start.13 = (bf16[240,256]{1,0:T(8,128)(2,1)S(1)}, bf16[240,256]{1,0:T(8,128)(2,1)S(1)}, u32[]{:S(2)}, u32[]{:S(2)}) collective-permute-start(bf16[240,256]{1,0:T(8,128)(2,1)S(1)} %get-tuple-element.48), channel_id=1, source_target_pairs={{0,6},{1,7},{2,4},{3,5},{4,2},{5,3},{6,0},{7,1},{8,14},{9,15},{10,... | collective-permute-start | bytes 368648 | tf_op jit(solution)/shard_map/ppermute | solution.py:429
  32.6 7.8 %collective-permute-start.14 = (bf16[336,128]{1,0:T(8,128)(2,1)S(1)}, bf16[336,128]{1,0:T(8,128)(2,1)S(1)}, u32[]{:S(2)}, u32[]{:S(2)}) collective-permute-start(bf16[336,128]{1,0:T(8,128)(2,1)S(1)} %get-tuple-element.54), channel_id=1, source_target_pairs={{0,8},{8,0},{16,24},{24,16},{1,9},{9,1},{17,25},{25,17},{2,10},{10... | collective-permute-start | bytes 258056 | tf_op jit(solution)/shard_map/ppermute | solution.py:435
  34.2 6.3 %collective-permute-start.15 = (bf16[336,128]{1,0:T(8,128)(2,1)S(1)}, bf16[336,128]{1,0:T(8,128)(2,1)S(1)}, u32[]{:S(2)}, u32[]{:S(2)}) collective-permute-start(bf16[336,128]{1,0:T(8,128)(2,1)S(1)} %get-tuple-element.55), channel_id=1, source_target_pairs={{0,16},{8,24},{16,0},{24,8},{1,17},{9,25},{17,1},{25,9},{2,18},{10... | collective-permute-start | bytes 258056 | tf_op jit(solution)/shard_map/ppermute | solution.py:435
  35.0 5.4 %collective-permute-start.16 = (bf16[336,128]{1,0:T(8,128)(2,1)S(1)}, bf16[336,128]{1,0:T(8,128)(2,1)S(1)}, u32[]{:S(2)}, u32[]{:S(2)}) collective-permute-start(bf16[336,128]{1,0:T(8,128)(2,1)S(1)} %get-tuple-element.56), channel_id=1, source_target_pairs={{0,24},{8,16},{16,8},{24,0},{1,25},{9,17},{17,9},{25,1},{2,26},{10... | collective-permute-start | bytes 258056 | tf_op jit(solution)/shard_map/ppermute | solution.py:435

commit v4 on v3

--- a/solution.py
+++ b/solution.py
@@ -436,7 +436,6 @@
 
     packed_rows = 2 * cbp + CELLS + CELLS // 2
     taps_first = pltpu.with_memory_space_constraint(weight.transpose(1, 0, 2), pltpu.HBM)
-    taps_other = swap(taps_first)
     sent = call(
         (prepare_kernel, nc, ir, irp),
         tuple(
@@ -454,6 +453,7 @@
         [hbm] * 3,
     )
     sent, taps_first = sent[:nc], sent[nc]
+    taps_other = swap(taps_first)
     own = [sent[0]] + [along_chips(sent[j], j) for j in range(1, nc)]
     other = [swap(x) for x in own]
     w_block = call(

time: 41.5 us -> 40.3 us (0.971)
  starting transfers between devices: 17.9 us -> 19.1 us
  Pallas kernels: 12.6 us -> 11.7 us
  waiting for transfers between devices: 8.66 us -> 7.87 us
  local copies, waits for them, and re-layouts: 1.33 us -> 0.67 us
    ppermute x6, waiting for transfers between devices: 2.43 us -> 0.76 us  [along_dp(): return lax.ppermute(x, 'dp', [(i, i ^ j) for i in range(nd)])]
    ppermute x6, starting transfers between devices: 7.11 us -> 8.35 us  [along_dp(): return lax.ppermute(x, 'dp', [(i, i ^ j) for i in range(nd)])]
    pallas_call x8, Pallas kernels: 12.6 us -> 11.7 us  [call(): pl.pallas_call(body, out_shape=out, in_specs=(specs or [vmem] * len(args)...]
    ppermute x6, waiting for transfers between devices: 6 us -> 6.88 us  [along_chips(): return lax.ppermute(x, 'tile', [(i, i ^ 2 * j) for i in range(n)])]
    unnamed x16 -> x14, local copies, waits for them, and re-layouts: 1.33 us -> 0.67 us
  transfers between devices with their start and end apart: 17 -> 17, of which waited for: 5 -> 5; matrix products, arithmetic and copies ran while one was open for 0% -> 0% of each run, Pallas kernels for 18% -> 13%
where the time goes in v4:
time: 40.3 us; the launch traced here: 40.1 us
  starting transfers between devices  19.1 us (47%)
  Pallas kernels  11.7 us (29%)
  waiting for transfers between devices  7.87 us (20%)
  between operations  0.77 us (2%)
  local copies, waits for them, and re-layouts  0.67 us (2%)
    pallas_call x8, Pallas kernels, call(): pl.pallas_call(body, out_shape=out, in_specs=(specs or [vmem] * len(args)...  11.7 us
    ppermute x6, starting transfers between devices, along_chips(): return lax.ppermute(x, 'tile', [(i, i ^ 2 * j) for i in range(n)])  9.69 us
    ppermute x6, starting transfers between devices, along_dp(): return lax.ppermute(x, 'dp', [(i, i ^ j) for i in range(nd)])  8.35 us
    ppermute x6, waiting for transfers between devices, along_chips(): return lax.ppermute(x, 'tile', [(i, i ^ 2 * j) for i in range(n)])  6.88 us
    ppermute x5, starting transfers between devices, swap(): return lax.ppermute(x, 'tile', [(i, i ^ 1) for i in range(n)])  1.1 us
  transfers between devices with their start and end apart: 17, of which 5 were waited for; matrix products, arithmetic and copies ran while one was open for 0% of the time, Pallas kernels for 13%

profile of v4, /device:TPU:0, one launch (start us, length us, event | category | flops | bytes accessed | tf_op | source)
XLA Modules:
  0.0 40.1 jit_solution(5542172759070678322)
XLA Ops:
  0.6 1.1 %shard_map.122 = (bf16[480,128]{1,0:T(8,128)(2,1)S(1)}, bf16[480,128]{1,0:T(8,128)(2,1)S(1)}, bf16[480,128]{1,0:T(8,128)(2,1)S(1)}, bf16[480,128]{1,0:T(8,128)(2,1)S(1)}, bf16[27,24,48]{2,1,0:T(8,128)(2,1)S(1)}) custom-call(bf16[256,192]{1,0:T(8,128)(2,1)} %bitcast.13, bf16[256,192]{1,0:T(8,128)(2,1)} %bitcast.14, bf16[27,24,48]{2,1,0:T(8,128)(2,1)} %bitcast.12), custom_call_target="tpu_custom_call" | custom-call | flops 1000000000 | tf_op jit(solution)/shard_map/pallas_call | solution.py:418
  1.8 0.5 %collective-permute-start = (bf16[27,24,48]{2,1,0:T(8,128)(2,1)S(1)}, bf16[27,24,48]{2,1,0:T(8,128)(2,1)S(1)}, u32[]{:S(2)}, u32[]{:S(2)}) collective-permute-start(bf16[27,24,48]{2,1,0:T(8,128)(2,1)S(1)} %get-tuple-element.38.refs_0_), channel_id=1, source_target_pairs={{0,1},{1,0},{2,3},{3,2},{4,5},{5,4},{6,7},{7,6},{8,9},{9,8},{10,11... | collective-permute-start | bytes 186632 | tf_op jit(solution)/shard_map/ppermute | solution.py:432
  2.3 2.6 %collective-permute-start.4 = (bf16[480,128]{1,0:T(8,128)(2,1)S(1)}, bf16[480,128]{1,0:T(8,128)(2,1)S(1)}, u32[]{:S(2)}, u32[]{:S(2)}) collective-permute-start(bf16[480,128]{1,0:T(8,128)(2,1)S(1)} %get-tuple-element.42), channel_id=1, source_target_pairs={{0,2},{1,3},{2,0},{3,1},{4,6},{5,7},{6,4},{7,5},{8,10},{9,11},{10,... | collective-permute-start | bytes 368648 | tf_op jit(solution)/shard_map/ppermute | solution.py:429
  5.0 2.6 %collective-permute-start.5 = (bf16[480,128]{1,0:T(8,128)(2,1)S(1)}, bf16[480,128]{1,0:T(8,128)(2,1)S(1)}, u32[]{:S(2)}, u32[]{:S(2)}) collective-permute-start(bf16[480,128]{1,0:T(8,128)(2,1)S(1)} %get-tuple-element.43), channel_id=1, source_target_pairs={{0,4},{1,5},{2,6},{3,7},{4,0},{5,1},{6,2},{7,3},{8,12},{9,13},{10,... | collective-permute-start | bytes 368648 | tf_op jit(solution)/shard_map/ppermute | solution.py:429
  7.5 0.0 collective-permute-start.6
  7.5 0.0 collective-permute-done.refs_1_
  7.6 0.0 copy-start.1
  7.6 0.0 copy-start.2
  7.6 0.0 copy-start.4
  7.6 0.0 copy-start.5
  7.6 0.0 copy-start.6
  7.6 0.2 shard_map.123.refs_2_
  7.8 2.7 %collective-permute-start.3 = (bf16[672,128]{1,0:T(8,128)(2,1)S(1)}, bf16[672,128]{1,0:T(8,128)(2,1)S(1)}, u32[]{:S(2)}, u32[]{:S(2)}) collective-permute-start(bf16[672,128]{1,0:T(8,128)(2,1)S(1)} %shard_map.123.refs_2_), channel_id=1, source_target_pairs={{0,24},{8,16},{16,8},{24,0},{1,25},{9,17},{17,9},{25,1},{2,26},{10... | collective-permute-start | bytes 516104 | tf_op jit(solution)/shard_map/ppermute | solution.py:435
  10.5 0.5 %collective-permute-start.2 = (bf16[672,128]{1,0:T(8,128)(2,1)S(1)}, bf16[672,128]{1,0:T(8,128)(2,1)S(1)}, u32[]{:S(2)}, u32[]{:S(2)}) collective-permute-start(bf16[672,128]{1,0:T(8,128)(2,1)S(1)} %shard_map.123.refs_2_), channel_id=1, source_target_pairs={{0,16},{8,24},{16,0},{24,8},{1,17},{9,25},{17,1},{25,9},{2,18},{10... | collective-permute-start | bytes 516104 | tf_op jit(solution)/shard_map/ppermute | solution.py:435
  11.0 0.0 collective-permute-done.4.refs_7_
  11.0 1.6 %collective-permute-start.1 = (bf16[672,128]{1,0:T(8,128)(2,1)S(1)}, bf16[672,128]{1,0:T(8,128)(2,1)S(1)}, u32[]{:S(2)}, u32[]{:S(2)}) collective-permute-start(bf16[672,128]{1,0:T(8,128)(2,1)S(1)} %shard_map.123.refs_2_), channel_id=1, source_target_pairs={{0,8},{8,0},{16,24},{24,16},{1,9},{9,1},{17,25},{25,17},{2,10},{10... | collective-permute-start | bytes 516104 | tf_op jit(solution)/shard_map/ppermute | solution.py:435
  12.6 0.0 copy-start
  12.6 0.0 copy-start.3
  12.6 0.0 copy-done.1
  12.6 0.0 copy-done.2
  12.6 0.0 copy-done.4
  12.6 0.0 copy-done.5
  12.6 0.0 copy-done.6
  12.6 0.6 %copy-done = f32[192]{0:T(256)S(1)} copy-done((f32[192]{0:T(256)S(1)}, f32[192]{0:T(256)}, u32[]{:S(2)}) %copy-start) | copy-done | bytes 792
  13.2 0.0 copy-done.3
  13.2 1.1 %shard_map.121 = (f32[8,2048]{1,0:T(8,128)S(1)}, f32[2048,128]{1,0:T(8,128)S(1)}, f32[2,48,128]{2,1,0:T(8,128)S(1)}, f32[4,8,128]{2,1,0:T(8,128)S(1)}, f32[8,256...) custom-call(s32[1,8]{1,0:T(1,128)S(1)} %copy-done.3, ...), custom_call_target="tpu_custom_call" | custom-call | flops 10000000000 | tf_op jit(solution)/shard_map/pallas_call | solution.py:418
  14.4 2.9 %collective-permute-done.5.refs_8_ = bf16[480,128]{1,0:T(8,128)(2,1)S(1)} collective-permute-done((bf16[480,128]{1,0:T(8,128)(2,1)S(1)}, bf16[480,128]{1,0:T(8,128)(2,1)S(1)}, u32[]{:S(2)}, u32[]{:S(2)}) %collective-permute-start.5) | collective-permute-done | bytes 122912 | tf_op jit(solution)/shard_map/ppermute | solution.py:429
  17.3 0.0 collective-permute-start.7
  17.3 0.0 collective-permute-done.6.refs_9_
  17.3 0.5 %collective-permute-start.8 = (bf16[480,128]{1,0:T(8,128)(2,1)S(1)}, bf16[480,128]{1,0:T(8,128)(2,1)S(1)}, u32[]{:S(2)}, u32[]{:S(2)}) collective-permute-start(bf16[480,128]{1,0:T(8,128)(2,1)S(1)} %collective-permute-done.4.refs_7_), channel_id=1, source_target_pairs={{0,1},{1,0},{2,3},{3,2},{4,5},{5,4},{6,7},{7,6},{8,9},{9,8},{10,11... | collective-permute-start | bytes 368648 | tf_op jit(solution)/shard_map/ppermute | solution.py:432
  17.8 0.0 collective-permute-done.3.refs_5_
  17.9 0.1 collective-permute-start.9
  17.9 0.7 %collective-permute-done.2.refs_4_ = bf16[672,128]{1,0:T(8,128)(2,1)S(1)} collective-permute-done((bf16[672,128]{1,0:T(8,128)(2,1)S(1)}, bf16[672,128]{1,0:T(8,128)(2,1)S(1)}, u32[]{:S(2)}, u32[]{:S(2)}) %collective-permute-start.2) | collective-permute-done | bytes 172064 | tf_op jit(solution)/shard_map/ppermute | solution.py:435
  18.6 0.0 collective-permute-start.10
  18.6 0.1 collective-permute-done.1.refs_3_
  18.7 1.0 %shard_map.124 = (bf16[3,192,432]{2,1,0:T(8,128)(2,1)S(1)}, bf16[432,768]{1,0:T(8,128)(2,1)S(1)}) custom-call(bf16[2,512,256]{2,1,0:T(8,128)(2,1)S(1)} %get-tuple-element.36.refs_0_, bf16[2,256,512]{2,1,0:T(8,128)(2,1)S(1)} %get-tuple-element.37.refs_1_, bf16[672,128]{1,0:T(8,128)(2,1)S(1)} %shard_map.123.refs_2_, ...), custom_call_target="tpu_custom_call" | custom-call | flops 10000000000 | tf_op jit(solution)/shard_map/pallas_call | solution.py:418
  19.7 0.0 collective-permute-done.7.refs_10_
  19.7 0.0 collective-permute-done.8.refs_11_
  19.7 0.0 collective-permute-done.9.refs_12_
  19.7 0.2 collective-permute-done.10.refs_13_
  19.9 4.4 %shard_map.125 = (f32[240,256]{1,0:T(8,128)S(1)}, bf16[240,256]{1,0:T(8,128)(2,1)S(1)}, bf16[240,256]{1,0:T(8,128)(2,1)S(1)}, bf16[240,256]{1,0:T(8,128)(2,1)S(1...) custom-call(f32[8,2048]{1,0:T(8,128)S(1)} %get-tuple-element.32.refs_0_, ...), custom_call_target="tpu_custom_call" | custom-call | flops 5000000000 | tf_op jit(solution)/shard_map/pallas_call | solution.py:418
  24.3 1.8 %collective-permute-start.11 = (bf16[240,256]{1,0:T(8,128)(2,1)S(1)}, bf16[240,256]{1,0:T(8,128)(2,1)S(1)}, u32[]{:S(2)}, u32[]{:S(2)}) collective-permute-start(bf16[240,256]{1,0:T(8,128)(2,1)S(1)} %get-tuple-element.46), channel_id=1, source_target_pairs={{0,2},{1,3},{2,0},{3,1},{4,6},{5,7},{6,4},{7,5},{8,10},{9,11},{10,... | collective-permute-start | bytes 368648 | tf_op jit(solution)/shard_map/ppermute | solution.py:429
  26.1 2.4 %collective-permute-start.12 = (bf16[240,256]{1,0:T(8,128)(2,1)S(1)}, bf16[240,256]{1,0:T(8,128)(2,1)S(1)}, u32[]{:S(2)}, u32[]{:S(2)}) collective-permute-start(bf16[240,256]{1,0:T(8,128)(2,1)S(1)} %get-tuple-element.47), channel_id=1, source_target_pairs={{0,4},{1,5},{2,6},{3,7},{4,0},{5,1},{6,2},{7,3},{8,12},{9,13},{10,... | collective-permute-start | bytes 368648 | tf_op jit(solution)/shard_map/ppermute | solution.py:429
  28.4 0.3 collective-permute-start.13
  28.8 2.2 %shard_map.127 = (f32[336,128]{1,0:T(8,128)S(1)}, bf16[336,128]{1,0:T(8,128)(2,1)S(1)}, bf16[336,128]{1,0:T(8,128)(2,1)S(1)}, bf16[336,128]{1,0:T(8,128)(2,1)S(1)}) custom-call(bf16[3,24,2048]{2,1,0:T(8,128)(2,1)S(1)} %get-tuple-element.51.refs_0_, bf16[2048,256]{1,0:T(8,128)(2,1)S(1)} %get-tuple-element.52.refs_1_), custom_call_target="tpu_custom_call" | custom-call | flops 3000000000 | tf_op jit(solution)/shard_map/pallas_call | solution.py:418
  30.9 1.6 %collective-permute-start.14 = (bf16[336,128]{1,0:T(8,128)(2,1)S(1)}, bf16[336,128]{1,0:T(8,128)(2,1)S(1)}, u32[]{:S(2)}, u32[]{:S(2)}) collective-permute-start(bf16[336,128]{1,0:T(8,128)(2,1)S(1)} %get-tuple-element.54), channel_id=1, source_target_pairs={{0,8},{8,0},{16,24},{24,16},{1,9},{9,1},{17,25},{25,17},{2,10},{10... | collective-permute-start | bytes 258056 | tf_op jit(solution)/shard_map/ppermute | solution.py:435
  32.5 1.3 %collective-permute-start.15 = (bf16[336,128]{1,0:T(8,128)(2,1)S(1)}, bf16[336,128]{1,0:T(8,128)(2,1)S(1)}, u32[]{:S(2)}, u32[]{:S(2)}) collective-permute-start(bf16[336,128]{1,0:T(8,128)(2,1)S(1)} %get-tuple-element.55), channel_id=1, source_target_pairs={{0,16},{8,24},{16,0},{24,8},{1,17},{9,25},{17,1},{25,9},{2,18},{10... | collective-permute-start | bytes 258056 | tf_op jit(solution)/shard_map/ppermute | solution.py:435
  33.8 0.0 collective-permute-done.11.refs_3_.refs_4_
  33.8 0.7 %collective-permute-start.16 = (bf16[336,128]{1,0:T(8,128)(2,1)S(1)}, bf16[336,128]{1,0:T(8,128)(2,1)S(1)}, u32[]{:S(2)}, u32[]{:S(2)}) collective-permute-start(bf16[336,128]{1,0:T(8,128)(2,1)S(1)} %get-tuple-element.56), channel_id=1, source_target_pairs={{0,24},{8,16},{16,8},{24,0},{1,25},{9,17},{17,9},{25,1},{2,26},{10... | collective-permute-start | bytes 258056 | tf_op jit(solution)/shard_map/ppermute | solution.py:435
  34.5 3.9 %collective-permute-done.12.refs_4_.refs_5_ = bf16[240,256]{1,0:T(8,128)(2,1)S(1)} collective-permute-done((bf16[240,256]{1,0:T(8,128)(2,1)S(1)}, bf16[240,256]{1,0:T(8,128)(2,1)S(1)}, u32[]{:S(2)}, u32[]{:S(2)}) %collective-permute-start.12) | collective-permute-done | bytes 122912 | tf_op jit(solution)/shard_map/ppermute | solution.py:429
  38.4 0.0 collective-permute-done.13.refs_5_
  38.4 0.8 %shard_map.126 = (bf16[256,192]{1,0:T(8,128)(2,1)}, bf16[256,192]{1,0:T(8,128)(2,1)}) custom-call(f32[192,128]{1,0:T(8,128)S(1)} %get-tuple-element.30.refs_0_, f32[8,256]{1,0:T(8,128)S(1)} %get-tuple-element.31.refs_1_, f32[240,256]{1,0:T(8,128)S(1)} %get-tuple-element.45.refs_2_, bf16[240,256]{1,0:T(8,128)(2,1)S(1)} %collective-permute-done.11.refs_3_.refs_4_, ...), custom_call_target="tpu_custom_call" | custom-call | flops 1000000000 | tf_op jit(solution)/shard_map/pallas_call | solution.py:418
  39.3 0.0 collective-permute-done.14.refs_1_
  39.3 0.0 collective-permute-done.15.refs_2_
  39.3 0.0 collective-permute-done.16.refs_3_
  39.3 0.9 %shard_map.128 = f32[27,24,48]{2,1,0:T(8,128)} custom-call(f32[336,128]{1,0:T(8,128)S(1)} %get-tuple-element.53.refs_0_, bf16[336,128]{1,0:T(8,128)(2,1)S(1)} %collective-permute-done.14.refs_1_, bf16[336,128]{1,0:T(8,128)(2,1)S(1)} %collective-permute-done.15.refs_2_, bf16[336,128]{1,0:T(8,128)(2,1)S(1)} %collective-permute-done.16.refs_3_, ...), custom_call_target="tpu_custom_call" | custom-call | flops 1000000000 | tf_op jit(solution)/shard_map/pallas_call | solution.py:418
Async XLA Ops:
  1.8 5.8 %collective-permute-start = (bf16[27,24,48]{2,1,0:T(8,128)(2,1)S(1)}, bf16[27,24,48]{2,1,0:T(8,128)(2,1)S(1)}, u32[]{:S(2)}, u32[]{:S(2)}) collective-permute-start(bf16[27,24,48]{2,1,0:T(8,128)(2,1)S(1)} %get-tuple-element.38.refs_0_), channel_id=1, source_target_pairs={{0,1},{1,0},{2,3},{3,2},{4,5},{5,4},{6,7},{7,6},{8,9},{9,8},{10,11... | collective-permute-start | bytes 186632 | tf_op jit(solution)/shard_map/ppermute | solution.py:432
  2.3 8.7 %collective-permute-start.4 = (bf16[480,128]{1,0:T(8,128)(2,1)S(1)}, bf16[480,128]{1,0:T(8,128)(2,1)S(1)}, u32[]{:S(2)}, u32[]{:S(2)}) collective-permute-start(bf16[480,128]{1,0:T(8,128)(2,1)S(1)} %get-tuple-element.42), channel_id=1, source_target_pairs={{0,2},{1,3},{2,0},{3,1},{4,6},{5,7},{6,4},{7,5},{8,10},{9,11},{10,... | collective-permute-start | bytes 368648 | tf_op jit(solution)/shard_map/ppermute | solution.py:429
  5.0 12.4 %collective-permute-start.5 = (bf16[480,128]{1,0:T(8,128)(2,1)S(1)}, bf16[480,128]{1,0:T(8,128)(2,1)S(1)}, u32[]{:S(2)}, u32[]{:S(2)}) collective-permute-start(bf16[480,128]{1,0:T(8,128)(2,1)S(1)} %get-tuple-element.43), channel_id=1, source_target_pairs={{0,4},{1,5},{2,6},{3,7},{4,0},{5,1},{6,2},{7,3},{8,12},{9,13},{10,... | collective-permute-start | bytes 368648 | tf_op jit(solution)/shard_map/ppermute | solution.py:429
  7.5 9.8 %collective-permute-start.6 = (bf16[480,128]{1,0:T(8,128)(2,1)S(1)}, bf16[480,128]{1,0:T(8,128)(2,1)S(1)}, u32[]{:S(2)}, u32[]{:S(2)}) collective-permute-start(bf16[480,128]{1,0:T(8,128)(2,1)S(1)} %get-tuple-element.44), channel_id=1, source_target_pairs={{0,6},{1,7},{2,4},{3,5},{4,2},{5,3},{6,0},{7,1},{8,14},{9,15},{10,... | collective-permute-start | bytes 368648 | tf_op jit(solution)/shard_map/ppermute | solution.py:429
  7.6 5.0 %copy-start.1 = (f32[192]{0:T(256)S(1)}, f32[192]{0:T(256)}, u32[]{:S(2)}) copy-start(f32[192]{0:T(256)} %param.15) | copy-start | bytes 2308
  7.6 5.0 %copy-start.2 = (f32[192]{0:T(256)S(1)}, f32[192]{0:T(256)}, u32[]{:S(2)}) copy-start(f32[192]{0:T(256)} %param.13) | copy-start | bytes 2308
  7.6 5.0 %copy-start.4 = (s32[1,8]{1,0:T(1,128)S(1)}, s32[1,8]{1,0:T(1,128)}, u32[]{:S(2)}) copy-start(s32[1,8]{1,0:T(1,128)} %refs_1_.1) | copy-start | bytes 100
  7.6 5.0 %copy-start.5 = (s32[1,8]{1,0:T(1,128)S(1)}, s32[1,8]{1,0:T(1,128)}, u32[]{:S(2)}) copy-start(s32[1,8]{1,0:T(1,128)} %refs_2_.1) | copy-start | bytes 100
  7.6 5.0 %copy-start.6 = (s32[1,8]{1,0:T(1,128)S(1)}, s32[1,8]{1,0:T(1,128)}, u32[]{:S(2)}) copy-start(s32[1,8]{1,0:T(1,128)} %refs_3_.1) | copy-start | bytes 100
  7.8 10.1 %collective-permute-start.3 = (bf16[672,128]{1,0:T(8,128)(2,1)S(1)}, bf16[672,128]{1,0:T(8,128)(2,1)S(1)}, u32[]{:S(2)}, u32[]{:S(2)}) collective-permute-start(bf16[672,128]{1,0:T(8,128)(2,1)S(1)} %shard_map.123.refs_2_), channel_id=1, source_target_pairs={{0,24},{8,16},{16,8},{24,0},{1,25},{9,17},{17,9},{25,1},{2,26},{10... | collective-permute-start | bytes 516104 | tf_op jit(solution)/shard_map/ppermute | solution.py:435
  10.5 8.1 %collective-permute-start.2 = (bf16[672,128]{1,0:T(8,128)(2,1)S(1)}, bf16[672,128]{1,0:T(8,128)(2,1)S(1)}, u32[]{:S(2)}, u32[]{:S(2)}) collective-permute-start(bf16[672,128]{1,0:T(8,128)(2,1)S(1)} %shard_map.123.refs_2_), channel_id=1, source_target_pairs={{0,16},{8,24},{16,0},{24,8},{1,17},{9,25},{17,1},{25,9},{2,18},{10... | collective-permute-start | bytes 516104 | tf_op jit(solution)/shard_map/ppermute | solution.py:435
  11.0 7.7 %collective-permute-start.1 = (bf16[672,128]{1,0:T(8,128)(2,1)S(1)}, bf16[672,128]{1,0:T(8,128)(2,1)S(1)}, u32[]{:S(2)}, u32[]{:S(2)}) collective-permute-start(bf16[672,128]{1,0:T(8,128)(2,1)S(1)} %shard_map.123.refs_2_), channel_id=1, source_target_pairs={{0,8},{8,0},{16,24},{24,16},{1,9},{9,1},{17,25},{25,17},{2,10},{10... | collective-permute-start | bytes 516104 | tf_op jit(solution)/shard_map/ppermute | solution.py:435
  12.6 0.7 %copy-start = (f32[192]{0:T(256)S(1)}, f32[192]{0:T(256)}, u32[]{:S(2)}) copy-start(f32[192]{0:T(256)} %param.14) | copy-start | bytes 2308
  12.6 0.7 %copy-start.3 = (s32[1,8]{1,0:T(1,128)S(1)}, s32[1,8]{1,0:T(1,128)}, u32[]{:S(2)}) copy-start(s32[1,8]{1,0:T(1,128)} %refs_0_.1) | copy-start | bytes 100
  17.3 2.3 %collective-permute-start.7 = (bf16[480,128]{1,0:T(8,128)(2,1)S(1)}, bf16[480,128]{1,0:T(8,128)(2,1)S(1)}, u32[]{:S(2)}, u32[]{:S(2)}) collective-permute-start(bf16[480,128]{1,0:T(8,128)(2,1)S(1)} %get-tuple-element.41.refs_6_), channel_id=1, source_target_pairs={{0,1},{1,0},{2,3},{3,2},{4,5},{5,4},{6,7},{7,6},{8,9},{9,8},{10,11... | collective-permute-start | bytes 368648 | tf_op jit(solution)/shard_map/ppermute | solution.py:432
  17.3 2.3 %collective-permute-start.8 = (bf16[480,128]{1,0:T(8,128)(2,1)S(1)}, bf16[480,128]{1,0:T(8,128)(2,1)S(1)}, u32[]{:S(2)}, u32[]{:S(2)}) collective-permute-start(bf16[480,128]{1,0:T(8,128)(2,1)S(1)} %collective-permute-done.4.refs_7_), channel_id=1, source_target_pairs={{0,1},{1,0},{2,3},{3,2},{4,5},{5,4},{6,7},{7,6},{8,9},{9,8},{10,11... | collective-permute-start | bytes 368648 | tf_op jit(solution)/shard_map/ppermute | solution.py:432
  17.9 1.8 %collective-permute-start.9 = (bf16[480,128]{1,0:T(8,128)(2,1)S(1)}, bf16[480,128]{1,0:T(8,128)(2,1)S(1)}, u32[]{:S(2)}, u32[]{:S(2)}) collective-permute-start(bf16[480,128]{1,0:T(8,128)(2,1)S(1)} %collective-permute-done.5.refs_8_), channel_id=1, source_target_pairs={{0,1},{1,0},{2,3},{3,2},{4,5},{5,4},{6,7},{7,6},{8,9},{9,8},{10,11... | collective-permute-start | bytes 368648 | tf_op jit(solution)/shard_map/ppermute | solution.py:432
  18.6 1.3 %collective-permute-start.10 = (bf16[480,128]{1,0:T(8,128)(2,1)S(1)}, bf16[480,128]{1,0:T(8,128)(2,1)S(1)}, u32[]{:S(2)}, u32[]{:S(2)}) collective-permute-start(bf16[480,128]{1,0:T(8,128)(2,1)S(1)} %collective-permute-done.6.refs_9_), channel_id=1, source_target_pairs={{0,1},{1,0},{2,3},{3,2},{4,5},{5,4},{6,7},{7,6},{8,9},{9,8},{10,11... | collective-permute-start | bytes 368648 | tf_op jit(solution)/shard_map/ppermute | solution.py:432
  24.3 9.5 %collective-permute-start.11 = (bf16[240,256]{1,0:T(8,128)(2,1)S(1)}, bf16[240,256]{1,0:T(8,128)(2,1)S(1)}, u32[]{:S(2)}, u32[]{:S(2)}) collective-permute-start(bf16[240,256]{1,0:T(8,128)(2,1)S(1)} %get-tuple-element.46), channel_id=1, source_target_pairs={{0,2},{1,3},{2,0},{3,1},{4,6},{5,7},{6,4},{7,5},{8,10},{9,11},{10,... | collective-permute-start | bytes 368648 | tf_op jit(solution)/shard_map/ppermute | solution.py:429
  26.1 12.4 %collective-permute-start.12 = (bf16[240,256]{1,0:T(8,128)(2,1)S(1)}, bf16[240,256]{1,0:T(8,128)(2,1)S(1)}, u32[]{:S(2)}, u32[]{:S(2)}) collective-permute-start(bf16[240,256]{1,0:T(8,128)(2,1)S(1)} %get-tuple-element.47), channel_id=1, source_target_pairs={{0,4},{1,5},{2,6},{3,7},{4,0},{5,1},{6,2},{7,3},{8,12},{9,13},{10,... | collective-permute-start | bytes 368648 | tf_op jit(solution)/shard_map/ppermute | solution.py:429
  28.4 10.0 %collective-permute-start.13 = (bf16[240,256]{1,0:T(8,128)(2,1)S(1)}, bf16[240,256]{1,0:T(8,128)(2,1)S(1)}, u32[]{:S(2)}, u32[]{:S(2)}) collective-permute-start(bf16[240,256]{1,0:T(8,128)(2,1)S(1)} %get-tuple-element.48), channel_id=1, source_target_pairs={{0,6},{1,7},{2,4},{3,5},{4,2},{5,3},{6,0},{7,1},{8,14},{9,15},{10,... | collective-permute-start | bytes 368648 | tf_op jit(solution)/shard_map/ppermute | solution.py:429
  30.9 8.3 %collective-permute-start.14 = (bf16[336,128]{1,0:T(8,128)(2,1)S(1)}, bf16[336,128]{1,0:T(8,128)(2,1)S(1)}, u32[]{:S(2)}, u32[]{:S(2)}) collective-permute-start(bf16[336,128]{1,0:T(8,128)(2,1)S(1)} %get-tuple-element.54), channel_id=1, source_target_pairs={{0,8},{8,0},{16,24},{24,16},{1,9},{9,1},{17,25},{25,17},{2,10},{10... | collective-permute-start | bytes 258056 | tf_op jit(solution)/shard_map/ppermute | solution.py:435
  32.5 6.8 %collective-permute-start.15 = (bf16[336,128]{1,0:T(8,128)(2,1)S(1)}, bf16[336,128]{1,0:T(8,128)(2,1)S(1)}, u32[]{:S(2)}, u32[]{:S(2)}) collective-permute-start(bf16[336,128]{1,0:T(8,128)(2,1)S(1)} %get-tuple-element.55), channel_id=1, source_target_pairs={{0,16},{8,24},{16,0},{24,8},{1,17},{9,25},{17,1},{25,9},{2,18},{10... | collective-permute-start | bytes 258056 | tf_op jit(solution)/shard_map/ppermute | solution.py:435
  33.8 5.5 %collective-permute-start.16 = (bf16[336,128]{1,0:T(8,128)(2,1)S(1)}, bf16[336,128]{1,0:T(8,128)(2,1)S(1)}, u32[]{:S(2)}, u32[]{:S(2)}) collective-permute-start(bf16[336,128]{1,0:T(8,128)(2,1)S(1)} %get-tuple-element.56), channel_id=1, source_target_pairs={{0,24},{8,16},{16,8},{24,0},{1,25},{9,17},{17,9},{25,1},{2,26},{10... | collective-permute-start | bytes 258056 | tf_op jit(solution)/shard_map/ppermute | solution.py:435

commit v5 on v4

--- a/solution.py
+++ b/solution.py
@@ -229,7 +229,8 @@
             low = ref[2 * cbp : 2 * cbp + CELLS].astype(F32)
             high = ref[2 * cbp + CELLS :].astype(F32)
             right = [jnp.where(lane < 64, high, 0.0), jnp.where(lane < 64, roll(high, 64), 0.0)]
-            grads[m] = jnp.concatenate([low, jnp.concatenate(right, axis=0)], axis=1)
+            keep = rows_ref[pl.ds(pl.multiple_of(m * CELLS, CELLS), CELLS)]
+            grads[m] = jnp.concatenate([low * keep, jnp.concatenate(right, axis=0) * keep], axis=1)
     gamma, beta = columns_ref[0][:, :1], columns_ref[1][:, :1]
     counted = tiles_ref[3, 0:1]
 
@@ -290,9 +291,6 @@
     for k in range(nc):
         ends[k, :channels] = total[:, k * CELLS : (k + 1) * CELLS]
 
-    for m in range(n):
-        keep = rows_ref[m * CELLS : (m + 1) * CELLS]
-        grads[m] = grads[m] * jnp.concatenate([keep, keep], axis=1)
     split = (FRAMES, HEIGHT, WIDTH, WIDE)
     for m in range(n):
         here = grads[m]

time: 40.3 us -> 40.1 us (level)
  no operation moved by 1% of the time
where the time goes in v5:
time: 40.1 us; the launch traced here: 39.9 us
  starting transfers between devices  19.1 us (48%)
  Pallas kernels  11.4 us (28%)
  waiting for transfers between devices  7.88 us (20%)
  between operations  0.77 us (2%)
  local copies, waits for them, and re-layouts  0.67 us (2%)
    pallas_call x8, Pallas kernels, call(): pl.pallas_call(body, out_shape=out, in_specs=(specs or [vmem] * len(args)...  11.4 us
    ppermute x6, starting transfers between devices, along_chips(): return lax.ppermute(x, 'tile', [(i, i ^ 2 * j) for i in range(n)])  9.69 us
    ppermute x6, starting transfers between devices, along_dp(): return lax.ppermute(x, 'dp', [(i, i ^ j) for i in range(nd)])  8.35 us
    ppermute x6, waiting for transfers between devices, along_chips(): return lax.ppermute(x, 'tile', [(i, i ^ 2 * j) for i in range(n)])  6.88 us
    ppermute x5, starting transfers between devices, swap(): return lax.ppermute(x, 'tile', [(i, i ^ 1) for i in range(n)])  1.1 us
  transfers between devices with their start and end apart: 17, of which 5 were waited for; matrix products, arithmetic and copies ran while one was open for 0% of the time, Pallas kernels for 13%

profile of v5, /device:TPU:0, one launch (start us, length us, event | category | flops | bytes accessed | tf_op | source)
XLA Modules:
  0.0 39.9 jit_solution(4010232881987196555)
XLA Ops:
  0.6 1.1 %shard_map.122 = (bf16[480,128]{1,0:T(8,128)(2,1)S(1)}, bf16[480,128]{1,0:T(8,128)(2,1)S(1)}, bf16[480,128]{1,0:T(8,128)(2,1)S(1)}, bf16[480,128]{1,0:T(8,128)(2,1)S(1)}, bf16[27,24,48]{2,1,0:T(8,128)(2,1)S(1)}) custom-call(bf16[256,192]{1,0:T(8,128)(2,1)} %bitcast.13, bf16[256,192]{1,0:T(8,128)(2,1)} %bitcast.14, bf16[27,24,48]{2,1,0:T(8,128)(2,1)} %bitcast.12), custom_call_target="tpu_custom_call" | custom-call | flops 1000000000 | tf_op jit(solution)/shard_map/pallas_call | solution.py:416
  1.8 0.5 %collective-permute-start = (bf16[27,24,48]{2,1,0:T(8,128)(2,1)S(1)}, bf16[27,24,48]{2,1,0:T(8,128)(2,1)S(1)}, u32[]{:S(2)}, u32[]{:S(2)}) collective-permute-start(bf16[27,24,48]{2,1,0:T(8,128)(2,1)S(1)} %get-tuple-element.38.refs_0_), channel_id=1, source_target_pairs={{0,1},{1,0},{2,3},{3,2},{4,5},{5,4},{6,7},{7,6},{8,9},{9,8},{10,11... | collective-permute-start | bytes 186632 | tf_op jit(solution)/shard_map/ppermute | solution.py:430
  2.3 2.6 %collective-permute-start.4 = (bf16[480,128]{1,0:T(8,128)(2,1)S(1)}, bf16[480,128]{1,0:T(8,128)(2,1)S(1)}, u32[]{:S(2)}, u32[]{:S(2)}) collective-permute-start(bf16[480,128]{1,0:T(8,128)(2,1)S(1)} %get-tuple-element.42), channel_id=1, source_target_pairs={{0,2},{1,3},{2,0},{3,1},{4,6},{5,7},{6,4},{7,5},{8,10},{9,11},{10,... | collective-permute-start | bytes 368648 | tf_op jit(solution)/shard_map/ppermute | solution.py:427
  5.0 2.6 %collective-permute-start.5 = (bf16[480,128]{1,0:T(8,128)(2,1)S(1)}, bf16[480,128]{1,0:T(8,128)(2,1)S(1)}, u32[]{:S(2)}, u32[]{:S(2)}) collective-permute-start(bf16[480,128]{1,0:T(8,128)(2,1)S(1)} %get-tuple-element.43), channel_id=1, source_target_pairs={{0,4},{1,5},{2,6},{3,7},{4,0},{5,1},{6,2},{7,3},{8,12},{9,13},{10,... | collective-permute-start | bytes 368648 | tf_op jit(solution)/shard_map/ppermute | solution.py:427
  7.5 0.0 collective-permute-start.6
  7.5 0.0 collective-permute-done.refs_1_
  7.6 0.0 copy-start.1
  7.6 0.0 copy-start.2
  7.6 0.0 copy-start.4
  7.6 0.0 copy-start.5
  7.6 0.0 copy-start.6
  7.6 0.2 shard_map.123.refs_2_
  7.8 2.7 %collective-permute-start.3 = (bf16[672,128]{1,0:T(8,128)(2,1)S(1)}, bf16[672,128]{1,0:T(8,128)(2,1)S(1)}, u32[]{:S(2)}, u32[]{:S(2)}) collective-permute-start(bf16[672,128]{1,0:T(8,128)(2,1)S(1)} %shard_map.123.refs_2_), channel_id=1, source_target_pairs={{0,24},{8,16},{16,8},{24,0},{1,25},{9,17},{17,9},{25,1},{2,26},{10... | collective-permute-start | bytes 516104 | tf_op jit(solution)/shard_map/ppermute | solution.py:433
  10.5 0.5 %collective-permute-start.2 = (bf16[672,128]{1,0:T(8,128)(2,1)S(1)}, bf16[672,128]{1,0:T(8,128)(2,1)S(1)}, u32[]{:S(2)}, u32[]{:S(2)}) collective-permute-start(bf16[672,128]{1,0:T(8,128)(2,1)S(1)} %shard_map.123.refs_2_), channel_id=1, source_target_pairs={{0,16},{8,24},{16,0},{24,8},{1,17},{9,25},{17,1},{25,9},{2,18},{10... | collective-permute-start | bytes 516104 | tf_op jit(solution)/shard_map/ppermute | solution.py:433
  11.0 0.0 collective-permute-done.4.refs_7_
  11.0 1.6 %collective-permute-start.1 = (bf16[672,128]{1,0:T(8,128)(2,1)S(1)}, bf16[672,128]{1,0:T(8,128)(2,1)S(1)}, u32[]{:S(2)}, u32[]{:S(2)}) collective-permute-start(bf16[672,128]{1,0:T(8,128)(2,1)S(1)} %shard_map.123.refs_2_), channel_id=1, source_target_pairs={{0,8},{8,0},{16,24},{24,16},{1,9},{9,1},{17,25},{25,17},{2,10},{10... | collective-permute-start | bytes 516104 | tf_op jit(solution)/shard_map/ppermute | solution.py:433
  12.6 0.0 copy-start
  12.6 0.0 copy-start.3
  12.6 0.0 copy-done.1
  12.6 0.0 copy-done.2
  12.6 0.0 copy-done.4
  12.6 0.0 copy-done.5
  12.6 0.0 copy-done.6
  12.6 0.6 %copy-done = f32[192]{0:T(256)S(1)} copy-done((f32[192]{0:T(256)S(1)}, f32[192]{0:T(256)}, u32[]{:S(2)}) %copy-start) | copy-done | bytes 792
  13.2 0.0 copy-done.3
  13.2 1.1 %shard_map.121 = (f32[8,2048]{1,0:T(8,128)S(1)}, f32[2048,128]{1,0:T(8,128)S(1)}, f32[2,48,128]{2,1,0:T(8,128)S(1)}, f32[4,8,128]{2,1,0:T(8,128)S(1)}, f32[8,256...) custom-call(s32[1,8]{1,0:T(1,128)S(1)} %copy-done.3, ...), custom_call_target="tpu_custom_call" | custom-call | flops 10000000000 | tf_op jit(solution)/shard_map/pallas_call | solution.py:416
  14.4 2.9 %collective-permute-done.5.refs_8_ = bf16[480,128]{1,0:T(8,128)(2,1)S(1)} collective-permute-done((bf16[480,128]{1,0:T(8,128)(2,1)S(1)}, bf16[480,128]{1,0:T(8,128)(2,1)S(1)}, u32[]{:S(2)}, u32[]{:S(2)}) %collective-permute-start.5) | collective-permute-done | bytes 122912 | tf_op jit(solution)/shard_map/ppermute | solution.py:427
  17.3 0.0 collective-permute-start.7
  17.3 0.0 collective-permute-done.6.refs_9_
  17.3 0.5 %collective-permute-start.8 = (bf16[480,128]{1,0:T(8,128)(2,1)S(1)}, bf16[480,128]{1,0:T(8,128)(2,1)S(1)}, u32[]{:S(2)}, u32[]{:S(2)}) collective-permute-start(bf16[480,128]{1,0:T(8,128)(2,1)S(1)} %collective-permute-done.4.refs_7_), channel_id=1, source_target_pairs={{0,1},{1,0},{2,3},{3,2},{4,5},{5,4},{6,7},{7,6},{8,9},{9,8},{10,11... | collective-permute-start | bytes 368648 | tf_op jit(solution)/shard_map/ppermute | solution.py:430
  17.8 0.0 collective-permute-done.3.refs_5_
  17.9 0.1 collective-permute-start.9
  17.9 0.7 %collective-permute-done.2.refs_4_ = bf16[672,128]{1,0:T(8,128)(2,1)S(1)} collective-permute-done((bf16[672,128]{1,0:T(8,128)(2,1)S(1)}, bf16[672,128]{1,0:T(8,128)(2,1)S(1)}, u32[]{:S(2)}, u32[]{:S(2)}) %collective-permute-start.2) | collective-permute-done | bytes 172064 | tf_op jit(solution)/shard_map/ppermute | solution.py:433
  18.6 0.0 collective-permute-start.10
  18.6 0.1 collective-permute-done.1.refs_3_
  18.7 1.0 %shard_map.124 = (bf16[3,192,432]{2,1,0:T(8,128)(2,1)S(1)}, bf16[432,768]{1,0:T(8,128)(2,1)S(1)}) custom-call(bf16[2,512,256]{2,1,0:T(8,128)(2,1)S(1)} %get-tuple-element.36.refs_0_, bf16[2,256,512]{2,1,0:T(8,128)(2,1)S(1)} %get-tuple-element.37.refs_1_, bf16[672,128]{1,0:T(8,128)(2,1)S(1)} %shard_map.123.refs_2_, ...), custom_call_target="tpu_custom_call" | custom-call | flops 10000000000 | tf_op jit(solution)/shard_map/pallas_call | solution.py:416
  19.7 0.0 collective-permute-done.7.refs_10_
  19.7 0.0 collective-permute-done.8.refs_11_
  19.7 0.0 collective-permute-done.9.refs_12_
  19.7 0.2 collective-permute-done.10.refs_13_
  19.9 4.2 %shard_map.125 = (f32[240,256]{1,0:T(8,128)S(1)}, bf16[240,256]{1,0:T(8,128)(2,1)S(1)}, bf16[240,256]{1,0:T(8,128)(2,1)S(1)}, bf16[240,256]{1,0:T(8,128)(2,1)S(1...) custom-call(f32[8,2048]{1,0:T(8,128)S(1)} %get-tuple-element.32.refs_0_, ...), custom_call_target="tpu_custom_call" | custom-call | flops 5000000000 | tf_op jit(solution)/shard_map/pallas_call | solution.py:416
  24.1 1.8 %collective-permute-start.11 = (bf16[240,256]{1,0:T(8,128)(2,1)S(1)}, bf16[240,256]{1,0:T(8,128)(2,1)S(1)}, u32[]{:S(2)}, u32[]{:S(2)}) collective-permute-start(bf16[240,256]{1,0:T(8,128)(2,1)S(1)} %get-tuple-element.46), channel_id=1, source_target_pairs={{0,2},{1,3},{2,0},{3,1},{4,6},{5,7},{6,4},{7,5},{8,10},{9,11},{10,... | collective-permute-start | bytes 368648 | tf_op jit(solution)/shard_map/ppermute | solution.py:427
  25.8 2.4 %collective-permute-start.12 = (bf16[240,256]{1,0:T(8,128)(2,1)S(1)}, bf16[240,256]{1,0:T(8,128)(2,1)S(1)}, u32[]{:S(2)}, u32[]{:S(2)}) collective-permute-start(bf16[240,256]{1,0:T(8,128)(2,1)S(1)} %get-tuple-element.47), channel_id=1, source_target_pairs={{0,4},{1,5},{2,6},{3,7},{4,0},{5,1},{6,2},{7,3},{8,12},{9,13},{10,... | collective-permute-start | bytes 368648 | tf_op jit(solution)/shard_map/ppermute | solution.py:427
  28.2 0.3 collective-permute-start.13
  28.5 2.2 %shard_map.127 = (f32[336,128]{1,0:T(8,128)S(1)}, bf16[336,128]{1,0:T(8,128)(2,1)S(1)}, bf16[336,128]{1,0:T(8,128)(2,1)S(1)}, bf16[336,128]{1,0:T(8,128)(2,1)S(1)}) custom-call(bf16[3,24,2048]{2,1,0:T(8,128)(2,1)S(1)} %get-tuple-element.51.refs_0_, bf16[2048,256]{1,0:T(8,128)(2,1)S(1)} %get-tuple-element.52.refs_1_), custom_call_target="tpu_custom_call" | custom-call | flops 3000000000 | tf_op jit(solution)/shard_map/pallas_call | solution.py:416
  30.7 1.6 %collective-permute-start.14 = (bf16[336,128]{1,0:T(8,128)(2,1)S(1)}, bf16[336,128]{1,0:T(8,128)(2,1)S(1)}, u32[]{:S(2)}, u32[]{:S(2)}) collective-permute-start(bf16[336,128]{1,0:T(8,128)(2,1)S(1)} %get-tuple-element.54), channel_id=1, source_target_pairs={{0,8},{8,0},{16,24},{24,16},{1,9},{9,1},{17,25},{25,17},{2,10},{10... | collective-permute-start | bytes 258056 | tf_op jit(solution)/shard_map/ppermute | solution.py:433
  32.3 1.3 %collective-permute-start.15 = (bf16[336,128]{1,0:T(8,128)(2,1)S(1)}, bf16[336,128]{1,0:T(8,128)(2,1)S(1)}, u32[]{:S(2)}, u32[]{:S(2)}) collective-permute-start(bf16[336,128]{1,0:T(8,128)(2,1)S(1)} %get-tuple-element.55), channel_id=1, source_target_pairs={{0,16},{8,24},{16,0},{24,8},{1,17},{9,25},{17,1},{25,9},{2,18},{10... | collective-permute-start | bytes 258056 | tf_op jit(solution)/shard_map/ppermute | solution.py:433
  33.6 0.0 collective-permute-done.11.refs_3_.refs_4_
  33.6 0.7 %collective-permute-start.16 = (bf16[336,128]{1,0:T(8,128)(2,1)S(1)}, bf16[336,128]{1,0:T(8,128)(2,1)S(1)}, u32[]{:S(2)}, u32[]{:S(2)}) collective-permute-start(bf16[336,128]{1,0:T(8,128)(2,1)S(1)} %get-tuple-element.56), channel_id=1, source_target_pairs={{0,24},{8,16},{16,8},{24,0},{1,25},{9,17},{17,9},{25,1},{2,26},{10... | collective-permute-start | bytes 258056 | tf_op jit(solution)/shard_map/ppermute | solution.py:433
  34.3 3.9 %collective-permute-done.12.refs_4_.refs_5_ = bf16[240,256]{1,0:T(8,128)(2,1)S(1)} collective-permute-done((bf16[240,256]{1,0:T(8,128)(2,1)S(1)}, bf16[240,256]{1,0:T(8,128)(2,1)S(1)}, u32[]{:S(2)}, u32[]{:S(2)}) %collective-permute-start.12) | collective-permute-done | bytes 122912 | tf_op jit(solution)/shard_map/ppermute | solution.py:427
  38.2 0.0 collective-permute-done.13.refs_5_
  38.2 0.8 %shard_map.126 = (bf16[256,192]{1,0:T(8,128)(2,1)}, bf16[256,192]{1,0:T(8,128)(2,1)}) custom-call(f32[192,128]{1,0:T(8,128)S(1)} %get-tuple-element.30.refs_0_, f32[8,256]{1,0:T(8,128)S(1)} %get-tuple-element.31.refs_1_, f32[240,256]{1,0:T(8,128)S(1)} %get-tuple-element.45.refs_2_, bf16[240,256]{1,0:T(8,128)(2,1)S(1)} %collective-permute-done.11.refs_3_.refs_4_, ...), custom_call_target="tpu_custom_call" | custom-call | flops 1000000000 | tf_op jit(solution)/shard_map/pallas_call | solution.py:416
  39.1 0.0 collective-permute-done.14.refs_1_
  39.1 0.0 collective-permute-done.15.refs_2_
  39.1 0.0 collective-permute-done.16.refs_3_
  39.1 0.9 %shard_map.128 = f32[27,24,48]{2,1,0:T(8,128)} custom-call(f32[336,128]{1,0:T(8,128)S(1)} %get-tuple-element.53.refs_0_, bf16[336,128]{1,0:T(8,128)(2,1)S(1)} %collective-permute-done.14.refs_1_, bf16[336,128]{1,0:T(8,128)(2,1)S(1)} %collective-permute-done.15.refs_2_, bf16[336,128]{1,0:T(8,128)(2,1)S(1)} %collective-permute-done.16.refs_3_, ...), custom_call_target="tpu_custom_call" | custom-call | flops 1000000000 | tf_op jit(solution)/shard_map/pallas_call | solution.py:416
Async XLA Ops:
  1.8 5.8 %collective-permute-start = (bf16[27,24,48]{2,1,0:T(8,128)(2,1)S(1)}, bf16[27,24,48]{2,1,0:T(8,128)(2,1)S(1)}, u32[]{:S(2)}, u32[]{:S(2)}) collective-permute-start(bf16[27,24,48]{2,1,0:T(8,128)(2,1)S(1)} %get-tuple-element.38.refs_0_), channel_id=1, source_target_pairs={{0,1},{1,0},{2,3},{3,2},{4,5},{5,4},{6,7},{7,6},{8,9},{9,8},{10,11... | collective-permute-start | bytes 186632 | tf_op jit(solution)/shard_map/ppermute | solution.py:430
  2.3 8.7 %collective-permute-start.4 = (bf16[480,128]{1,0:T(8,128)(2,1)S(1)}, bf16[480,128]{1,0:T(8,128)(2,1)S(1)}, u32[]{:S(2)}, u32[]{:S(2)}) collective-permute-start(bf16[480,128]{1,0:T(8,128)(2,1)S(1)} %get-tuple-element.42), channel_id=1, source_target_pairs={{0,2},{1,3},{2,0},{3,1},{4,6},{5,7},{6,4},{7,5},{8,10},{9,11},{10,... | collective-permute-start | bytes 368648 | tf_op jit(solution)/shard_map/ppermute | solution.py:427
  5.0 12.4 %collective-permute-start.5 = (bf16[480,128]{1,0:T(8,128)(2,1)S(1)}, bf16[480,128]{1,0:T(8,128)(2,1)S(1)}, u32[]{:S(2)}, u32[]{:S(2)}) collective-permute-start(bf16[480,128]{1,0:T(8,128)(2,1)S(1)} %get-tuple-element.43), channel_id=1, source_target_pairs={{0,4},{1,5},{2,6},{3,7},{4,0},{5,1},{6,2},{7,3},{8,12},{9,13},{10,... | collective-permute-start | bytes 368648 | tf_op jit(solution)/shard_map/ppermute | solution.py:427
  7.5 9.8 %collective-permute-start.6 = (bf16[480,128]{1,0:T(8,128)(2,1)S(1)}, bf16[480,128]{1,0:T(8,128)(2,1)S(1)}, u32[]{:S(2)}, u32[]{:S(2)}) collective-permute-start(bf16[480,128]{1,0:T(8,128)(2,1)S(1)} %get-tuple-element.44), channel_id=1, source_target_pairs={{0,6},{1,7},{2,4},{3,5},{4,2},{5,3},{6,0},{7,1},{8,14},{9,15},{10,... | collective-permute-start | bytes 368648 | tf_op jit(solution)/shard_map/ppermute | solution.py:427
  7.6 5.0 %copy-start.1 = (f32[192]{0:T(256)S(1)}, f32[192]{0:T(256)}, u32[]{:S(2)}) copy-start(f32[192]{0:T(256)} %param.15) | copy-start | bytes 2308
  7.6 5.0 %copy-start.2 = (f32[192]{0:T(256)S(1)}, f32[192]{0:T(256)}, u32[]{:S(2)}) copy-start(f32[192]{0:T(256)} %param.13) | copy-start | bytes 2308
  7.6 5.0 %copy-start.4 = (s32[1,8]{1,0:T(1,128)S(1)}, s32[1,8]{1,0:T(1,128)}, u32[]{:S(2)}) copy-start(s32[1,8]{1,0:T(1,128)} %refs_1_.1) | copy-start | bytes 100
  7.6 5.0 %copy-start.5 = (s32[1,8]{1,0:T(1,128)S(1)}, s32[1,8]{1,0:T(1,128)}, u32[]{:S(2)}) copy-start(s32[1,8]{1,0:T(1,128)} %refs_2_.1) | copy-start | bytes 100
  7.6 5.0 %copy-start.6 = (s32[1,8]{1,0:T(1,128)S(1)}, s32[1,8]{1,0:T(1,128)}, u32[]{:S(2)}) copy-start(s32[1,8]{1,0:T(1,128)} %refs_3_.1) | copy-start | bytes 100
  7.8 10.1 %collective-permute-start.3 = (bf16[672,128]{1,0:T(8,128)(2,1)S(1)}, bf16[672,128]{1,0:T(8,128)(2,1)S(1)}, u32[]{:S(2)}, u32[]{:S(2)}) collective-permute-start(bf16[672,128]{1,0:T(8,128)(2,1)S(1)} %shard_map.123.refs_2_), channel_id=1, source_target_pairs={{0,24},{8,16},{16,8},{24,0},{1,25},{9,17},{17,9},{25,1},{2,26},{10... | collective-permute-start | bytes 516104 | tf_op jit(solution)/shard_map/ppermute | solution.py:433
  10.5 8.1 %collective-permute-start.2 = (bf16[672,128]{1,0:T(8,128)(2,1)S(1)}, bf16[672,128]{1,0:T(8,128)(2,1)S(1)}, u32[]{:S(2)}, u32[]{:S(2)}) collective-permute-start(bf16[672,128]{1,0:T(8,128)(2,1)S(1)} %shard_map.123.refs_2_), channel_id=1, source_target_pairs={{0,16},{8,24},{16,0},{24,8},{1,17},{9,25},{17,1},{25,9},{2,18},{10... | collective-permute-start | bytes 516104 | tf_op jit(solution)/shard_map/ppermute | solution.py:433
  11.0 7.7 %collective-permute-start.1 = (bf16[672,128]{1,0:T(8,128)(2,1)S(1)}, bf16[672,128]{1,0:T(8,128)(2,1)S(1)}, u32[]{:S(2)}, u32[]{:S(2)}) collective-permute-start(bf16[672,128]{1,0:T(8,128)(2,1)S(1)} %shard_map.123.refs_2_), channel_id=1, source_target_pairs={{0,8},{8,0},{16,24},{24,16},{1,9},{9,1},{17,25},{25,17},{2,10},{10... | collective-permute-start | bytes 516104 | tf_op jit(solution)/shard_map/ppermute | solution.py:433
  12.6 0.7 %copy-start = (f32[192]{0:T(256)S(1)}, f32[192]{0:T(256)}, u32[]{:S(2)}) copy-start(f32[192]{0:T(256)} %param.14) | copy-start | bytes 2308
  12.6 0.7 %copy-start.3 = (s32[1,8]{1,0:T(1,128)S(1)}, s32[1,8]{1,0:T(1,128)}, u32[]{:S(2)}) copy-start(s32[1,8]{1,0:T(1,128)} %refs_0_.1) | copy-start | bytes 100
  17.3 2.3 %collective-permute-start.7 = (bf16[480,128]{1,0:T(8,128)(2,1)S(1)}, bf16[480,128]{1,0:T(8,128)(2,1)S(1)}, u32[]{:S(2)}, u32[]{:S(2)}) collective-permute-start(bf16[480,128]{1,0:T(8,128)(2,1)S(1)} %get-tuple-element.41.refs_6_), channel_id=1, source_target_pairs={{0,1},{1,0},{2,3},{3,2},{4,5},{5,4},{6,7},{7,6},{8,9},{9,8},{10,11... | collective-permute-start | bytes 368648 | tf_op jit(solution)/shard_map/ppermute | solution.py:430
  17.3 2.3 %collective-permute-start.8 = (bf16[480,128]{1,0:T(8,128)(2,1)S(1)}, bf16[480,128]{1,0:T(8,128)(2,1)S(1)}, u32[]{:S(2)}, u32[]{:S(2)}) collective-permute-start(bf16[480,128]{1,0:T(8,128)(2,1)S(1)} %collective-permute-done.4.refs_7_), channel_id=1, source_target_pairs={{0,1},{1,0},{2,3},{3,2},{4,5},{5,4},{6,7},{7,6},{8,9},{9,8},{10,11... | collective-permute-start | bytes 368648 | tf_op jit(solution)/shard_map/ppermute | solution.py:430
  17.9 1.8 %collective-permute-start.9 = (bf16[480,128]{1,0:T(8,128)(2,1)S(1)}, bf16[480,128]{1,0:T(8,128)(2,1)S(1)}, u32[]{:S(2)}, u32[]{:S(2)}) collective-permute-start(bf16[480,128]{1,0:T(8,128)(2,1)S(1)} %collective-permute-done.5.refs_8_), channel_id=1, source_target_pairs={{0,1},{1,0},{2,3},{3,2},{4,5},{5,4},{6,7},{7,6},{8,9},{9,8},{10,11... | collective-permute-start | bytes 368648 | tf_op jit(solution)/shard_map/ppermute | solution.py:430
  18.6 1.3 %collective-permute-start.10 = (bf16[480,128]{1,0:T(8,128)(2,1)S(1)}, bf16[480,128]{1,0:T(8,128)(2,1)S(1)}, u32[]{:S(2)}, u32[]{:S(2)}) collective-permute-start(bf16[480,128]{1,0:T(8,128)(2,1)S(1)} %collective-permute-done.6.refs_9_), channel_id=1, source_target_pairs={{0,1},{1,0},{2,3},{3,2},{4,5},{5,4},{6,7},{7,6},{8,9},{9,8},{10,11... | collective-permute-start | bytes 368648 | tf_op jit(solution)/shard_map/ppermute | solution.py:430
  24.1 9.5 %collective-permute-start.11 = (bf16[240,256]{1,0:T(8,128)(2,1)S(1)}, bf16[240,256]{1,0:T(8,128)(2,1)S(1)}, u32[]{:S(2)}, u32[]{:S(2)}) collective-permute-start(bf16[240,256]{1,0:T(8,128)(2,1)S(1)} %get-tuple-element.46), channel_id=1, source_target_pairs={{0,2},{1,3},{2,0},{3,1},{4,6},{5,7},{6,4},{7,5},{8,10},{9,11},{10,... | collective-permute-start | bytes 368648 | tf_op jit(solution)/shard_map/ppermute | solution.py:427
  25.8 12.4 %collective-permute-start.12 = (bf16[240,256]{1,0:T(8,128)(2,1)S(1)}, bf16[240,256]{1,0:T(8,128)(2,1)S(1)}, u32[]{:S(2)}, u32[]{:S(2)}) collective-permute-start(bf16[240,256]{1,0:T(8,128)(2,1)S(1)} %get-tuple-element.47), channel_id=1, source_target_pairs={{0,4},{1,5},{2,6},{3,7},{4,0},{5,1},{6,2},{7,3},{8,12},{9,13},{10,... | collective-permute-start | bytes 368648 | tf_op jit(solution)/shard_map/ppermute | solution.py:427
  28.2 10.0 %collective-permute-start.13 = (bf16[240,256]{1,0:T(8,128)(2,1)S(1)}, bf16[240,256]{1,0:T(8,128)(2,1)S(1)}, u32[]{:S(2)}, u32[]{:S(2)}) collective-permute-start(bf16[240,256]{1,0:T(8,128)(2,1)S(1)} %get-tuple-element.48), channel_id=1, source_target_pairs={{0,6},{1,7},{2,4},{3,5},{4,2},{5,3},{6,0},{7,1},{8,14},{9,15},{10,... | collective-permute-start | bytes 368648 | tf_op jit(solution)/shard_map/ppermute | solution.py:427
  30.7 8.3 %collective-permute-start.14 = (bf16[336,128]{1,0:T(8,128)(2,1)S(1)}, bf16[336,128]{1,0:T(8,128)(2,1)S(1)}, u32[]{:S(2)}, u32[]{:S(2)}) collective-permute-start(bf16[336,128]{1,0:T(8,128)(2,1)S(1)} %get-tuple-element.54), channel_id=1, source_target_pairs={{0,8},{8,0},{16,24},{24,16},{1,9},{9,1},{17,25},{25,17},{2,10},{10... | collective-permute-start | bytes 258056 | tf_op jit(solution)/shard_map/ppermute | solution.py:433
  32.3 6.8 %collective-permute-start.15 = (bf16[336,128]{1,0:T(8,128)(2,1)S(1)}, bf16[336,128]{1,0:T(8,128)(2,1)S(1)}, u32[]{:S(2)}, u32[]{:S(2)}) collective-permute-start(bf16[336,128]{1,0:T(8,128)(2,1)S(1)} %get-tuple-element.55), channel_id=1, source_target_pairs={{0,16},{8,24},{16,0},{24,8},{1,17},{9,25},{17,1},{25,9},{2,18},{10... | collective-permute-start | bytes 258056 | tf_op jit(solution)/shard_map/ppermute | solution.py:433
  33.6 5.5 %collective-permute-start.16 = (bf16[336,128]{1,0:T(8,128)(2,1)S(1)}, bf16[336,128]{1,0:T(8,128)(2,1)S(1)}, u32[]{:S(2)}, u32[]{:S(2)}) collective-permute-start(bf16[336,128]{1,0:T(8,128)(2,1)S(1)} %get-tuple-element.56), channel_id=1, source_target_pairs={{0,24},{8,16},{16,8},{24,0},{1,25},{9,17},{17,9},{25,1},{2,26},{10... | collective-permute-start | bytes 258056 | tf_op jit(solution)/shard_map/ppermute | solution.py:433
